TPU v7x, 256 devices: a whole 4x4x8 slice. The times are simulated.
256 devices in a mesh: pool: 32 (over x, y, core), tgt: 8 (over z).
Axes of the slice: x: 4, y: 4, z: 8, core: 2. Of those that a mesh axis runs over, the one named last changes fastest.
Arguments:
- pool_hidden: bfloat16 [32768, 14336], P('pool', 'tgt'), may hold values from -8 to 8
- pool_grad: bfloat16 [32768, 4096], P('pool', 'tgt'), may hold values from -8 to 8
- target_hidden: bfloat16 [49152, 14336], P('pool', 'tgt'), may hold values from -8 to 8
- target_grad: bfloat16 [49152, 4096], P('pool', 'tgt'), may hold values from -8 to 8
- in_factor: bfloat16 [14336, 128], P('tgt'), may hold values from -0.046875 to 0.046875
- out_factor: bfloat16 [4096, 64], P('tgt'), may hold values from -0.09375 to 0.09375
- example_of_token: int32 [256, 192], P(('pool', 'tgt')), may hold values from 0 to 15, never falling along the last dimension, each value on 1 to 24 neighbouring positions
- owner_map: int32 [32768, 1], P(('pool', 'tgt')), may hold values from 0 to 31; in each aligned block of 128 rows (0 to 127, 128 to 255, ...) at most 8 rows name the same one
Outputs:
- delivered_weight: float32 [32, 8, 32, 8], P('pool', 'tgt')
- delivered_token: int32 [32, 8, 32, 8], P('pool', 'tgt')
Inputs may be any that keep to these rules, and one draw needn't show every extreme that they name: `example_of_token`: within each row, numbers never fall; every one of the 16 examples has 1 to 24 tokens, one exactly 24. `owner_map`: among the 128 tokens of one device at most 8 have the same owner; some owner gets exactly 8 from some device.
All inputs are finite; a program needn't handle non-finite values.
Results may differ from a plain program's by a relative error of at most 0.0028.
Values may be sent and summed in bfloat16 or wider, within the bound.
No kernel may reach another device: no remote copies, remote signals or barrier semaphores. Data moves between devices by JAX's collectives and lax.ppermute only.
A program may use at most 128 MiB of HBM per device.

v0:
```python
import jax
import jax.numpy as jnp
from jax import lax
from jax.sharding import PartitionSpec as P

EX_DEV = 16


def project(factor, rows_data):
    return lax.dot_general(
        factor, rows_data, (((0,), (1,)), ((), ())), preferred_element_type=jnp.float32
    )


def prepare_targets(target_in, target_out, example_of_token):
    highest = lax.Precision.HIGHEST
    gram_in = lax.dot_general(target_in, target_in, (((0,), (0,)), ((), ())), precision=highest)
    gram_out = lax.dot_general(target_out, target_out, (((0,), (0,)), ((), ())), precision=highest)
    example_hot = (
        example_of_token[0][:, None] == jnp.arange(EX_DEV, dtype=jnp.int32)[None, :]
    ).astype(jnp.float32)
    spread = jnp.dot(gram_in * gram_out, example_hot, precision=highest)
    norm_sq = jnp.sum(example_hot * spread, axis=0)
    token_sq = jnp.sum(example_hot * norm_sq[None, :], axis=1)
    token_scale = lax.rsqrt(token_sq + 1e-06)
    scaled_in = (target_in * token_scale[None, :]).astype(jnp.bfloat16)
    return (scaled_in, target_out.astype(jnp.bfloat16), example_of_token.astype(jnp.bfloat16))


def squares(score):
    return lax.psum(jnp.sum(score * score), ("pool", "tgt"))


def shards(
    pool_hidden,
    pool_grad,
    target_hidden,
    target_grad,
    in_factor,
    out_factor,
    example_of_token,
    owner_map,
):
    groups = lax.axis_size("tgt")
    pool_count = lax.axis_size("pool")
    tgt_index = lax.axis_index("tgt")
    pool_index = lax.axis_index("pool")
    sub_rows = example_of_token.shape[1]
    pool_in_part = project(in_factor, pool_hidden)
    pool_out_part = project(out_factor, pool_grad)
    target_in_part = project(in_factor, target_hidden)
    target_out_part = project(out_factor, target_grad)
    pool_in, pool_out, target_in, target_out = (
        lax.psum_scatter(pool_in_part, "tgt", scatter_dimension=1, tiled=True),
        lax.psum_scatter(pool_out_part, "tgt", scatter_dimension=1, tiled=True),
        lax.psum_scatter(target_in_part, "tgt", scatter_dimension=1, tiled=True),
        lax.psum_scatter(target_out_part, "tgt", scatter_dimension=1, tiled=True),
    )
    scaled_in, target_low, seg_code = prepare_targets(target_in, target_out, example_of_token)
    pool_scale = lax.rsqrt(
        jnp.sum(pool_in * pool_in, axis=0) * jnp.sum(pool_out * pool_out, axis=0) + 1e-06
    )
    left_in = pool_in.astype(jnp.bfloat16)
    left_out = pool_out.astype(jnp.bfloat16)
    row_total = left_in.shape[1]
    start_best = jnp.full((row_total,), -2.0, jnp.float32)
    part_in = lax.all_gather(scaled_in, ("pool", "tgt"), axis=1, tiled=True)
    part_out = lax.all_gather(target_low, ("pool", "tgt"), axis=1, tiled=True)
    part_seg = lax.all_gather(seg_code, ("pool", "tgt"), axis=1, tiled=True)
    num_blocks = part_in.shape[1] // sub_rows
    match_in = lax.dot_general(
        left_in, part_in, (((0,), (0,)), ((), ())), preferred_element_type=jnp.float32
    )
    match_out = lax.dot_general(
        left_out, part_out, (((0,), (0,)), ((), ())), preferred_element_type=jnp.float32
    )
    joined = (match_in * match_out).astype(jnp.bfloat16).reshape(row_total, num_blocks, sub_rows)
    seg_ids = part_seg.astype(jnp.int32).reshape(num_blocks, sub_rows)
    example_hot = (
        seg_ids[:, :, None] == jnp.arange(EX_DEV, dtype=jnp.int32)[None, None, :]
    ).astype(jnp.bfloat16)
    per_example = jnp.einsum(
        "rbs,bse->rbe", joined, example_hot, preferred_element_type=jnp.float32
    )
    best_match = jnp.maximum(start_best, jnp.max(per_example, axis=(1, 2)))
    score = best_match * pool_scale
    total_sq = squares(score)
    own_rows = score.shape[0]
    slot_count = max(2, 2 * own_rows // pool_count)
    weight = score * lax.rsqrt(total_sq / (own_rows * groups * pool_count) + 1e-06)
    owners = owner_map[:, 0]
    owner_hot = (owners[:, None] == jnp.arange(pool_count, dtype=jnp.int32)[None, :]).astype(
        jnp.int32
    )
    ranking = jnp.sum(jnp.cumsum(owner_hot, axis=0) * owner_hot, axis=1) - 1
    select = (owners[None, None, :] == jnp.arange(pool_count, dtype=jnp.int32)[:, None, None]) & (
        ranking[None, None, :] == jnp.arange(slot_count, dtype=jnp.int32)[None, :, None]
    )
    send_weight = jnp.sum(jnp.where(select, weight[None, None, :], jnp.float32(0.0)), axis=2)
    token_ids = (pool_index * groups + tgt_index) * own_rows + jnp.arange(own_rows, dtype=jnp.int32)
    send_token = jnp.sum(jnp.where(select, token_ids[None, None, :], 0), axis=2)
    send_token = jnp.where(jnp.any(select, axis=2), send_token, -1)
    got_weight, got_token = (
        lax.all_to_all(send_weight, "pool", split_axis=0, concat_axis=0, tiled=True),
        lax.all_to_all(send_token, "pool", split_axis=0, concat_axis=0, tiled=True),
    )
    return (got_weight[None, None, :, :], got_token[None, None, :, :])


def solution(mesh):
    placed = (
        P("pool", "tgt"),
        P("pool", "tgt"),
        P("pool", "tgt"),
        P("pool", "tgt"),
        P("tgt", None),
        P("tgt", None),
        P(("pool", "tgt"), None),
        P(("pool", "tgt"), None),
    )
    return jax.shard_map(
        shards,
        mesh=mesh,
        in_specs=placed,
        out_specs=(P("pool", "tgt", None, None), P("pool", "tgt", None, None)),
        check_vma=False,
    )
```

profile of v0, /device:TPU:1, one launch (start us, length us, event | category | flops | bytes accessed | tf_op | source)
XLA Modules:
  0.0 660.6 jit_solution(1105286505458318520)
XLA Ops:
  8.1 1.6 copy-done
  9.7 2.3 convolution_bitcast_fusion
  12.1 5.2 fusion.16
  18.4 1.2 fusion.15
  19.6 4.2 fusion.13
  23.9 25.2 %reduce-scatter.13.cloned.1.call-done = f32[192,64]{1,0:T(8,128)} async-done(((f32[1536,64]{1,0:T(8,128)}), f32[192,64]{1,0:T(8,128)}) %reduce-scatter.13.cloned.1.call-update) | async-done | bytes 49168
  49.0 1.6 copy.24
  50.7 37.5 %reduce-scatter.9.cloned.1.call-done = f32[128,192]{0,1:T(8,128)} async-done(((f32[128,1536]{0,1:T(8,128)}), f32[128,192]{0,1:T(8,128)}) %reduce-scatter.9.cloned.1.call-update) | async-done | bytes 98320 | tf_op jit(solution)/shard_map/reduce_scatter | solution.py:56
  88.2 1.3 fusion.14
  89.5 1.3 convolution_multiply_fusion.1
  91.3 1.6 multiply_convert_fusion
  95.2 12.5 %all-to-all-start.1 = ((s32[32,1,8]{2,1,0:T(1,128)}), s32[32,1,8]{2,1,0:T(1,128)S(1)}, u32[]{:S(2)}, u32[]{:S(2)}) async-start(s32[32,1,8]{2,1,0:T(1,128)} %bitcast.9), calls=%async_computation.4 | async-start | bytes 32768 | tf_op jit(solution)/shard_map/all_to_all | solution.py:105
  107.7 162.2 %all-reduce.3.cloned.1.call-done = bf16[49152]{0:T(1024)(128)(2,1)} async-done(((bf16[49152]{0:T(1024)(128)(2,1)}), bf16[49152]{0:T(1024)(128)(2,1)}) %all-reduce.3.cloned.1.call-update) | async-done | bytes 98320
  272.6 115.7 %all-gather.6.cloned.1.call-done = bf16[256,192,64]{1,2,0:T(8,128)(2,1)} async-done(((bf16[1,192,64]{1,2,0:T(8,128)(2,1)}), bf16[256,192,64]{1,2,0:T(8,128)(2,1)}) %all-gather.6.cloned.1.call-update) | async-done | bytes 6291472 | tf_op jit(solution)/shard_map/all_gather | solution.py:68
  388.3 11.4 %copy.17 = bf16[256,192,64]{1,0,2:T(8,128)(2,1)} copy(bf16[256,192,64]{1,2,0:T(8,128)(2,1)} %all-gather.6.cloned.1.call-done) | data formatting | bytes 12582912 | tf_op jit(solution)/shard_map/all_gather | solution.py:68
  399.7 13.1 %reshape.105 = bf16[49152,64]{0,1:T(8,128)(2,1)} reshape(bf16[256,192,64]{1,0,2:T(8,128)(2,1)} %copy.17) | data formatting | bytes 12582912
  412.8 97.1 %all-gather.4.cloned.1.call-done = bf16[128,49152]{0,1:T(8,128)(2,1)} async-done(((bf16[128,192]{0,1:T(8,128)(2,1)}), bf16[128,49152]{0,1:T(8,128)(2,1)}) %all-gather.4.cloned.1.call-update) | async-done | bytes 12582928 | tf_op jit(solution)/shard_map/all_gather | solution.py:67
  509.9 12.9 %fusion.8 = f32[128,49152]{1,0:T(8,128)} fusion(bf16[128,49152]{0,1:T(8,128)(2,1)} %all-gather.4.cloned.1.call-done, f32[128,128]{1,0:T(8,128)S(1)} %copy-done.6), kind=kOutput, calls=%fused_computation.22 | convolution fusion | flops 1610629120 | bytes 37814272 | tf_op jit(solution)/shard_map/dot_general | solution.py:71
  522.8 16.7 %fusion = bf16[128,49152]{1,0:T(8,128)(2,1)} fusion(f32[128,49152]{1,0:T(8,128)} %fusion.8, bf16[49152,64]{0,1:T(8,128)(2,1)} %reshape.105, f32[64,128]{1,0:T(8,128)S(1)} %copy-done.7), kind=kOutput, calls=%fused_computation.1 | convolution fusion | flops 817897472 | bytes 44072960 | tf_op jit(solution)/shard_map/dot_general | solution.py:74
  539.6 16.6 %copy.18 = bf16[128,49152]{0,1:T(8,128)(2,1)} copy(bf16[128,49152]{1,0:T(8,128)(2,1)} %fusion) | data formatting | bytes 25165824 | tf_op jit(solution)/shard_map/convert_element_type | solution.py:77
  556.2 8.1 %fusion.3 = f32[128]{0:T(128)S(1)} fusion(bf16[128,256,192]{0,2,1:T(8,128)(2,1)} %bitcast.37, s32[256,192]{1,0:T(8,128)S(1)} %reshape.101), kind=kOutput, calls=%fused_computation.6 | convolution fusion | flops 202637184 | bytes 12780032 | tf_op jit(solution)/shard_map/rbs,bse->rbe/dot_general | solution.py:82
  564.8 74.5 %psum.7 = f32[]{:T(128)} all-reduce(f32[]{:T(128)} %get-tuple-element.6), channel_id=1, replica_groups=mesh['pool'=32,'tgt'=8] {'pool','tgt'}, use_global_device_ids=true, to_apply=%region_12.13 | all-reduce | flops 1 | bytes 8 | tf_op jit(solution)/shard_map/psum | solution.py:31
  640.8 4.8 all-to-all-start
  646.3 6.3 all-to-all-done
  (61 shorter events, 9.5 us)
Async XLA Ops:
  8.0 1.7 copy-start
  8.0 10.3 %copy-start.5 = (bf16[512,64]{0,1:T(8,128)(2,1)S(1)}, bf16[512,64]{0,1:T(8,128)(2,1)}, u32[]{:S(2)}) copy-start(bf16[512,64]{0,1:T(8,128)(2,1)} %param.13) | copy-start | bytes 196612
  8.0 11.6 %copy-start.2 = (bf16[1792,128]{1,0:T(8,128)(2,1)S(1)}, bf16[1792,128]{1,0:T(8,128)(2,1)}, u32[]{:S(2)}) copy-start(bf16[1792,128]{1,0:T(8,128)(2,1)} %param.12) | copy-start | bytes 1376260
  8.0 9.3 %copy-start.9 = (s32[1,192]{1,0:T(1,128)S(1)}, s32[1,192]{1,0:T(1,128)}, u32[]{:S(2)}) copy-start(s32[1,192]{1,0:T(1,128)} %param.14) | copy-start | bytes 2308
  8.0 10.3 %copy-start.3 = (bf16[1024,512]{1,0:T(8,128)(2,1)S(1)}, bf16[1024,512]{1,0:T(8,128)(2,1)}, u32[]{:S(2)}) copy-start(bf16[1024,512]{1,0:T(8,128)(2,1)} %param.9) | copy-start | bytes 3145732
  8.1 41.0 %reduce-scatter.13.cloned.1.call-start = ((), (), s32[]{:S(2)}) async-start(), calls=%async_computation.12 | async-start | bytes 884736
  12.0 76.1 %reduce-scatter.9.cloned.1.call-start = ((), (), s32[]{:S(2)}) async-start(), calls=%async_computation.7 | async-start | bytes 884736 | tf_op jit(solution)/shard_map/reduce_scatter | solution.py:56
  17.3 75.6 %copy-start.8 = (s32[128,1]{0,1:T(1,128)S(1)}, s32[128,1]{0,1:T(1,128)}, u32[]{:S(2)}) copy-start(s32[128,1]{0,1:T(1,128)} %param.15) | copy-start | bytes 1540
  17.3 252.6 %all-reduce.3.cloned.1.call-start = ((), (), s32[]{:S(2)}) async-start(), calls=%async_computation.10 | async-start | bytes 196608
  17.6 0.6 copy-start.4
  18.3 252.6 %reduce-scatter.11.cloned.1.call-start = ((), (), s32[]{:S(2)}) async-start(), calls=%async_computation.9 | async-start | bytes 294912 | tf_op jit(solution)/shard_map/reduce_scatter | solution.py:55
  19.6 252.2 %reduce-scatter.7.cloned.1.call-start = ((), (), s32[]{:S(2)}) async-start(), calls=%async_computation.6 | async-start | bytes 589824 | tf_op jit(solution)/shard_map/reduce_scatter | solution.py:54
  23.8 364.5 %all-gather.6.cloned.1.call-start = ((), (), s32[]{:S(2)}) async-start(), calls=%async_computation.11 | async-start | bytes 8421376 | tf_op jit(solution)/shard_map/all_gather | solution.py:68
  50.6 459.3 %all-gather.4.cloned.1.call-start = ((), (), s32[]{:S(2)}) async-start(), calls=%async_computation.8 | async-start | bytes 12632064 | tf_op jit(solution)/shard_map/all_gather | solution.py:67
  95.2 545.6 %all-to-all-start.1 = ((s32[32,1,8]{2,1,0:T(1,128)}), s32[32,1,8]{2,1,0:T(1,128)S(1)}, u32[]{:S(2)}, u32[]{:S(2)}) async-start(s32[32,1,8]{2,1,0:T(1,128)} %bitcast.9), calls=%async_computation.4 | async-start | bytes 32768 | tf_op jit(solution)/shard_map/all_to_all | solution.py:105
  399.7 110.2 %copy-start.6 = (f32[128,128]{1,0:T(8,128)S(1)}, f32[128,128]{1,0:T(8,128)}, u32[]{:S(2)}) copy-start(f32[128,128]{1,0:T(8,128)} %reduce-scatter.7.cloned.1.call-done) | copy-start | bytes 196612
  412.8 110.0 %copy-start.7 = (f32[64,128]{1,0:T(8,128)S(1)}, f32[64,128]{1,0:T(8,128)}, u32[]{:S(2)}) copy-start(f32[64,128]{1,0:T(8,128)} %reduce-scatter.11.cloned.1.call-done) | copy-start | bytes 98308
  556.2 97.1 %copy-start.1 = (bf16[1536,512]{1,0:T(8,128)(2,1)S(1)}, bf16[1536,512]{1,0:T(8,128)(2,1)}, u32[]{:S(2)}) copy-start(bf16[1536,512]{1,0:T(8,128)(2,1)} %param.11) | copy-start | bytes 4718596
  640.8 11.8 %all-to-all-start = ((f32[32,1,8]{2,1,0:T(1,128)}), f32[32,1,8]{2,1,0:T(1,128)S(1)}, u32[]{:S(2)}, u32[]{:S(2)}) async-start(f32[32,1,8]{2,1,0:T(1,128)} %bitcast.6), calls=%async_computation.3 | async-start | bytes 32768 | tf_op jit(solution)/shard_map/all_to_all | solution.py:104
Sparse Core Ops, SparseCore 0:
  12.2 36.8 reduce-scatter.12
  51.7 36.3 reduce-scatter.8
  90.7 35.4 reduce-scatter.10
  128.7 36.7 reduce-scatter.6
Sparse Core Ops, SparseCore 1:
  23.3 246.6 all-reduce.2
  273.5 114.8 all-gather.5
  392.0 117.8 all-gather.3
where the time goes:
time: 662 us; the launch traced here: 661 us
  waiting for transfers between devices  444 us (67%)
  blocking collectives  74.5 us (11%)
  matrix products  53.5 us (8%)
  local copies, waits for them, and re-layouts  46.7 us (7%)
  starting transfers between devices  17.6 us (3%)
  between operations  16.4 us (2%)
  other arithmetic  7.92 us (1%)
    unnamed x9, waiting for transfers between devices  187 us
    all_gather x1, waiting for transfers between devices, shards(): part_out = lax.all_gather(target_low, ('pool', 'tgt'), axis=1, tiled=True)  116 us
    all_gather x1, waiting for transfers between devices, shards(): part_in = lax.all_gather(scaled_in, ('pool', 'tgt'), axis=1, tiled=True)  97.1 us
    psum x1, blocking collectives, squares(): return lax.psum(jnp.sum(score * score), ('pool', 'tgt'))  74.5 us
    reduce_scatter x1, waiting for transfers between devices, shards(): lax.psum_scatter(target_in_part, 'tgt', scatter_dimension=1, tiled=True)  37.5 us
    unnamed x26, local copies, waits for them, and re-layouts  18.6 us
    dot_general x1, matrix products, shards(): lax.dot_general(left_out, part_out, (((0,), (0,)), ((), ())), preferred_e...  16.7 us
    convert_element_type x1, local copies, waits for them, and re-layouts, shards(): (match_in * match_out).astype(jnp.bfloat16)  16.6 us
  transfers between devices with their start and end apart: 9, of which 6 were waited for; matrix products, arithmetic and copies ran while one was open for 16% of the time, Pallas kernels for 0%

commit v1 on v0

v1 whole, which is shorter than its diff:
```python
import functools

import jax
import jax.numpy as jnp
from jax import lax
from jax.experimental import pallas as pl
from jax.experimental.pallas import tpu as pltpu
from jax.sharding import PartitionSpec as P

KH = 128
KG = 64
ROWS = 128
TOK = 192
EX = 16
CAP = 8
GROUP = 8
F32 = jnp.float32
BF16 = jnp.bfloat16
HIGHEST = lax.Precision.HIGHEST
MSG = ROWS + TOK + (ROWS + TOK) // 2
TMSG = TOK + TOK // 2 + 16
PMSG = ROWS + ROWS // 2
MB = 1024 * 1024


def dot_nt(a, b, precision=None):
    return lax.dot_general(
        a, b, (((1,), (1,)), ((), ())), preferred_element_type=F32, precision=precision
    )


def lane_mask(shape, low):
    lane = lax.broadcasted_iota(jnp.int32, shape, 1)
    return (lane < KG) if low else (lane >= KG)


def project_kernel(order, s_ref, ph, pg, th, tg, fin, fout, *rest):
    outs, lo_ref, hi_ref = rest[:-2], rest[-2], rest[-1]
    step = pl.program_id(0)

    @pl.when(step == 0)
    def _():
        zero = jnp.zeros(fout.shape, BF16)
        lo_ref[...] = jnp.concatenate([fout[...], zero], axis=1)
        hi_ref[...] = jnp.concatenate([zero, fout[...]], axis=1)

    dot = functools.partial(jnp.dot, preferred_element_type=F32)
    pool_in = dot(ph[...], fin[...])
    tgt_in = dot(th[...], fin[...])
    half = ROWS // 2
    pool_out = dot(pg[0:half, :], lo_ref[...]) + dot(pg[half:ROWS, :], hi_ref[...])
    half = TOK // 2
    tgt_out = dot(tg[0:half, :], lo_ref[...]) + dot(tg[half:TOK, :], hi_ref[...])
    for i, out in enumerate(outs):

        @pl.when(step == i)
        def _(out=out):
            out[0:ROWS, :] = pool_in.astype(out.dtype)
            out[ROWS : ROWS + TOK, :] = tgt_in.astype(out.dtype)
            out[ROWS + TOK : ROWS + TOK + ROWS // 2, :] = pool_out.astype(out.dtype)
            out[ROWS + TOK + ROWS // 2 : MSG, :] = tgt_out.astype(out.dtype)


def project(t, order, ph, pg, th, tg, fin, fout):
    n = 8
    table = (t + jnp.array(order, jnp.int32)) % n
    row = lambda i, s: (s[i], 0)
    fixed = lambda i, s: (0, 0)
    return pl.pallas_call(
        functools.partial(project_kernel, order),
        grid_spec=pltpu.PrefetchScalarGridSpec(
            num_scalar_prefetch=1,
            grid=(len(order),),
            in_specs=[
                pl.BlockSpec((ROWS, ph.shape[1]), row),
                pl.BlockSpec((ROWS, pg.shape[1]), row),
                pl.BlockSpec((TOK, th.shape[1]), row),
                pl.BlockSpec((TOK, tg.shape[1]), row),
                pl.BlockSpec(fin.shape, fixed),
                pl.BlockSpec(fout.shape, fixed),
            ],
            out_specs=[pl.BlockSpec((MSG, KH), fixed) for _ in order],
            scratch_shapes=[pltpu.VMEM((fout.shape[0], 2 * KG), BF16)] * 2,
        ),
        out_shape=[jax.ShapeDtypeStruct((MSG, KH), BF16 if k else F32) for k in order],
        compiler_params=pltpu.CompilerParams(vmem_limit_bytes=24 * MB),
        cost_estimate=pl.CostEstimate(
            flops=len(order) * 170_000_000, bytes_accessed=len(order) * 1_600_000, transcendentals=0
        ),
        name="project",
    )(table, ph, pg, th, tg, fin, fout)


def prepare_kernel(own, *rest):
    parts, ids_ref, tmsg, pmsg, scale_ref = rest[:7], rest[7], rest[8], rest[9], rest[10]
    total = own[...]
    for part in parts:
        total = total + part[...].astype(F32)
    pool_in = total[0:ROWS]
    tgt_in = total[ROWS : ROWS + TOK]
    pool_out = total[ROWS + TOK : ROWS + TOK + ROWS // 2]
    tgt_out = total[ROWS + TOK + ROWS // 2 : MSG]

    pmsg[0:ROWS, :] = pool_in.astype(BF16)
    pmsg[ROWS:PMSG, :] = pool_out.astype(BF16)
    low = lane_mask(pool_out.shape, True)
    zero = jnp.zeros_like(pool_out)
    out_rows = jnp.concatenate(
        [jnp.where(low, pool_out, zero), jnp.where(low, zero, pool_out)], axis=0
    )
    in_sq = jnp.sum((pool_in * pool_in).T, axis=0, keepdims=True)
    out_sq = jnp.sum((out_rows * out_rows).T, axis=0, keepdims=True)
    scale_ref[...] = jnp.broadcast_to(lax.rsqrt(in_sq * out_sq + 1e-06), scale_ref.shape)

    ids = ids_ref[...].astype(F32)
    first = ids[0:1, :]
    second = jnp.where(lane_mask((1, KH), True), ids[1:2, :], -1.0)
    column = jnp.concatenate(
        [jnp.broadcast_to(first, (KH, KH)).T, jnp.broadcast_to(second, (KH, KH)).T], axis=0
    )
    same = jnp.concatenate([column == first, column == second], axis=1)
    pad = jnp.zeros((2 * KH - TOK, KH), F32)
    wide_in = jnp.concatenate([tgt_in, pad], axis=0)
    low = lane_mask(tgt_out.shape, True)
    zero = jnp.zeros_like(tgt_out)
    wide_out = jnp.concatenate(
        [
            jnp.where(low, tgt_out, zero),
            jnp.where(low, pltpu.roll(tgt_out, KG, 1), zero),
            pad,
        ],
        axis=0,
    )
    gram = dot_nt(wide_in, wide_in, HIGHEST) * dot_nt(wide_out, wide_out, HIGHEST)
    spread = jnp.sum(jnp.where(same, gram, 0.0), axis=0, keepdims=True)
    token_sq = jnp.sum(jnp.where(same, spread, 0.0), axis=1, keepdims=True)
    scaled = (tgt_in * lax.rsqrt(token_sq[0:TOK] + 1e-06)).astype(BF16)
    low_out = tgt_out.astype(BF16)
    ids_low = ids_ref[...]
    for i in range(tmsg.shape[0]):
        tmsg[i, 0:TOK, :] = scaled
        tmsg[i, TOK : TOK + TOK // 2, :] = low_out
        tmsg[i, TOK + TOK // 2 : TMSG, :] = ids_low


def prepare(own, parts, ids, copies):
    return pl.pallas_call(
        prepare_kernel,
        out_shape=[
            jax.ShapeDtypeStruct((copies, TMSG, KH), BF16),
            jax.ShapeDtypeStruct((PMSG, KH), BF16),
            jax.ShapeDtypeStruct((8, ROWS), F32),
        ],
        compiler_params=pltpu.CompilerParams(vmem_limit_bytes=24 * MB),
        cost_estimate=pl.CostEstimate(flops=200_000_000, bytes_accessed=3_000_000, transcendentals=0),
        name="prepare",
    )(own, *parts, ids)


def score_kernel(last, t_ref, *refs):
    pools, refs = refs[:8], refs[8:]
    if last:
        tmsg, prev, scale, out, pin, pout, t_in, t_out, hot, best, rows = refs
    else:
        tmsg, out, pin, pout, t_in, t_out, hot, best, rows = refs
    half = ROWS // 2
    low = lane_mask((half, KH), True)
    for k, pool in enumerate(pools):
        pin[k * ROWS : (k + 1) * ROWS, :] = pool[0:ROWS, :]
        packed = pool[ROWS:PMSG, :].astype(F32)
        turned = pltpu.roll(packed, KG, 1)
        pout[k * ROWS : k * ROWS + half, :] = jnp.where(low, packed, turned).astype(BF16)
        pout[k * ROWS + half : (k + 1) * ROWS, :] = jnp.where(low, turned, packed).astype(BF16)
    best[...] = jnp.full(best.shape, -jnp.inf, F32)

    lane = lax.broadcasted_iota(jnp.int32, (1, KH), 1)
    keep_low = (lane < KG).astype(F32).astype(BF16)
    keep_high = (lane >= KG).astype(F32).astype(BF16)
    width = GROUP * TOK
    tile = 256
    example = lax.broadcasted_iota(jnp.int32, (GROUP * EX, KH), 0).astype(F32)

    def group(g, carry):
        for pair in range(GROUP // 2):
            b0 = g * GROUP + 2 * pair
            b1 = b0 + 1
            at = pair * 2 * TOK
            t_in[at : at + TOK, :] = tmsg[b0, 0:TOK, :]
            t_in[at + TOK : at + TOK + 64, :] = tmsg[b1, 128:TOK, :]
            t_in[at + TOK + 64 : at + 2 * TOK, :] = tmsg[b1, 0:128, :]
            o0 = tmsg[b0, TOK : TOK + 96, :]
            o1 = tmsg[b1, TOK : TOK + 96, :]
            t_out[at : at + 96, :] = o0 * keep_low
            t_out[at + 96 : at + TOK, :] = o0 * keep_high
            t_out[at + TOK : at + TOK + 64, :] = o1[32:96] * keep_high
            t_out[at + TOK + 64 : at + TOK + 160, :] = o1 * keep_low
            t_out[at + TOK + 160 : at + 2 * TOK, :] = o1[0:32] * keep_high
            i0 = tmsg[b0, TOK + 96 : TMSG, :].astype(F32) + float(2 * pair * EX)
            i1 = tmsg[b1, TOK + 96 : TMSG, :].astype(F32) + float((2 * pair + 1) * EX)
            mixed = jnp.where(lane < KG, i0[1:2, :], i1[1:2, :])
            hot[:, at : at + 128] = (example == i0[0:1, :]).astype(F32).astype(BF16)
            hot[:, at + 128 : at + 256] = (example == mixed).astype(F32).astype(BF16)
            hot[:, at + 256 : at + 384] = (example == i1[0:1, :]).astype(F32).astype(BF16)

        chunk = 256

        def rows_of(c, carry):
            at = pl.ds(pl.multiple_of(c * chunk, chunk), chunk)
            left_in = pin[at, :]
            left_out = pout[at, :]
            total = None
            for i in range(width // tile):
                cols = slice(i * tile, (i + 1) * tile)
                joined = dot_nt(left_in, t_in[cols, :]) * dot_nt(left_out, t_out[cols, :])
                part = dot_nt(joined.astype(BF16), hot[:, cols])
                total = part if total is None else total + part
            best[at, :] = jnp.maximum(best[at, :], total)
            return carry

        return lax.fori_loop(0, pin.shape[0] // chunk, rows_of, carry)

    lax.fori_loop(0, tmsg.shape[0] // GROUP, group, 0)
    t = t_ref[0]
    for k in range(8):
        row = jnp.max(best[k * ROWS : (k + 1) * ROWS, :].T, axis=0, keepdims=True)
        rows[pl.ds(lax.rem(t + 8 - k, 8), 1), :] = row
    if last:
        final = jnp.maximum(rows[...], prev[...])
        for i in range(out.shape[0]):
            out[i, 0:8, :] = final
            out[i, 8:16, :] = scale[...]
    else:
        out[...] = rows[...]


def score(t, pools, tmsg, *more):
    last = len(more) > 0
    width = GROUP * TOK
    shape = (8, 16, ROWS) if last else (8, ROWS)
    vmem = pl.BlockSpec(memory_space=pltpu.VMEM)
    return pl.pallas_call(
        functools.partial(score_kernel, last),
        in_specs=[pl.BlockSpec(memory_space=pltpu.SMEM)] + [vmem] * (9 + len(more)),
        out_specs=vmem,
        out_shape=jax.ShapeDtypeStruct(shape, F32),
        scratch_shapes=[
            pltpu.VMEM((8 * ROWS, KH), BF16),
            pltpu.VMEM((8 * ROWS, KH), BF16),
            pltpu.VMEM((width, KH), BF16),
            pltpu.VMEM((width, KH), BF16),
            pltpu.VMEM((GROUP * EX, width), BF16),
            pltpu.VMEM((8 * ROWS, GROUP * EX), F32),
            pltpu.VMEM((8, ROWS), F32),
        ],
        compiler_params=pltpu.CompilerParams(vmem_limit_bytes=24 * MB),
        cost_estimate=pl.CostEstimate(
            flops=5_000_000_000, bytes_accessed=2_000_000, transcendentals=0
        ),
        name="score_last" if last else "score_first",
    )(t[None], *pools, tmsg, *more)


def slots_kernel(t_ref, got, owner, out):
    t = t_ref[0]
    first = t_ref[1]
    best = got[0, 0:8, :]
    for i in range(1, 8):
        best = jnp.maximum(best, got[i, 0:8, :])
    sub = lax.broadcasted_iota(jnp.int32, (8, ROWS), 0)
    scale = jnp.zeros((8, ROWS), F32)
    for i in range(8):
        scale = jnp.where(sub == i, got[i, 8:16, :], scale)
    value = best * scale
    square = jnp.sum(value * value)
    mine = jnp.sum(jnp.where(sub == t, value, 0.0), axis=0, keepdims=True)

    column = jnp.broadcast_to(owner[...].astype(F32), (ROWS, ROWS))
    across = column.T
    row = lax.broadcasted_iota(jnp.int32, (ROWS, ROWS), 0)
    lane = lax.broadcasted_iota(jnp.int32, (ROWS, ROWS), 1)
    earlier = jnp.where((column == across) & (row < lane), 1.0, 0.0)
    rank = jnp.sum(earlier, axis=0, keepdims=True)
    number = (first + 1 + lax.broadcasted_iota(jnp.int32, (1, ROWS), 1)).astype(F32)
    owned = jnp.where(across[0:32] == row[0:32].astype(F32), 1.0, 0.0)
    slot = row.astype(F32)
    filled = jnp.where(slot == rank, mine, 0.0) + jnp.where(slot == rank + CAP, number, 0.0)
    placed = dot_nt(owned, jnp.where(row < 2 * CAP, filled, 0.0), HIGHEST)
    out[...] = jnp.where(lane[0:32] == 2 * CAP, square, placed)


def slots(t, first, got, owner):
    vmem = pl.BlockSpec(memory_space=pltpu.VMEM)
    return pl.pallas_call(
        slots_kernel,
        in_specs=[pl.BlockSpec(memory_space=pltpu.SMEM), vmem, vmem],
        out_specs=vmem,
        out_shape=jax.ShapeDtypeStruct((32, ROWS), F32),
        name="slots",
    )(jnp.stack([t, first]), got, owner)


def finish_kernel(tokens, got, weight, token):
    square = jnp.sum(got[:, 2 * CAP : 2 * CAP + 1])
    norm = lax.rsqrt(jnp.full((1, CAP), square / tokens + 1e-06, F32))
    weight[...] = got[:, 0:CAP] * norm
    token[...] = got[:, CAP : 2 * CAP].astype(jnp.int32) - 1


def finish(got, tokens):
    return pl.pallas_call(
        functools.partial(finish_kernel, tokens),
        out_shape=[
            jax.ShapeDtypeStruct((32, CAP), F32),
            jax.ShapeDtypeStruct((32, CAP), jnp.int32),
        ],
        name="finish",
    )(got)


def shift(x, axis, n, k):
    return lax.ppermute(x, axis, [(i, (i + k) % n) for i in range(n)])


def shards(ph, pg, th, tg, fin, fout, example, owner):
    n_tgt = lax.axis_size("tgt")
    n_pool = lax.axis_size("pool")
    t = lax.axis_index("tgt")
    p = lax.axis_index("pool")
    ids = jnp.zeros((16, KH), BF16)
    wide = example.astype(BF16)
    ids = ids.at[0:1, :].set(wide[:, 0:KH])
    ids = ids.at[1:2, :].set(jnp.concatenate([wide[:, KH:TOK]] * 2, axis=1))

    order = (4, 3, 5, 2, 6, 1, 7, 0)
    messages = project(t, order, ph, pg, th, tg, fin, fout)
    parts = [shift(messages[i], "tgt", n_tgt, k) for i, k in enumerate(order) if k]
    tmsg, pmsg, scale = prepare(messages[-1], parts, ids, n_pool // 2)

    same_core = [[2 * i + c for i in range(n_pool // 2)] for c in range(2)]
    near = lax.all_to_all(
        tmsg, "pool", split_axis=0, concat_axis=0, tiled=True, axis_index_groups=same_core
    )
    pools = [pmsg] + [shift(pmsg, "tgt", n_tgt, k) for k in range(1, n_tgt)]
    far = lax.ppermute(near, "pool", [(i, i ^ 1) for i in range(n_pool)])
    partial = score(t, pools, near)
    best = score(t, pools, far, partial, scale)
    got = lax.all_to_all(best, "tgt", split_axis=0, concat_axis=0, tiled=True)
    sent = slots(t, (p * n_tgt + t) * ROWS, got, owner)
    arrived = lax.all_to_all(sent, "pool", split_axis=0, concat_axis=0, tiled=True)
    weight, token = finish(arrived, float(n_pool * n_tgt * ROWS))
    return (weight[None, None], token[None, None])


def solution(mesh):
    rows = P("pool", "tgt")
    both = P(("pool", "tgt"), None)
    placed = (rows, rows, rows, rows, P("tgt", None), P("tgt", None), both, both)
    return jax.shard_map(
        shards,
        mesh=mesh,
        in_specs=placed,
        out_specs=(P("pool", "tgt", None, None), P("pool", "tgt", None, None)),
        check_vma=False,
    )
```

time: 662 us -> 143 us (0.22)
  waiting for transfers between devices: 444 us -> 24.4 us
  matrix products: 53.5 us -> 0 us
  blocking collectives: 74.5 us -> 37.8 us
  local copies, waits for them, and re-layouts: 46.7 us -> 13.4 us
  Pallas kernels: 0 us -> 28.3 us
  starting transfers between devices: 17.6 us -> 35.8 us
  between operations: 16.4 us -> 0.73 us
    all_gather x2 -> x0, waiting for transfers between devices: 213 us -> none  [the longest x1 116 us: shards(): part_out = lax.all_gather(target_low, ('pool', 'tgt'), axis=1, tiled=True)]
    unnamed x9 -> x0, waiting for transfers between devices: 187 us -> none
    psum x1 -> x0, blocking collectives: 74.5 us -> none  [squares(): return lax.psum(jnp.sum(score * score), ('pool', 'tgt'))]
    dot_general x9 -> x0, matrix products: 51.2 us -> none  [the longest x1 16.7 us: shards(): lax.dot_general(left_out, part_out, (((0,), (0,)), ((), ())), preferred_e...]
    all_to_all x0 -> x2, blocking collectives: none -> 37.8 us  [the longest x1 24.5 us: shards(): lax.all_to_all(tmsg, 'pool', split_axis=0, concat_axis=0, tiled=True, axi...]
    reduce_scatter x3 -> x0, waiting for transfers between devices: 37.5 us -> none  [the longest x1 37.5 us: shards(): lax.psum_scatter(target_in_part, 'tgt', scatter_dimension=1, tiled=True)]
    ppermute x0 -> x15, starting transfers between devices: none -> 31.1 us  [the longest x14 29 us: shift(): return lax.ppermute(x, axis, [(i, (i + k) % n) for i in range(n)])]
    pallas_call x0 -> x6, Pallas kernels: none -> 28.3 us  [the longest x2 18.8 us: score(): pl.pallas_call(functools.partial(score_kernel, last), in_specs=[pl.BlockS...]
  transfers between devices with their start and end apart: 9 -> 16, of which waited for: 6 -> 8; matrix products, arithmetic and copies ran while one was open for 16% -> 1% of each run, Pallas kernels for 0% -> 6%
where the time goes in v1:
time: 143 us; the launch traced here: 142 us
  blocking collectives  37.8 us (26%)
  starting transfers between devices  35.8 us (25%)
  Pallas kernels  28.3 us (20%)
  waiting for transfers between devices  24.4 us (17%)
  local copies, waits for them, and re-layouts  13.4 us (9%)
    ppermute x14, starting transfers between devices, shift(): return lax.ppermute(x, axis, [(i, (i + k) % n) for i in range(n)])  29 us
    all_to_all x1, blocking collectives, shards(): lax.all_to_all(tmsg, 'pool', split_axis=0, concat_axis=0, tiled=True, axi...  24.5 us
    pallas_call x2, Pallas kernels, score(): pl.pallas_call(functools.partial(score_kernel, last), in_specs=[pl.BlockS...  18.8 us
    ppermute x14, waiting for transfers between devices, shift(): return lax.ppermute(x, axis, [(i, (i + k) % n) for i in range(n)])  18.6 us
    unnamed x20, local copies, waits for them, and re-layouts  13.3 us
    all_to_all x1, blocking collectives, shards(): lax.all_to_all(sent, 'pool', split_axis=0, concat_axis=0, tiled=True)  13.2 us
    all_to_all x1, waiting for transfers between devices, shards(): got = lax.all_to_all(best, 'tgt', split_axis=0, concat_axis=0, tiled=True)  5.85 us
    pallas_call x1, Pallas kernels, project(): pl.pallas_call(functools.partial(project_kernel, order), grid_spec=pltpu....  5.45 us
  transfers between devices with their start and end apart: 16, of which 8 were waited for; matrix products, arithmetic and copies ran while one was open for 1% of the time, Pallas kernels for 6%

profile of v1, /device:TPU:1, one launch (start us, length us, event | category | flops | bytes accessed | tf_op | source)
XLA Modules:
  0.0 141.8 jit_solution(5886647256767781134)
XLA Ops:
  2.3 2.6 %copy-done = bf16[1536,1792]{1,0:T(8,128)(2,1)S(1)} copy-done((bf16[1536,1792]{1,0:T(8,128)(2,1)S(1)}, bf16[1536,1792]{1,0:T(8,128)(2,1)}, u32[]{:S(2)}) %copy-start) | copy-done | bytes 5505048
  4.8 2.0 %copy-done.1 = bf16[1024,1792]{1,0:T(8,128)(2,1)S(1)} copy-done((bf16[1024,1792]{1,0:T(8,128)(2,1)S(1)}, bf16[1024,1792]{1,0:T(8,128)(2,1)}, u32[]{:S(2)}) %copy-start.1) | copy-done | bytes 3670040
  10.5 5.4 %project.1 = (bf16[480,128]{1,0:T(8,128)(2,1)S(1)}, bf16[480,128]{1,0:T(8,128)(2,1)S(1)}, bf16[480,128]{1,0:T(8,128)(2,1)S(1)}, bf16[480,128]{1,0:T(8,128)(2,1)S...) custom-call(s32[8]{0:T(128)S(1)} %and_select_fusion.s_ref, ...), custom_call_target="tpu_custom_call" | custom-call | flops 1360000000 | bytes 12800000 | tf_op jit(solution)/shard_map/project/pallas_call | solution.py:69
  16.0 7.8 %collective-permute-start = (bf16[480,128]{1,0:T(8,128)(2,1)S(1)}, bf16[480,128]{1,0:T(8,128)(2,1)S(1)}, u32[]{:S(2)}, u32[]{:S(2)}) collective-permute-start(bf16[480,128]{1,0:T(8,128)(2,1)S(1)} %get-tuple-element.40), channel_id=1, source_target_pairs={{0,4},{1,5},{2,6},{3,7},{4,0},{5,1},{6,2},{7,3},{8,12},{9,13},{10,... | collective-permute-start | bytes 368648 | tf_op jit(solution)/shard_map/ppermute | solution.py:321
  23.8 1.6 %collective-permute-start.1 = (bf16[480,128]{1,0:T(8,128)(2,1)S(1)}, bf16[480,128]{1,0:T(8,128)(2,1)S(1)}, u32[]{:S(2)}, u32[]{:S(2)}) collective-permute-start(bf16[480,128]{1,0:T(8,128)(2,1)S(1)} %get-tuple-element.41), channel_id=1, source_target_pairs={{0,3},{1,4},{2,5},{3,6},{4,7},{5,0},{6,1},{7,2},{8,11},{9,12},{10,... | collective-permute-start | bytes 368648 | tf_op jit(solution)/shard_map/ppermute | solution.py:321
  25.4 2.8 %collective-permute-start.2 = (bf16[480,128]{1,0:T(8,128)(2,1)S(1)}, bf16[480,128]{1,0:T(8,128)(2,1)S(1)}, u32[]{:S(2)}, u32[]{:S(2)}) collective-permute-start(bf16[480,128]{1,0:T(8,128)(2,1)S(1)} %get-tuple-element.42), channel_id=1, source_target_pairs={{0,5},{1,6},{2,7},{3,0},{4,1},{5,2},{6,3},{7,4},{8,13},{9,14},{10,... | collective-permute-start | bytes 368648 | tf_op jit(solution)/shard_map/ppermute | solution.py:321
  29.5 2.4 %collective-permute-start.4 = (bf16[480,128]{1,0:T(8,128)(2,1)S(1)}, bf16[480,128]{1,0:T(8,128)(2,1)S(1)}, u32[]{:S(2)}, u32[]{:S(2)}) collective-permute-start(bf16[480,128]{1,0:T(8,128)(2,1)S(1)} %get-tuple-element.44), channel_id=1, source_target_pairs={{0,6},{1,7},{2,0},{3,1},{4,2},{5,3},{6,4},{7,5},{8,14},{9,15},{10,... | collective-permute-start | bytes 368648 | tf_op jit(solution)/shard_map/ppermute | solution.py:321
  32.6 7.2 %collective-permute-done.1.rest_1_ = bf16[480,128]{1,0:T(8,128)(2,1)S(1)} collective-permute-done((bf16[480,128]{1,0:T(8,128)(2,1)S(1)}, bf16[480,128]{1,0:T(8,128)(2,1)S(1)}, u32[]{:S(2)}, u32[]{:S(2)}) %collective-permute-start.1) | collective-permute-done | bytes 122912 | tf_op jit(solution)/shard_map/ppermute | solution.py:321
  39.9 3.1 %collective-permute-done.4.rest_4_ = bf16[480,128]{1,0:T(8,128)(2,1)S(1)} collective-permute-done((bf16[480,128]{1,0:T(8,128)(2,1)S(1)}, bf16[480,128]{1,0:T(8,128)(2,1)S(1)}, u32[]{:S(2)}, u32[]{:S(2)}) %collective-permute-start.4) | collective-permute-done | bytes 122912 | tf_op jit(solution)/shard_map/ppermute | solution.py:321
  43.0 3.0 %collective-permute-done.5.rest_5_ = bf16[480,128]{1,0:T(8,128)(2,1)S(1)} collective-permute-done((bf16[480,128]{1,0:T(8,128)(2,1)S(1)}, bf16[480,128]{1,0:T(8,128)(2,1)S(1)}, u32[]{:S(2)}, u32[]{:S(2)}) %collective-permute-start.5) | collective-permute-done | bytes 122912 | tf_op jit(solution)/shard_map/ppermute | solution.py:321
  47.5 24.5 %all_to_all.21.refs_8_ = bf16[16,304,128]{2,1,0:T(8,128)(2,1)S(1)} all-to-all(bf16[16,304,128]{2,1,0:T(8,128)(2,1)S(1)} %get-tuple-element.48), channel_id=1, replica_groups={{0,16,32,48,64,80,96,112,128,144,160,176,192,208,224,240},{8,24,40,56,7..., dimensions={0} | all-to-all | bytes 2490368 | tf_op jit(solution)/shard_map/all_to_all | solution.py:340
  72.0 2.1 %collective-permute-start.14 = (bf16[16,304,128]{2,1,0:T(8,128)(2,1)S(1)}, bf16[16,304,128]{2,1,0:T(8,128)(2,1)S(1)}, u32[]{:S(2)}, u32[]{:S(2)}) collective-permute-start(bf16[16,304,128]{2,1,0:T(8,128)(2,1)S(1)} %all_to_all.21.refs_8_), channel_id=1, source_target_pairs={{0,8},{8,0},{16,24},{24,16},{32,40},{40,32},{48,56},{56,48},{64,72... | collective-permute-start | bytes 3735560 | tf_op jit(solution)/shard_map/ppermute | solution.py:344
  75.4 1.9 %collective-permute-start.9 = (bf16[192,128]{1,0:T(8,128)(2,1)S(1)}, bf16[192,128]{1,0:T(8,128)(2,1)S(1)}, u32[]{:S(2)}, u32[]{:S(2)}) collective-permute-start(bf16[192,128]{1,0:T(8,128)(2,1)S(1)} %get-tuple-element.47.refs_0_), channel_id=1, source_target_pairs={{0,3},{1,4},{2,5},{3,6},{4,7},{5,0},{6,1},{7,2},{8,11},{9,12},{10,... | collective-permute-start | bytes 147464 | tf_op jit(solution)/shard_map/ppermute | solution.py:321
  77.2 3.3 %collective-permute-start.10 = (bf16[192,128]{1,0:T(8,128)(2,1)S(1)}, bf16[192,128]{1,0:T(8,128)(2,1)S(1)}, u32[]{:S(2)}, u32[]{:S(2)}) collective-permute-start(bf16[192,128]{1,0:T(8,128)(2,1)S(1)} %get-tuple-element.47.refs_0_), channel_id=1, source_target_pairs={{0,4},{1,5},{2,6},{3,7},{4,0},{5,1},{6,2},{7,3},{8,12},{9,13},{10,... | collective-permute-start | bytes 147464 | tf_op jit(solution)/shard_map/ppermute | solution.py:321
  80.5 3.7 %collective-permute-start.11 = (bf16[192,128]{1,0:T(8,128)(2,1)S(1)}, bf16[192,128]{1,0:T(8,128)(2,1)S(1)}, u32[]{:S(2)}, u32[]{:S(2)}) collective-permute-start(bf16[192,128]{1,0:T(8,128)(2,1)S(1)} %get-tuple-element.47.refs_0_), channel_id=1, source_target_pairs={{0,5},{1,6},{2,7},{3,0},{4,1},{5,2},{6,3},{7,4},{8,13},{9,14},{10,... | collective-permute-start | bytes 147464 | tf_op jit(solution)/shard_map/ppermute | solution.py:321
  85.0 1.5 %collective-permute-start.13 = (bf16[192,128]{1,0:T(8,128)(2,1)S(1)}, bf16[192,128]{1,0:T(8,128)(2,1)S(1)}, u32[]{:S(2)}, u32[]{:S(2)}) collective-permute-start(bf16[192,128]{1,0:T(8,128)(2,1)S(1)} %get-tuple-element.47.refs_0_), channel_id=1, source_target_pairs={{0,7},{1,0},{2,1},{3,2},{4,3},{5,4},{6,5},{7,6},{8,15},{9,8},{10,9... | collective-permute-start | bytes 147464 | tf_op jit(solution)/shard_map/ppermute | solution.py:321
  87.3 3.8 %collective-permute-done.12.refs_6_ = bf16[192,128]{1,0:T(8,128)(2,1)S(1)} collective-permute-done((bf16[192,128]{1,0:T(8,128)(2,1)S(1)}, bf16[192,128]{1,0:T(8,128)(2,1)S(1)}, u32[]{:S(2)}, u32[]{:S(2)}) %collective-permute-start.12) | collective-permute-done | bytes 49184 | tf_op jit(solution)/shard_map/ppermute | solution.py:321
  91.1 9.1 %score_first.1.refs_9_ = f32[8,128]{1,0:T(8,128)S(1)} custom-call(s32[1]{0:T(128)} %bitcast.t_ref, bf16[192,128]{1,0:T(8,128)(2,1)S(1)} %get-tuple-element.47.refs_0_, bf16[192,128]{1,0:T(8,128)(2,1)S(1)} %collective-permute-done.7.refs_1_, bf16[192,128]{1,0:T(8,128)(2,1)S(1)} %collective-permute-done.8.refs_2_, ...), custom_call_target="tpu_custom_call" | custom-call | flops 5000000000 | bytes 2000000 | tf_op jit(solution)/shard_map/score_first/pallas_call | solution.py:241
  100.2 9.7 %score_last.1 = f32[8,16,128]{2,1,0:T(8,128)} custom-call(s32[1]{0:T(128)} %bitcast.t_ref, bf16[192,128]{1,0:T(8,128)(2,1)S(1)} %get-tuple-element.47.refs_0_, bf16[192,128]{1,0:T(8,128)(2,1)S(1)} %collective-permute-done.7.refs_1_, bf16[192,128]{1,0:T(8,128)(2,1)S(1)} %collective-permute-done.8.refs_2_, ...), custom_call_target="tpu_custom_call" | custom-call | flops 5000000000 | bytes 2000000 | tf_op jit(solution)/shard_map/score_last/pallas_call | solution.py:241
  110.0 4.7 %all-to-all-start.1 = ((f32[8,16,128]{2,1,0:T(8,128)}), f32[8,16,128]{2,1,0:T(8,128)S(1)}, u32[]{:S(2)}, u32[]{:S(2)}) async-start(f32[8,16,128]{2,1,0:T(8,128)} %score_last.1), calls=%async_computation.1 | async-start | bytes 131072 | tf_op jit(solution)/shard_map/all_to_all | solution.py:347
  116.0 5.9 %all-to-all-done.1.got = f32[8,16,128]{2,1,0:T(8,128)S(1)} async-done(((f32[8,16,128]{2,1,0:T(8,128)}), f32[8,16,128]{2,1,0:T(8,128)S(1)}, u32[]{:S(2)}, u32[]{:S(2)}) %all-to-all-start.1) | async-done | bytes 65568 | tf_op jit(solution)/shard_map/all_to_all | solution.py:347
  122.5 1.8 %slots.1 = f32[32,128]{1,0:T(8,128)} custom-call(s32[2]{0:T(128)} %pad_add_fusion.t_ref, f32[8,16,128]{2,1,0:T(8,128)} %copy-done.5, s32[128,1]{1,0:T(8,128)} %copy.16.owner), custom_call_target="tpu_custom_call" | custom-call | tf_op jit(solution)/shard_map/slots/pallas_call | solution.py:293
  124.3 13.2 %all_to_all.22 = f32[32,1,128]{2,1,0:T(1,128)} all-to-all(f32[32,1,128]{2,1,0:T(1,128)} %bitcast.8), channel_id=1, replica_groups=mesh['pool'=32,'tgt'=8] {'pool'}, dimensions={0} | all-to-all | bytes 32768 | tf_op jit(solution)/shard_map/all_to_all | solution.py:349
  137.5 1.5 %finish.1 = (f32[32,8]{1,0:T(8,128)}, s32[32,8]{1,0:T(8,128)}) custom-call(f32[32,128]{1,0:T(8,128)} %bitcast.9), custom_call_target="tpu_custom_call" | custom-call | tf_op jit(solution)/shard_map/finish/pallas_call | solution.py:310
  (44 shorter events, 16.5 us)
Async XLA Ops:
  2.3 2.6 %copy-start = (bf16[1536,1792]{1,0:T(8,128)(2,1)S(1)}, bf16[1536,1792]{1,0:T(8,128)(2,1)}, u32[]{:S(2)}) copy-start(bf16[1536,1792]{1,0:T(8,128)(2,1)} %th.1) | copy-start | bytes 16515076
  4.8 2.0 %copy-start.1 = (bf16[1024,1792]{1,0:T(8,128)(2,1)S(1)}, bf16[1024,1792]{1,0:T(8,128)(2,1)}, u32[]{:S(2)}) copy-start(bf16[1024,1792]{1,0:T(8,128)(2,1)} %ph.1) | copy-start | bytes 11010052
  6.9 1.4 copy-start.2
  8.3 1.2 copy-start.3
  9.5 1.0 copy-start.4
  10.5 29.2 %copy-start.6 = (s32[1,192]{1,0:T(1,128)S(1)}, s32[1,192]{1,0:T(1,128)}, u32[]{:S(2)}) copy-start(s32[1,192]{1,0:T(1,128)} %param.19) | copy-start | bytes 2308
  16.0 15.9 %collective-permute-start = (bf16[480,128]{1,0:T(8,128)(2,1)S(1)}, bf16[480,128]{1,0:T(8,128)(2,1)S(1)}, u32[]{:S(2)}, u32[]{:S(2)}) collective-permute-start(bf16[480,128]{1,0:T(8,128)(2,1)S(1)} %get-tuple-element.40), channel_id=1, source_target_pairs={{0,4},{1,5},{2,6},{3,7},{4,0},{5,1},{6,2},{7,3},{8,12},{9,13},{10,... | collective-permute-start | bytes 368648 | tf_op jit(solution)/shard_map/ppermute | solution.py:321
  23.8 15.9 %collective-permute-start.1 = (bf16[480,128]{1,0:T(8,128)(2,1)S(1)}, bf16[480,128]{1,0:T(8,128)(2,1)S(1)}, u32[]{:S(2)}, u32[]{:S(2)}) collective-permute-start(bf16[480,128]{1,0:T(8,128)(2,1)S(1)} %get-tuple-element.41), channel_id=1, source_target_pairs={{0,3},{1,4},{2,5},{3,6},{4,7},{5,0},{6,1},{7,2},{8,11},{9,12},{10,... | collective-permute-start | bytes 368648 | tf_op jit(solution)/shard_map/ppermute | solution.py:321
  25.4 14.5 %collective-permute-start.2 = (bf16[480,128]{1,0:T(8,128)(2,1)S(1)}, bf16[480,128]{1,0:T(8,128)(2,1)S(1)}, u32[]{:S(2)}, u32[]{:S(2)}) collective-permute-start(bf16[480,128]{1,0:T(8,128)(2,1)S(1)} %get-tuple-element.42), channel_id=1, source_target_pairs={{0,5},{1,6},{2,7},{3,0},{4,1},{5,2},{6,3},{7,4},{8,13},{9,14},{10,... | collective-permute-start | bytes 368648 | tf_op jit(solution)/shard_map/ppermute | solution.py:321
  28.3 11.6 %collective-permute-start.3 = (bf16[480,128]{1,0:T(8,128)(2,1)S(1)}, bf16[480,128]{1,0:T(8,128)(2,1)S(1)}, u32[]{:S(2)}, u32[]{:S(2)}) collective-permute-start(bf16[480,128]{1,0:T(8,128)(2,1)S(1)} %get-tuple-element.43), channel_id=1, source_target_pairs={{0,2},{1,3},{2,4},{3,5},{4,6},{5,7},{6,0},{7,1},{8,10},{9,11},{10,... | collective-permute-start | bytes 368648 | tf_op jit(solution)/shard_map/ppermute | solution.py:321
  29.5 13.5 %collective-permute-start.4 = (bf16[480,128]{1,0:T(8,128)(2,1)S(1)}, bf16[480,128]{1,0:T(8,128)(2,1)S(1)}, u32[]{:S(2)}, u32[]{:S(2)}) collective-permute-start(bf16[480,128]{1,0:T(8,128)(2,1)S(1)} %get-tuple-element.44), channel_id=1, source_target_pairs={{0,6},{1,7},{2,0},{3,1},{4,2},{5,3},{6,4},{7,5},{8,14},{9,15},{10,... | collective-permute-start | bytes 368648 | tf_op jit(solution)/shard_map/ppermute | solution.py:321
  31.9 14.1 %collective-permute-start.5 = (bf16[480,128]{1,0:T(8,128)(2,1)S(1)}, bf16[480,128]{1,0:T(8,128)(2,1)S(1)}, u32[]{:S(2)}, u32[]{:S(2)}) collective-permute-start(bf16[480,128]{1,0:T(8,128)(2,1)S(1)} %get-tuple-element.45), channel_id=1, source_target_pairs={{0,1},{1,2},{2,3},{3,4},{4,5},{5,6},{6,7},{7,0},{8,9},{9,10},{10,1... | collective-permute-start | bytes 368648 | tf_op jit(solution)/shard_map/ppermute | solution.py:321
  39.8 6.9 %collective-permute-start.6 = (bf16[480,128]{1,0:T(8,128)(2,1)S(1)}, bf16[480,128]{1,0:T(8,128)(2,1)S(1)}, u32[]{:S(2)}, u32[]{:S(2)}) collective-permute-start(bf16[480,128]{1,0:T(8,128)(2,1)S(1)} %get-tuple-element.46), channel_id=1, source_target_pairs={{0,7},{1,0},{2,1},{3,2},{4,3},{5,4},{6,5},{7,6},{8,15},{9,8},{10,9... | collective-permute-start | bytes 368648 | tf_op jit(solution)/shard_map/ppermute | solution.py:321
  72.0 28.2 %collective-permute-start.14 = (bf16[16,304,128]{2,1,0:T(8,128)(2,1)S(1)}, bf16[16,304,128]{2,1,0:T(8,128)(2,1)S(1)}, u32[]{:S(2)}, u32[]{:S(2)}) collective-permute-start(bf16[16,304,128]{2,1,0:T(8,128)(2,1)S(1)} %all_to_all.21.refs_8_), channel_id=1, source_target_pairs={{0,8},{8,0},{16,24},{24,16},{32,40},{40,32},{48,56},{56,48},{64,72... | collective-permute-start | bytes 3735560 | tf_op jit(solution)/shard_map/ppermute | solution.py:344
  74.1 6.5 %collective-permute-start.7 = (bf16[192,128]{1,0:T(8,128)(2,1)S(1)}, bf16[192,128]{1,0:T(8,128)(2,1)S(1)}, u32[]{:S(2)}, u32[]{:S(2)}) collective-permute-start(bf16[192,128]{1,0:T(8,128)(2,1)S(1)} %get-tuple-element.47.refs_0_), channel_id=1, source_target_pairs={{0,1},{1,2},{2,3},{3,4},{4,5},{5,6},{6,7},{7,0},{8,9},{9,10},{10,1... | collective-permute-start | bytes 147464 | tf_op jit(solution)/shard_map/ppermute | solution.py:321
  74.1 10.2 %collective-permute-start.8 = (bf16[192,128]{1,0:T(8,128)(2,1)S(1)}, bf16[192,128]{1,0:T(8,128)(2,1)S(1)}, u32[]{:S(2)}, u32[]{:S(2)}) collective-permute-start(bf16[192,128]{1,0:T(8,128)(2,1)S(1)} %get-tuple-element.47.refs_0_), channel_id=1, source_target_pairs={{0,2},{1,3},{2,4},{3,5},{4,6},{5,7},{6,0},{7,1},{8,10},{9,11},{10,... | collective-permute-start | bytes 147464 | tf_op jit(solution)/shard_map/ppermute | solution.py:321
  75.4 9.6 %collective-permute-start.9 = (bf16[192,128]{1,0:T(8,128)(2,1)S(1)}, bf16[192,128]{1,0:T(8,128)(2,1)S(1)}, u32[]{:S(2)}, u32[]{:S(2)}) collective-permute-start(bf16[192,128]{1,0:T(8,128)(2,1)S(1)} %get-tuple-element.47.refs_0_), channel_id=1, source_target_pairs={{0,3},{1,4},{2,5},{3,6},{4,7},{5,0},{6,1},{7,2},{8,11},{9,12},{10,... | collective-permute-start | bytes 147464 | tf_op jit(solution)/shard_map/ppermute | solution.py:321
  77.2 9.8 %collective-permute-start.10 = (bf16[192,128]{1,0:T(8,128)(2,1)S(1)}, bf16[192,128]{1,0:T(8,128)(2,1)S(1)}, u32[]{:S(2)}, u32[]{:S(2)}) collective-permute-start(bf16[192,128]{1,0:T(8,128)(2,1)S(1)} %get-tuple-element.47.refs_0_), channel_id=1, source_target_pairs={{0,4},{1,5},{2,6},{3,7},{4,0},{5,1},{6,2},{7,3},{8,12},{9,13},{10,... | collective-permute-start | bytes 147464 | tf_op jit(solution)/shard_map/ppermute | solution.py:321
  80.5 6.8 %collective-permute-start.11 = (bf16[192,128]{1,0:T(8,128)(2,1)S(1)}, bf16[192,128]{1,0:T(8,128)(2,1)S(1)}, u32[]{:S(2)}, u32[]{:S(2)}) collective-permute-start(bf16[192,128]{1,0:T(8,128)(2,1)S(1)} %get-tuple-element.47.refs_0_), channel_id=1, source_target_pairs={{0,5},{1,6},{2,7},{3,0},{4,1},{5,2},{6,3},{7,4},{8,13},{9,14},{10,... | collective-permute-start | bytes 147464 | tf_op jit(solution)/shard_map/ppermute | solution.py:321
  84.2 6.9 %collective-permute-start.12 = (bf16[192,128]{1,0:T(8,128)(2,1)S(1)}, bf16[192,128]{1,0:T(8,128)(2,1)S(1)}, u32[]{:S(2)}, u32[]{:S(2)}) collective-permute-start(bf16[192,128]{1,0:T(8,128)(2,1)S(1)} %get-tuple-element.47.refs_0_), channel_id=1, source_target_pairs={{0,6},{1,7},{2,0},{3,1},{4,2},{5,3},{6,4},{7,5},{8,14},{9,15},{10,... | collective-permute-start | bytes 147464 | tf_op jit(solution)/shard_map/ppermute | solution.py:321
  85.0 6.1 %collective-permute-start.13 = (bf16[192,128]{1,0:T(8,128)(2,1)S(1)}, bf16[192,128]{1,0:T(8,128)(2,1)S(1)}, u32[]{:S(2)}, u32[]{:S(2)}) collective-permute-start(bf16[192,128]{1,0:T(8,128)(2,1)S(1)} %get-tuple-element.47.refs_0_), channel_id=1, source_target_pairs={{0,7},{1,0},{2,1},{3,2},{4,3},{5,4},{6,5},{7,6},{8,15},{9,8},{10,9... | collective-permute-start | bytes 147464 | tf_op jit(solution)/shard_map/ppermute | solution.py:321
  100.2 14.4 %copy-start.7 = (s32[128,1]{0,1:T(1,128)S(1)}, s32[128,1]{0,1:T(1,128)}, u32[]{:S(2)}) copy-start(s32[128,1]{0,1:T(1,128)} %param.20) | copy-start | bytes 1540
  110.0 11.9 %all-to-all-start.1 = ((f32[8,16,128]{2,1,0:T(8,128)}), f32[8,16,128]{2,1,0:T(8,128)S(1)}, u32[]{:S(2)}, u32[]{:S(2)}) async-start(f32[8,16,128]{2,1,0:T(8,128)} %score_last.1), calls=%async_computation.1 | async-start | bytes 131072 | tf_op jit(solution)/shard_map/all_to_all | solution.py:347
  121.9 0.6 copy-start.5

commit v2 on v1

--- a/solution.py
+++ b/solution.py
@@ -21,6 +21,7 @@
 TMSG = TOK + TOK // 2 + 16
 PMSG = ROWS + ROWS // 2
 MB = 1024 * 1024
+LIMITS = (53, 53, 53)
 
 
 def dot_nt(a, b, precision=None):
@@ -34,68 +35,105 @@
     return (lane < KG) if low else (lane >= KG)
 
 
-def project_kernel(order, s_ref, ph, pg, th, tg, fin, fout, *rest):
-    outs, lo_ref, hi_ref = rest[:-2], rest[-2], rest[-1]
-    step = pl.program_id(0)
-
-    @pl.when(step == 0)
-    def _():
-        zero = jnp.zeros(fout.shape, BF16)
-        lo_ref[...] = jnp.concatenate([fout[...], zero], axis=1)
-        hi_ref[...] = jnp.concatenate([zero, fout[...]], axis=1)
-
-    dot = functools.partial(jnp.dot, preferred_element_type=F32)
-    pool_in = dot(ph[...], fin[...])
-    tgt_in = dot(th[...], fin[...])
-    half = ROWS // 2
-    pool_out = dot(pg[0:half, :], lo_ref[...]) + dot(pg[half:ROWS, :], hi_ref[...])
-    half = TOK // 2
-    tgt_out = dot(tg[0:half, :], lo_ref[...]) + dot(tg[half:TOK, :], hi_ref[...])
-    for i, out in enumerate(outs):
-
-        @pl.when(step == i)
-        def _(out=out):
-            out[0:ROWS, :] = pool_in.astype(out.dtype)
-            out[ROWS : ROWS + TOK, :] = tgt_in.astype(out.dtype)
-            out[ROWS + TOK : ROWS + TOK + ROWS // 2, :] = pool_out.astype(out.dtype)
-            out[ROWS + TOK + ROWS // 2 : MSG, :] = tgt_out.astype(out.dtype)
-
-
-def project(t, order, ph, pg, th, tg, fin, fout):
-    n = 8
-    table = (t + jnp.array(order, jnp.int32)) % n
-    row = lambda i, s: (s[i], 0)
-    fixed = lambda i, s: (0, 0)
-    return pl.pallas_call(
-        functools.partial(project_kernel, order),
-        grid_spec=pltpu.PrefetchScalarGridSpec(
-            num_scalar_prefetch=1,
-            grid=(len(order),),
-            in_specs=[
-                pl.BlockSpec((ROWS, ph.shape[1]), row),
-                pl.BlockSpec((ROWS, pg.shape[1]), row),
-                pl.BlockSpec((TOK, th.shape[1]), row),
-                pl.BlockSpec((TOK, tg.shape[1]), row),
-                pl.BlockSpec(fin.shape, fixed),
-                pl.BlockSpec(fout.shape, fixed),
-            ],
-            out_specs=[pl.BlockSpec((MSG, KH), fixed) for _ in order],
-            scratch_shapes=[pltpu.VMEM((fout.shape[0], 2 * KG), BF16)] * 2,
-        ),
-        out_shape=[jax.ShapeDtypeStruct((MSG, KH), BF16 if k else F32) for k in order],
-        compiler_params=pltpu.CompilerParams(vmem_limit_bytes=24 * MB),
+def project_kernel(steps, kinds, t_ref, ph, pg, th, tg, fin, fout, *rest):
+    outs, (rows_in, rows_out, fin_v, fout_v, sems) = rest[:-5], rest[-5:]
+    t = t_ref[0]
+    weights = [
+        pltpu.make_async_copy(fout, fout_v, sems.at[0, 0]),
+        pltpu.make_async_copy(fin, fin_v, sems.at[0, 1]),
+    ]
+    for copy in weights:
+        copy.start()
+    moves = []
+    both = ROWS + TOK
+    for i, k in enumerate(steps):
+        who = lax.rem(t + k, 8)
+        pool = pl.ds(pl.multiple_of(who * ROWS, ROWS), ROWS)
+        tgt = pl.ds(pl.multiple_of(who * TOK, TOK), TOK)
+        at_pool = pl.ds(i * both, ROWS)
+        at_tgt = pl.ds(i * both + ROWS, TOK)
+        here = [
+            pltpu.make_async_copy(pg.at[pool, :], rows_out.at[at_pool, :], sems.at[i + 1, 0]),
+            pltpu.make_async_copy(tg.at[tgt, :], rows_out.at[at_tgt, :], sems.at[i + 1, 1]),
+            pltpu.make_async_copy(ph.at[pool, :], rows_in.at[at_pool, :], sems.at[i + 1, 2]),
+            pltpu.make_async_copy(th.at[tgt, :], rows_in.at[at_tgt, :], sems.at[i + 1, 3]),
+        ]
+        for copy in here:
+            copy.start()
+        moves.append(here)
+    for copy in weights:
+        copy.wait()
+    together = min(2, len(steps))
+    for first in range(0, len(steps), together):
+        count = min(together, len(steps) - first)
+        for i in range(first, first + count):
+            for copy in moves[i]:
+                copy.wait()
+        rows = slice(first * both, (first + count) * both)
+        sums_out = dot_nt(rows_out[rows, :], fout_v[...])
+        sums_in = jnp.dot(rows_in[rows, :], fin_v[...], preferred_element_type=F32)
+        for i in range(first, first + count):
+            which, slot = kinds[i]
+            out = outs[which]
+            lead = (i - first) * both
+            at = slot * MSG
+            out[at : at + both, :] = sums_in[lead : lead + both].astype(out.dtype)
+            at = at + both
+            for size in (ROWS, TOK):
+                half = size // 2
+                packed = jnp.concatenate(
+                    [sums_out[lead : lead + half], sums_out[lead + half : lead + size]], axis=1
+                )
+                out[at : at + half, :] = packed.astype(out.dtype)
+                lead = lead + size
+                at = at + half
+
+
+def project(limit, t, steps, kinds, dtypes, ph, pg, th, tg, fin, fout):
+    n = len(steps)
+    sizes = [sum(1 for which, _ in kinds if which == j) for j in range(len(dtypes))]
+    hbm = pl.BlockSpec(memory_space=pltpu.HBM)
+    vmem = pl.BlockSpec(memory_space=pltpu.VMEM)
+    return pl.pallas_call(
+        functools.partial(project_kernel, steps, kinds),
+        in_specs=[pl.BlockSpec(memory_space=pltpu.SMEM)] + [hbm] * 6,
+        out_specs=[vmem for _ in dtypes],
+        out_shape=[jax.ShapeDtypeStruct((c * MSG, KH), d) for c, d in zip(sizes, dtypes)],
+        scratch_shapes=[
+            pltpu.VMEM((n * (ROWS + TOK), ph.shape[1]), BF16),
+            pltpu.VMEM((n * (ROWS + TOK), pg.shape[1]), BF16),
+            pltpu.VMEM(fin.shape, BF16),
+            pltpu.VMEM(fout.shape, BF16),
+            pltpu.SemaphoreType.DMA((n + 1, 4)),
+        ],
+        compiler_params=pltpu.CompilerParams(vmem_limit_bytes=limit * MB),
         cost_estimate=pl.CostEstimate(
-            flops=len(order) * 170_000_000, bytes_accessed=len(order) * 1_600_000, transcendentals=0
+            flops=n * 170_000_000, bytes_accessed=n * 1_600_000, transcendentals=0
         ),
         name="project",
-    )(table, ph, pg, th, tg, fin, fout)
+    )(t[None], ph, pg, th, tg, fin, fout)
+
+
+def merge_kernel(from_low, from_high, mine_up, mine_down, up, down):
+    up[...] = (mine_up[...] + from_low[MSG : 2 * MSG, :].astype(F32)).astype(BF16)
+    down[...] = (mine_down[...] + from_high[MSG : 2 * MSG, :].astype(F32)).astype(BF16)
+
+
+def merge(*operands):
+    return pl.pallas_call(
+        merge_kernel,
+        out_shape=[jax.ShapeDtypeStruct((MSG, KH), BF16)] * 2,
+        compiler_params=pltpu.CompilerParams(vmem_limit_bytes=8 * MB),
+        cost_estimate=pl.CostEstimate(flops=200_000, bytes_accessed=1_500_000, transcendentals=0),
+        name="merge",
+    )(*operands)
 
 
 def prepare_kernel(own, *rest):
-    parts, ids_ref, tmsg, pmsg, scale_ref = rest[:7], rest[7], rest[8], rest[9], rest[10]
+    parts, (ids_ref, tmsg, pmsg, scale_ref) = rest[:-4], rest[-4:]
     total = own[...]
     for part in parts:
-        total = total + part[...].astype(F32)
+        total = total + part[0:MSG, :].astype(F32)
     pool_in = total[0:ROWS]
     tgt_in = total[ROWS : ROWS + TOK]
     pool_out = total[ROWS + TOK : ROWS + TOK + ROWS // 2]
@@ -177,7 +215,7 @@
     keep_low = (lane < KG).astype(F32).astype(BF16)
     keep_high = (lane >= KG).astype(F32).astype(BF16)
     width = GROUP * TOK
-    tile = 256
+    tile = 512
     example = lax.broadcasted_iota(jnp.int32, (GROUP * EX, KH), 0).astype(F32)
 
     def group(g, carry):
@@ -202,7 +240,7 @@
             hot[:, at + 128 : at + 256] = (example == mixed).astype(F32).astype(BF16)
             hot[:, at + 256 : at + 384] = (example == i1[0:1, :]).astype(F32).astype(BF16)
 
-        chunk = 256
+        chunk = 512
 
         def rows_of(c, carry):
             at = pl.ds(pl.multiple_of(c * chunk, chunk), chunk)
@@ -260,9 +298,9 @@
     )(t[None], *pools, tmsg, *more)
 
 
-def slots_kernel(t_ref, got, owner, out):
+def slots_kernel(t_ref, p_ref, got, owner, out):
     t = t_ref[0]
-    first = t_ref[1]
+    first = (p_ref[0] * 8 + t) * ROWS
     best = got[0, 0:8, :]
     for i in range(1, 8):
         best = jnp.maximum(best, got[i, 0:8, :])
@@ -274,8 +312,8 @@
     square = jnp.sum(value * value)
     mine = jnp.sum(jnp.where(sub == t, value, 0.0), axis=0, keepdims=True)
 
-    column = jnp.broadcast_to(owner[...].astype(F32), (ROWS, ROWS))
-    across = column.T
+    across = jnp.broadcast_to(owner[...].astype(F32), (ROWS, ROWS))
+    column = across.T
     row = lax.broadcasted_iota(jnp.int32, (ROWS, ROWS), 0)
     lane = lax.broadcasted_iota(jnp.int32, (ROWS, ROWS), 1)
     earlier = jnp.where((column == across) & (row < lane), 1.0, 0.0)
@@ -288,31 +326,35 @@
     out[...] = jnp.where(lane[0:32] == 2 * CAP, square, placed)
 
 
-def slots(t, first, got, owner):
+def slots(t, p, got, owner):
     vmem = pl.BlockSpec(memory_space=pltpu.VMEM)
+    smem = pl.BlockSpec(memory_space=pltpu.SMEM)
     return pl.pallas_call(
         slots_kernel,
-        in_specs=[pl.BlockSpec(memory_space=pltpu.SMEM), vmem, vmem],
+        in_specs=[smem, smem, vmem, vmem],
         out_specs=vmem,
         out_shape=jax.ShapeDtypeStruct((32, ROWS), F32),
+        compiler_params=pltpu.CompilerParams(vmem_limit_bytes=4 * MB),
         name="slots",
-    )(jnp.stack([t, first]), got, owner)
+    )(t[None], p[None], got, owner)
 
 
 def finish_kernel(tokens, got, weight, token):
     square = jnp.sum(got[:, 2 * CAP : 2 * CAP + 1])
-    norm = lax.rsqrt(jnp.full((1, CAP), square / tokens + 1e-06, F32))
-    weight[...] = got[:, 0:CAP] * norm
-    token[...] = got[:, CAP : 2 * CAP].astype(jnp.int32) - 1
+    norm = lax.rsqrt(jnp.full((CAP, 32), square / tokens + 1e-06, F32))
+    turned = jnp.concatenate([got[...], jnp.zeros((ROWS - 32, ROWS), F32)], axis=0).T
+    weight[...] = turned[0:CAP, 0:32] * norm
+    token[...] = turned[CAP : 2 * CAP, 0:32].astype(jnp.int32) - 1
 
 
 def finish(got, tokens):
     return pl.pallas_call(
         functools.partial(finish_kernel, tokens),
         out_shape=[
-            jax.ShapeDtypeStruct((32, CAP), F32),
-            jax.ShapeDtypeStruct((32, CAP), jnp.int32),
+            jax.ShapeDtypeStruct((CAP, 32), F32),
+            jax.ShapeDtypeStruct((CAP, 32), jnp.int32),
         ],
+        compiler_params=pltpu.CompilerParams(vmem_limit_bytes=4 * MB),
         name="finish",
     )(got)
 
@@ -331,24 +373,38 @@
     ids = ids.at[0:1, :].set(wide[:, 0:KH])
     ids = ids.at[1:2, :].set(jnp.concatenate([wide[:, KH:TOK]] * 2, axis=1))
 
-    order = (4, 3, 5, 2, 6, 1, 7, 0)
-    messages = project(t, order, ph, pg, th, tg, fin, fout)
-    parts = [shift(messages[i], "tgt", n_tgt, k) for i, k in enumerate(order) if k]
-    tmsg, pmsg, scale = prepare(messages[-1], parts, ids, n_pool // 2)
+    shared = (ph, pg, th, tg, fin, fout.T)
+    after = lax.optimization_barrier
+    up, down, opposite = project(
+        LIMITS[0], t, (1, 7, 3, 5, 4), ((0, 0), (1, 0), (0, 1), (1, 1), (2, 0)), (BF16,) * 3, *shared
+    )
+    from_low = shift(up, "tgt", n_tgt, 1)
+    from_high = shift(down, "tgt", n_tgt, n_tgt - 1)
+    across = shift(opposite, "tgt", n_tgt, 4)
+    t_next, up = after((t, up))
+    two_up, two_down = project(LIMITS[1], t_next, (2, 6), ((0, 0), (1, 0)), (F32, F32), *shared)
+    two_up, two_down = merge(from_low, from_high, two_up, two_down)
+    t_next, two_up = after((t, two_up))
+    from_low2 = shift(two_up, "tgt", n_tgt, 2)
+    from_high2 = shift(two_down, "tgt", n_tgt, n_tgt - 2)
+    (own,) = project(LIMITS[2], t_next, (0,), ((0, 0),), (F32,), *shared)
+    parts = [from_low, from_high, across, from_low2, from_high2]
+    tmsg, pmsg, scale = prepare(own, parts, ids, n_pool // 2)
 
     same_core = [[2 * i + c for i in range(n_pool // 2)] for c in range(2)]
     near = lax.all_to_all(
         tmsg, "pool", split_axis=0, concat_axis=0, tiled=True, axis_index_groups=same_core
     )
     pools = [pmsg] + [shift(pmsg, "tgt", n_tgt, k) for k in range(1, n_tgt)]
+    near, *pools = after((near, *pools))
     far = lax.ppermute(near, "pool", [(i, i ^ 1) for i in range(n_pool)])
     partial = score(t, pools, near)
     best = score(t, pools, far, partial, scale)
     got = lax.all_to_all(best, "tgt", split_axis=0, concat_axis=0, tiled=True)
-    sent = slots(t, (p * n_tgt + t) * ROWS, got, owner)
+    sent = slots(t, p, got, owner.T)
     arrived = lax.all_to_all(sent, "pool", split_axis=0, concat_axis=0, tiled=True)
     weight, token = finish(arrived, float(n_pool * n_tgt * ROWS))
-    return (weight[None, None], token[None, None])
+    return (weight.T[None, None], token.T[None, None])
 
 
 def solution(mesh):

time: 143 us -> 105 us (0.73)
  blocking collectives: 37.8 us -> 15.5 us
  local copies, waits for them, and re-layouts: 13.4 us -> 0.9 us
  waiting for transfers between devices: 24.4 us -> 14.4 us
  starting transfers between devices: 35.8 us -> 44.6 us
    all_to_all x1 -> x0, blocking collectives: 24.5 us -> none  [shards(): lax.all_to_all(tmsg, 'pool', split_axis=0, concat_axis=0, tiled=True, axi...]
    unnamed x20 -> x10, local copies, waits for them, and re-layouts: 13.3 us -> 0.86 us
    ppermute x14 -> x12, waiting for transfers between devices: 18.6 us -> 6.22 us  [shift(): return lax.ppermute(x, axis, [(i, (i + k) % n) for i in range(n)])]
    all_to_all x0 -> x1, starting transfers between devices: none -> 6.74 us  [shards(): lax.all_to_all(tmsg, 'pool', split_axis=0, concat_axis=0, tiled=True, axi...]
    pallas_call x2, Pallas kernels: 18.8 us -> 13.9 us  [score(): pl.pallas_call(functools.partial(score_kernel, last), in_specs=[pl.BlockS...]
    pallas_call x2 -> x5, Pallas kernels: 7.24 us -> 11.8 us  [the longest x3 11.5 us: project(): pl.pallas_call(functools.partial(project_kernel, steps, kinds), in_specs=...]
    ppermute x1, starting transfers between devices: 2.05 us -> 5.47 us  [shards(): far = lax.ppermute(near, 'pool', [(i, i ^ 1) for i in range(n_pool)])]
    all_to_all x1, blocking collectives: 13.2 us -> 15.5 us  [shards(): lax.all_to_all(sent, 'pool', split_axis=0, concat_axis=0, tiled=True)]
  transfers between devices with their start and end apart: 16 -> 15, of which waited for: 8 -> 7; matrix products, arithmetic and copies ran while one was open for 1% -> 0% of each run, Pallas kernels for 6% -> 12%
where the time goes in v2:
time: 105 us
  starting transfers between devices  44.6 us (42%)
  Pallas kernels  28.4 us (27%)
  blocking collectives  15.5 us (15%)
  waiting for transfers between devices  14.4 us (14%)
    ppermute x12, starting transfers between devices, shift(): return lax.ppermute(x, axis, [(i, (i + k) % n) for i in range(n)])  27.2 us
    all_to_all x1, blocking collectives, shards(): lax.all_to_all(sent, 'pool', split_axis=0, concat_axis=0, tiled=True)  15.5 us
    pallas_call x2, Pallas kernels, score(): pl.pallas_call(functools.partial(score_kernel, last), in_specs=[pl.BlockS...  13.9 us
    pallas_call x3, Pallas kernels, project(): pl.pallas_call(functools.partial(project_kernel, steps, kinds), in_specs=...  11.5 us
    all_to_all x1, waiting for transfers between devices, shards(): got = lax.all_to_all(best, 'tgt', split_axis=0, concat_axis=0, tiled=True)  7.14 us
    all_to_all x1, starting transfers between devices, shards(): lax.all_to_all(tmsg, 'pool', split_axis=0, concat_axis=0, tiled=True, axi...  6.74 us
    ppermute x12, waiting for transfers between devices, shift(): return lax.ppermute(x, axis, [(i, (i + k) % n) for i in range(n)])  6.22 us
    ppermute x1, starting transfers between devices, shards(): far = lax.ppermute(near, 'pool', [(i, i ^ 1) for i in range(n_pool)])  5.47 us
  transfers between devices with their start and end apart: 15, of which 7 were waited for; matrix products, arithmetic and copies ran while one was open for 0% of the time, Pallas kernels for 12%

profile of v2, /device:TPU:1, one launch (start us, length us, event | category | flops | bytes accessed | tf_op | source)
XLA Modules:
  0.0 104.7 jit_solution(6869599801253889854)
XLA Ops:
  0.6 0.8 copy-done.1
  1.5 6.1 %project.3 = (bf16[960,128]{1,0:T(8,128)(2,1)S(1)}, bf16[960,128]{1,0:T(8,128)(2,1)S(1)}, bf16[480,128]{1,0:T(8,128)(2,1)S(1)}) custom-call(s32[1]{0:T(128)} %bitcast.t_ref, bf16[1024,1792]{1,0:T(8,128)(2,1)} %ph.5, bf16[1024,512]{1,0:T(8,128)(2,1)} %pg.5, bf16[1536,1792]{1,0:T(8,128)(2,1)} %th.5, bf16[1536,512]{1,0:T(8,128)(2,1)} %tg.5, ...), custom_call_target="tpu_custom_call" | custom-call | flops 850000000 | bytes 8000000 | tf_op jit(solution)/shard_map/project/pallas_call | solution.py:97
  7.6 2.5 %collective-permute-start = (bf16[960,128]{1,0:T(8,128)(2,1)S(1)}, bf16[960,128]{1,0:T(8,128)(2,1)S(1)}, u32[]{:S(2)}, u32[]{:S(2)}) collective-permute-start(bf16[960,128]{1,0:T(8,128)(2,1)S(1)} %get-tuple-element.50), channel_id=1, source_target_pairs={{0,1},{1,2},{2,3},{3,4},{4,5},{5,6},{6,7},{7,0},{8,9},{9,10},{10,1... | collective-permute-start | bytes 737288 | tf_op jit(solution)/shard_map/ppermute | solution.py:363
  10.1 4.0 %collective-permute-start.1 = (bf16[960,128]{1,0:T(8,128)(2,1)S(1)}, bf16[960,128]{1,0:T(8,128)(2,1)S(1)}, u32[]{:S(2)}, u32[]{:S(2)}) collective-permute-start(bf16[960,128]{1,0:T(8,128)(2,1)S(1)} %get-tuple-element.51), channel_id=1, source_target_pairs={{0,7},{1,0},{2,1},{3,2},{4,3},{5,4},{6,5},{7,6},{8,15},{9,8},{10,9... | collective-permute-start | bytes 737288 | tf_op jit(solution)/shard_map/ppermute | solution.py:363
  14.1 3.9 %collective-permute-start.2 = (bf16[480,128]{1,0:T(8,128)(2,1)S(1)}, bf16[480,128]{1,0:T(8,128)(2,1)S(1)}, u32[]{:S(2)}, u32[]{:S(2)}) collective-permute-start(bf16[480,128]{1,0:T(8,128)(2,1)S(1)} %get-tuple-element.57), channel_id=1, source_target_pairs={{0,4},{1,5},{2,6},{3,7},{4,0},{5,1},{6,2},{7,3},{8,12},{9,13},{10,... | collective-permute-start | bytes 368648 | tf_op jit(solution)/shard_map/ppermute | solution.py:363
  18.1 3.1 %project.4 = (f32[480,128]{1,0:T(8,128)S(1)}, f32[480,128]{1,0:T(8,128)S(1)}) custom-call(s32[1]{0:T(128)} %bitcast.3.t_ref, bf16[1024,1792]{1,0:T(8,128)(2,1)} %ph.5, bf16[1024,512]{1,0:T(8,128)(2,1)} %pg.5, bf16[1536,1792]{1,0:T(8,128)(2,1)} %th.5, bf16[1536,512]{1,0:T(8,128)(2,1)} %tg.5, bf16[1792,128]{1,0:T(8,128)(2,1)} %fin.5, bf16[64,512]{1,0:T(8,128)(2,1)S(1)} %bitcast.17), custom_call_target="tpu_custom_call" | custom-call | flops 340000000 | bytes 3200000 | tf_op jit(solution)/shard_map/project/pallas_call | solution.py:97
  22.2 3.6 %collective-permute-start.4 = (bf16[480,128]{1,0:T(8,128)(2,1)S(1)}, bf16[480,128]{1,0:T(8,128)(2,1)S(1)}, u32[]{:S(2)}, u32[]{:S(2)}) collective-permute-start(bf16[480,128]{1,0:T(8,128)(2,1)S(1)} %get-tuple-element.59), channel_id=1, source_target_pairs={{0,6},{1,7},{2,0},{3,1},{4,2},{5,3},{6,4},{7,5},{8,14},{9,15},{10,... | collective-permute-start | bytes 368648 | tf_op jit(solution)/shard_map/ppermute | solution.py:363
  25.8 2.4 %project.5.own = f32[480,128]{1,0:T(8,128)S(1)} custom-call(s32[1]{0:T(128)} %bitcast.4.t_ref, bf16[1024,1792]{1,0:T(8,128)(2,1)} %ph.5, bf16[1024,512]{1,0:T(8,128)(2,1)} %pg.5, bf16[1536,1792]{1,0:T(8,128)(2,1)} %th.5, bf16[1536,512]{1,0:T(8,128)(2,1)} %tg.5, bf16[1792,128]{1,0:T(8,128)(2,1)S(1)} %copy-done, bf16[64,512]{1,0:T(8,128)(2,1)S(1)} %bitcast.18), custom_call_target="tpu_custom_call" | custom-call | flops 170000000 | bytes 1600000 | tf_op jit(solution)/shard_map/project/pallas_call | solution.py:97
  28.7 3.0 %collective-permute-done.4.rest_4_ = bf16[480,128]{1,0:T(8,128)(2,1)S(1)} collective-permute-done((bf16[480,128]{1,0:T(8,128)(2,1)S(1)}, bf16[480,128]{1,0:T(8,128)(2,1)S(1)}, u32[]{:S(2)}, u32[]{:S(2)}) %collective-permute-start.4) | collective-permute-done | bytes 122912 | tf_op jit(solution)/shard_map/ppermute | solution.py:363
  31.7 1.8 %prepare.1 = (bf16[16,304,128]{2,1,0:T(8,128)(2,1)}, bf16[192,128]{1,0:T(8,128)(2,1)S(1)}, f32[8,128]{1,0:T(8,128)S(1)}) custom-call(f32[480,128]{1,0:T(8,128)S(1)} %project.5.own, bf16[960,128]{1,0:T(8,128)(2,1)S(1)} %collective-permute-done.from_low.rest_0_, bf16[960,128]{1,0:T(8,128)(2,1)S(1)} %collective-permute-done.1.from_high.rest_1_, ...), custom_call_target="tpu_custom_call" | custom-call | flops 200000000 | bytes 3000000 | tf_op jit(solution)/shard_map/prepare/pallas_call | solution.py:185
  33.6 6.7 %all-to-all-start = ((bf16[16,304,128]{2,1,0:T(8,128)(2,1)}), bf16[16,304,128]{2,1,0:T(8,128)(2,1)S(1)}, u32[]{:S(2)}, u32[]{:S(2)}) async-start(bf16[16,304,128]{2,1,0:T(8,128)(2,1)} %get-tuple-element.60), calls=%async_computation | async-start | bytes 2490368 | tf_op jit(solution)/shard_map/all_to_all | solution.py:395
  40.3 1.4 %collective-permute-start.5 = (bf16[192,128]{1,0:T(8,128)(2,1)S(1)}, bf16[192,128]{1,0:T(8,128)(2,1)S(1)}, u32[]{:S(2)}, u32[]{:S(2)}) collective-permute-start(bf16[192,128]{1,0:T(8,128)(2,1)S(1)} %get-tuple-element.62.refs_0_), channel_id=1, source_target_pairs={{0,1},{1,2},{2,3},{3,4},{4,5},{5,6},{6,7},{7,0},{8,9},{9,10},{10,1... | collective-permute-start | bytes 147464 | tf_op jit(solution)/shard_map/ppermute | solution.py:363
  41.7 2.2 %collective-permute-start.6 = (bf16[192,128]{1,0:T(8,128)(2,1)S(1)}, bf16[192,128]{1,0:T(8,128)(2,1)S(1)}, u32[]{:S(2)}, u32[]{:S(2)}) collective-permute-start(bf16[192,128]{1,0:T(8,128)(2,1)S(1)} %get-tuple-element.62.refs_0_), channel_id=1, source_target_pairs={{0,2},{1,3},{2,4},{3,5},{4,6},{5,7},{6,0},{7,1},{8,10},{9,11},{10,... | collective-permute-start | bytes 147464 | tf_op jit(solution)/shard_map/ppermute | solution.py:363
  44.1 5.4 %collective-permute-start.8 = (bf16[192,128]{1,0:T(8,128)(2,1)S(1)}, bf16[192,128]{1,0:T(8,128)(2,1)S(1)}, u32[]{:S(2)}, u32[]{:S(2)}) collective-permute-start(bf16[192,128]{1,0:T(8,128)(2,1)S(1)} %get-tuple-element.62.refs_0_), channel_id=1, source_target_pairs={{0,4},{1,5},{2,6},{3,7},{4,0},{5,1},{6,2},{7,3},{8,12},{9,13},{10,... | collective-permute-start | bytes 147464 | tf_op jit(solution)/shard_map/ppermute | solution.py:363
  49.5 2.5 %collective-permute-start.10 = (bf16[192,128]{1,0:T(8,128)(2,1)S(1)}, bf16[192,128]{1,0:T(8,128)(2,1)S(1)}, u32[]{:S(2)}, u32[]{:S(2)}) collective-permute-start(bf16[192,128]{1,0:T(8,128)(2,1)S(1)} %get-tuple-element.62.refs_0_), channel_id=1, source_target_pairs={{0,6},{1,7},{2,0},{3,1},{4,2},{5,3},{6,4},{7,5},{8,14},{9,15},{10,... | collective-permute-start | bytes 147464 | tf_op jit(solution)/shard_map/ppermute | solution.py:363
  52.0 1.4 %collective-permute-start.11 = (bf16[192,128]{1,0:T(8,128)(2,1)S(1)}, bf16[192,128]{1,0:T(8,128)(2,1)S(1)}, u32[]{:S(2)}, u32[]{:S(2)}) collective-permute-start(bf16[192,128]{1,0:T(8,128)(2,1)S(1)} %get-tuple-element.62.refs_0_), channel_id=1, source_target_pairs={{0,7},{1,0},{2,1},{3,2},{4,3},{5,4},{6,5},{7,6},{8,15},{9,8},{10,9... | collective-permute-start | bytes 147464 | tf_op jit(solution)/shard_map/ppermute | solution.py:363
  53.4 1.1 %collective-permute-done.9.refs_5_ = bf16[192,128]{1,0:T(8,128)(2,1)S(1)} collective-permute-done((bf16[192,128]{1,0:T(8,128)(2,1)S(1)}, bf16[192,128]{1,0:T(8,128)(2,1)S(1)}, u32[]{:S(2)}, u32[]{:S(2)}) %collective-permute-start.9) | collective-permute-done | bytes 49184 | tf_op jit(solution)/shard_map/ppermute | solution.py:363
  55.3 1.1 %all-to-all-done.refs_8_ = bf16[16,304,128]{2,1,0:T(8,128)(2,1)S(1)} async-done(((bf16[16,304,128]{2,1,0:T(8,128)(2,1)}), bf16[16,304,128]{2,1,0:T(8,128)(2,1)S(1)}, u32[]{:S(2)}, u32[]{:S(2)}) %all-to-all-start) | async-done | bytes 1245216 | tf_op jit(solution)/shard_map/all_to_all | solution.py:395
  56.4 5.5 %collective-permute-start.12 = (bf16[16,304,128]{2,1,0:T(8,128)(2,1)S(1)}, bf16[16,304,128]{2,1,0:T(8,128)(2,1)S(1)}, u32[]{:S(2)}, u32[]{:S(2)}) collective-permute-start(bf16[16,304,128]{2,1,0:T(8,128)(2,1)S(1)} %all-to-all-done.refs_8_), channel_id=1, source_target_pairs={{0,8},{8,0},{16,24},{24,16},{32,40},{40,32},{48,56},{56,48},{64,72... | collective-permute-start | bytes 3735560 | tf_op jit(solution)/shard_map/ppermute | solution.py:400
  61.8 6.6 %score_first.1.refs_9_ = f32[8,128]{1,0:T(8,128)S(1)} custom-call(s32[1]{0:T(128)} %bitcast.t_ref, bf16[192,128]{1,0:T(8,128)(2,1)S(1)} %get-tuple-element.62.refs_0_, bf16[192,128]{1,0:T(8,128)(2,1)S(1)} %collective-permute-done.5.refs_1_, bf16[192,128]{1,0:T(8,128)(2,1)S(1)} %collective-permute-done.6.refs_2_, ...), custom_call_target="tpu_custom_call" | custom-call | flops 5000000000 | bytes 2000000 | tf_op jit(solution)/shard_map/score_first/pallas_call | solution.py:279
  68.5 7.3 %score_last.1 = f32[8,16,128]{2,1,0:T(8,128)} custom-call(s32[1]{0:T(128)} %bitcast.t_ref, bf16[192,128]{1,0:T(8,128)(2,1)S(1)} %get-tuple-element.62.refs_0_, bf16[192,128]{1,0:T(8,128)(2,1)S(1)} %collective-permute-done.5.refs_1_, bf16[192,128]{1,0:T(8,128)(2,1)S(1)} %collective-permute-done.6.refs_2_, ...), custom_call_target="tpu_custom_call" | custom-call | flops 5000000000 | bytes 2000000 | tf_op jit(solution)/shard_map/score_last/pallas_call | solution.py:279
  75.8 5.3 %all-to-all-start.1 = ((f32[8,16,128]{2,1,0:T(8,128)}), f32[8,16,128]{2,1,0:T(8,128)S(1)}, u32[]{:S(2)}, u32[]{:S(2)}) async-start(f32[8,16,128]{2,1,0:T(8,128)} %score_last.1), calls=%async_computation.1 | async-start | bytes 131072 | tf_op jit(solution)/shard_map/all_to_all | solution.py:403
  81.1 7.1 %all-to-all-done.1.got = f32[8,16,128]{2,1,0:T(8,128)S(1)} async-done(((f32[8,16,128]{2,1,0:T(8,128)}), f32[8,16,128]{2,1,0:T(8,128)S(1)}, u32[]{:S(2)}, u32[]{:S(2)}) %all-to-all-start.1) | async-done | bytes 65568 | tf_op jit(solution)/shard_map/all_to_all | solution.py:403
  88.5 15.5 %all_to_all.21 = f32[32,1,128]{2,1,0:T(1,128)S(1)} all-to-all(f32[32,1,128]{2,1,0:T(1,128)S(1)} %bitcast.20), channel_id=1, replica_groups=mesh['pool'=32,'tgt'=8] {'pool'}, dimensions={0} | all-to-all | bytes 32768 | tf_op jit(solution)/shard_map/all_to_all | solution.py:405
  (32 shorter events, 3.7 us)
Async XLA Ops:
  0.6 0.8 copy-start.1
  1.5 16.6 %copy-start.4 = (s32[1,192]{1,0:T(1,128)S(1)}, s32[1,192]{1,0:T(1,128)}, u32[]{:S(2)}) copy-start(s32[1,192]{1,0:T(1,128)} %param.18) | copy-start | bytes 2308
  7.6 13.7 %collective-permute-start = (bf16[960,128]{1,0:T(8,128)(2,1)S(1)}, bf16[960,128]{1,0:T(8,128)(2,1)S(1)}, u32[]{:S(2)}, u32[]{:S(2)}) collective-permute-start(bf16[960,128]{1,0:T(8,128)(2,1)S(1)} %get-tuple-element.50), channel_id=1, source_target_pairs={{0,1},{1,2},{2,3},{3,4},{4,5},{5,6},{6,7},{7,0},{8,9},{9,10},{10,1... | collective-permute-start | bytes 737288 | tf_op jit(solution)/shard_map/ppermute | solution.py:363
  10.1 11.9 %collective-permute-start.1 = (bf16[960,128]{1,0:T(8,128)(2,1)S(1)}, bf16[960,128]{1,0:T(8,128)(2,1)S(1)}, u32[]{:S(2)}, u32[]{:S(2)}) collective-permute-start(bf16[960,128]{1,0:T(8,128)(2,1)S(1)} %get-tuple-element.51), channel_id=1, source_target_pairs={{0,7},{1,0},{2,1},{3,2},{4,3},{5,4},{6,5},{7,6},{8,15},{9,8},{10,9... | collective-permute-start | bytes 737288 | tf_op jit(solution)/shard_map/ppermute | solution.py:363
  14.1 14.1 %collective-permute-start.2 = (bf16[480,128]{1,0:T(8,128)(2,1)S(1)}, bf16[480,128]{1,0:T(8,128)(2,1)S(1)}, u32[]{:S(2)}, u32[]{:S(2)}) collective-permute-start(bf16[480,128]{1,0:T(8,128)(2,1)S(1)} %get-tuple-element.57), channel_id=1, source_target_pairs={{0,4},{1,5},{2,6},{3,7},{4,0},{5,1},{6,2},{7,3},{8,12},{9,13},{10,... | collective-permute-start | bytes 368648 | tf_op jit(solution)/shard_map/ppermute | solution.py:363
  18.1 7.7 %copy-start = (bf16[1792,128]{1,0:T(8,128)(2,1)S(1)}, bf16[1792,128]{1,0:T(8,128)(2,1)}, u32[]{:S(2)}) copy-start(bf16[1792,128]{1,0:T(8,128)(2,1)} %fin.5) | copy-start | bytes 1376260
  18.1 7.7 %copy-start.2 = (bf16[512,64]{0,1:T(8,128)(2,1)S(1)}, bf16[512,64]{0,1:T(8,128)(2,1)}, u32[]{:S(2)}) copy-start(bf16[512,64]{0,1:T(8,128)(2,1)} %param.17) | copy-start | bytes 196612
  22.1 6.7 %collective-permute-start.3 = (bf16[480,128]{1,0:T(8,128)(2,1)S(1)}, bf16[480,128]{1,0:T(8,128)(2,1)S(1)}, u32[]{:S(2)}, u32[]{:S(2)}) collective-permute-start(bf16[480,128]{1,0:T(8,128)(2,1)S(1)} %get-tuple-element.58), channel_id=1, source_target_pairs={{0,2},{1,3},{2,4},{3,5},{4,6},{5,7},{6,0},{7,1},{8,10},{9,11},{10,... | collective-permute-start | bytes 368648 | tf_op jit(solution)/shard_map/ppermute | solution.py:363
  22.2 9.6 %collective-permute-start.4 = (bf16[480,128]{1,0:T(8,128)(2,1)S(1)}, bf16[480,128]{1,0:T(8,128)(2,1)S(1)}, u32[]{:S(2)}, u32[]{:S(2)}) collective-permute-start(bf16[480,128]{1,0:T(8,128)(2,1)S(1)} %get-tuple-element.59), channel_id=1, source_target_pairs={{0,6},{1,7},{2,0},{3,1},{4,2},{5,3},{6,4},{7,5},{8,14},{9,15},{10,... | collective-permute-start | bytes 368648 | tf_op jit(solution)/shard_map/ppermute | solution.py:363
  33.6 22.8 %all-to-all-start = ((bf16[16,304,128]{2,1,0:T(8,128)(2,1)}), bf16[16,304,128]{2,1,0:T(8,128)(2,1)S(1)}, u32[]{:S(2)}, u32[]{:S(2)}) async-start(bf16[16,304,128]{2,1,0:T(8,128)(2,1)} %get-tuple-element.60), calls=%async_computation | async-start | bytes 2490368 | tf_op jit(solution)/shard_map/all_to_all | solution.py:395
  40.3 9.2 %collective-permute-start.5 = (bf16[192,128]{1,0:T(8,128)(2,1)S(1)}, bf16[192,128]{1,0:T(8,128)(2,1)S(1)}, u32[]{:S(2)}, u32[]{:S(2)}) collective-permute-start(bf16[192,128]{1,0:T(8,128)(2,1)S(1)} %get-tuple-element.62.refs_0_), channel_id=1, source_target_pairs={{0,1},{1,2},{2,3},{3,4},{4,5},{5,6},{6,7},{7,0},{8,9},{9,10},{10,1... | collective-permute-start | bytes 147464 | tf_op jit(solution)/shard_map/ppermute | solution.py:363
  41.7 10.3 %collective-permute-start.6 = (bf16[192,128]{1,0:T(8,128)(2,1)S(1)}, bf16[192,128]{1,0:T(8,128)(2,1)S(1)}, u32[]{:S(2)}, u32[]{:S(2)}) collective-permute-start(bf16[192,128]{1,0:T(8,128)(2,1)S(1)} %get-tuple-element.62.refs_0_), channel_id=1, source_target_pairs={{0,2},{1,3},{2,4},{3,5},{4,6},{5,7},{6,0},{7,1},{8,10},{9,11},{10,... | collective-permute-start | bytes 147464 | tf_op jit(solution)/shard_map/ppermute | solution.py:363
  43.9 9.5 %collective-permute-start.7 = (bf16[192,128]{1,0:T(8,128)(2,1)S(1)}, bf16[192,128]{1,0:T(8,128)(2,1)S(1)}, u32[]{:S(2)}, u32[]{:S(2)}) collective-permute-start(bf16[192,128]{1,0:T(8,128)(2,1)S(1)} %get-tuple-element.62.refs_0_), channel_id=1, source_target_pairs={{0,3},{1,4},{2,5},{3,6},{4,7},{5,0},{6,1},{7,2},{8,11},{9,12},{10,... | collective-permute-start | bytes 147464 | tf_op jit(solution)/shard_map/ppermute | solution.py:363
  44.1 9.2 %collective-permute-start.8 = (bf16[192,128]{1,0:T(8,128)(2,1)S(1)}, bf16[192,128]{1,0:T(8,128)(2,1)S(1)}, u32[]{:S(2)}, u32[]{:S(2)}) collective-permute-start(bf16[192,128]{1,0:T(8,128)(2,1)S(1)} %get-tuple-element.62.refs_0_), channel_id=1, source_target_pairs={{0,4},{1,5},{2,6},{3,7},{4,0},{5,1},{6,2},{7,3},{8,12},{9,13},{10,... | collective-permute-start | bytes 147464 | tf_op jit(solution)/shard_map/ppermute | solution.py:363
  49.5 5.0 %collective-permute-start.9 = (bf16[192,128]{1,0:T(8,128)(2,1)S(1)}, bf16[192,128]{1,0:T(8,128)(2,1)S(1)}, u32[]{:S(2)}, u32[]{:S(2)}) collective-permute-start(bf16[192,128]{1,0:T(8,128)(2,1)S(1)} %get-tuple-element.62.refs_0_), channel_id=1, source_target_pairs={{0,5},{1,6},{2,7},{3,0},{4,1},{5,2},{6,3},{7,4},{8,13},{9,14},{10,... | collective-permute-start | bytes 147464 | tf_op jit(solution)/shard_map/ppermute | solution.py:363
  49.5 5.8 %collective-permute-start.10 = (bf16[192,128]{1,0:T(8,128)(2,1)S(1)}, bf16[192,128]{1,0:T(8,128)(2,1)S(1)}, u32[]{:S(2)}, u32[]{:S(2)}) collective-permute-start(bf16[192,128]{1,0:T(8,128)(2,1)S(1)} %get-tuple-element.62.refs_0_), channel_id=1, source_target_pairs={{0,6},{1,7},{2,0},{3,1},{4,2},{5,3},{6,4},{7,5},{8,14},{9,15},{10,... | collective-permute-start | bytes 147464 | tf_op jit(solution)/shard_map/ppermute | solution.py:363
  52.0 3.3 %collective-permute-start.11 = (bf16[192,128]{1,0:T(8,128)(2,1)S(1)}, bf16[192,128]{1,0:T(8,128)(2,1)S(1)}, u32[]{:S(2)}, u32[]{:S(2)}) collective-permute-start(bf16[192,128]{1,0:T(8,128)(2,1)S(1)} %get-tuple-element.62.refs_0_), channel_id=1, source_target_pairs={{0,7},{1,0},{2,1},{3,2},{4,3},{5,4},{6,5},{7,6},{8,15},{9,8},{10,9... | collective-permute-start | bytes 147464 | tf_op jit(solution)/shard_map/ppermute | solution.py:363
  56.4 12.1 %collective-permute-start.12 = (bf16[16,304,128]{2,1,0:T(8,128)(2,1)S(1)}, bf16[16,304,128]{2,1,0:T(8,128)(2,1)S(1)}, u32[]{:S(2)}, u32[]{:S(2)}) collective-permute-start(bf16[16,304,128]{2,1,0:T(8,128)(2,1)S(1)} %all-to-all-done.refs_8_), channel_id=1, source_target_pairs={{0,8},{8,0},{16,24},{24,16},{32,40},{40,32},{48,56},{56,48},{64,72... | collective-permute-start | bytes 3735560 | tf_op jit(solution)/shard_map/ppermute | solution.py:400
  68.5 19.7 %copy-start.3 = (s32[128,1]{0,1:T(1,128)S(1)}, s32[128,1]{0,1:T(1,128)}, u32[]{:S(2)}) copy-start(s32[128,1]{0,1:T(1,128)} %param.19) | copy-start | bytes 1540
  75.8 12.4 %all-to-all-start.1 = ((f32[8,16,128]{2,1,0:T(8,128)}), f32[8,16,128]{2,1,0:T(8,128)S(1)}, u32[]{:S(2)}, u32[]{:S(2)}) async-start(f32[8,16,128]{2,1,0:T(8,128)} %score_last.1), calls=%async_computation.1 | async-start | bytes 131072 | tf_op jit(solution)/shard_map/all_to_all | solution.py:403

commit v3 on v2

--- a/solution.py
+++ b/solution.py
@@ -21,7 +21,7 @@
 TMSG = TOK + TOK // 2 + 16
 PMSG = ROWS + ROWS // 2
 MB = 1024 * 1024
-LIMITS = (53, 53, 53)
+LIMITS = (60, 53, 53)
 
 
 def dot_nt(a, b, precision=None):
@@ -73,32 +73,33 @@
         sums_out = dot_nt(rows_out[rows, :], fout_v[...])
         sums_in = jnp.dot(rows_in[rows, :], fin_v[...], preferred_element_type=F32)
         for i in range(first, first + count):
-            which, slot = kinds[i]
-            out = outs[which]
             lead = (i - first) * both
-            at = slot * MSG
-            out[at : at + both, :] = sums_in[lead : lead + both].astype(out.dtype)
-            at = at + both
+            message = [sums_in[lead : lead + both]]
             for size in (ROWS, TOK):
                 half = size // 2
-                packed = jnp.concatenate(
-                    [sums_out[lead : lead + half], sums_out[lead + half : lead + size]], axis=1
+                message.append(
+                    jnp.concatenate(
+                        [sums_out[lead : lead + half], sums_out[lead + half : lead + size]], axis=1
+                    )
                 )
-                out[at : at + half, :] = packed.astype(out.dtype)
                 lead = lead + size
-                at = at + half
+            message = jnp.concatenate(message, axis=0)
+            for which, at, start, stop in kinds[i]:
+                out = outs[which]
+                out[at : at + stop - start, :] = message[start:stop].astype(out.dtype)
 
 
 def project(limit, t, steps, kinds, dtypes, ph, pg, th, tg, fin, fout):
     n = len(steps)
-    sizes = [sum(1 for which, _ in kinds if which == j) for j in range(len(dtypes))]
+    pieces = [piece for kind in kinds for piece in kind]
+    sizes = [sum(p[3] - p[2] for p in pieces if p[0] == j) for j in range(len(dtypes))]
     hbm = pl.BlockSpec(memory_space=pltpu.HBM)
     vmem = pl.BlockSpec(memory_space=pltpu.VMEM)
     return pl.pallas_call(
         functools.partial(project_kernel, steps, kinds),
         in_specs=[pl.BlockSpec(memory_space=pltpu.SMEM)] + [hbm] * 6,
         out_specs=[vmem for _ in dtypes],
-        out_shape=[jax.ShapeDtypeStruct((c * MSG, KH), d) for c, d in zip(sizes, dtypes)],
+        out_shape=[jax.ShapeDtypeStruct((c, KH), d) for c, d in zip(sizes, dtypes)],
         scratch_shapes=[
             pltpu.VMEM((n * (ROWS + TOK), ph.shape[1]), BF16),
             pltpu.VMEM((n * (ROWS + TOK), pg.shape[1]), BF16),
@@ -114,9 +115,14 @@
     )(t[None], ph, pg, th, tg, fin, fout)
 
 
-def merge_kernel(from_low, from_high, mine_up, mine_down, up, down):
-    up[...] = (mine_up[...] + from_low[MSG : 2 * MSG, :].astype(F32)).astype(BF16)
-    down[...] = (mine_down[...] + from_high[MSG : 2 * MSG, :].astype(F32)).astype(BF16)
+def merge_kernel(from_low, from_high, half_low, half_high, mine_up, mine_down, up, down):
+    half = MSG // 2
+    total = mine_up[...] + from_low[MSG : 2 * MSG, :].astype(F32)
+    up[0:half, :] = (total[0:half] + half_low[...].astype(F32)).astype(BF16)
+    up[half:MSG, :] = total[half:MSG].astype(BF16)
+    total = mine_down[...] + from_high[MSG : 2 * MSG, :].astype(F32)
+    down[0:half, :] = total[0:half].astype(BF16)
+    down[half:MSG, :] = (total[half:MSG] + half_high[...].astype(F32)).astype(BF16)
 
 
 def merge(*operands):
@@ -130,7 +136,7 @@
 
 
 def prepare_kernel(own, *rest):
-    parts, (ids_ref, tmsg, pmsg, scale_ref) = rest[:-4], rest[-4:]
+    parts, (ids_ref, tmsg, pmsg, scale_ref, message, sems) = rest[:-6], rest[-6:]
     total = own[...]
     for part in parts:
         total = total + part[0:MSG, :].astype(F32)
@@ -138,17 +144,6 @@
     tgt_in = total[ROWS : ROWS + TOK]
     pool_out = total[ROWS + TOK : ROWS + TOK + ROWS // 2]
     tgt_out = total[ROWS + TOK + ROWS // 2 : MSG]
-
-    pmsg[0:ROWS, :] = pool_in.astype(BF16)
-    pmsg[ROWS:PMSG, :] = pool_out.astype(BF16)
-    low = lane_mask(pool_out.shape, True)
-    zero = jnp.zeros_like(pool_out)
-    out_rows = jnp.concatenate(
-        [jnp.where(low, pool_out, zero), jnp.where(low, zero, pool_out)], axis=0
-    )
-    in_sq = jnp.sum((pool_in * pool_in).T, axis=0, keepdims=True)
-    out_sq = jnp.sum((out_rows * out_rows).T, axis=0, keepdims=True)
-    scale_ref[...] = jnp.broadcast_to(lax.rsqrt(in_sq * out_sq + 1e-06), scale_ref.shape)
 
     ids = ids_ref[...].astype(F32)
     first = ids[0:1, :]
@@ -172,44 +167,61 @@
     gram = dot_nt(wide_in, wide_in, HIGHEST) * dot_nt(wide_out, wide_out, HIGHEST)
     spread = jnp.sum(jnp.where(same, gram, 0.0), axis=0, keepdims=True)
     token_sq = jnp.sum(jnp.where(same, spread, 0.0), axis=1, keepdims=True)
-    scaled = (tgt_in * lax.rsqrt(token_sq[0:TOK] + 1e-06)).astype(BF16)
-    low_out = tgt_out.astype(BF16)
-    ids_low = ids_ref[...]
-    for i in range(tmsg.shape[0]):
-        tmsg[i, 0:TOK, :] = scaled
-        tmsg[i, TOK : TOK + TOK // 2, :] = low_out
-        tmsg[i, TOK + TOK // 2 : TMSG, :] = ids_low
+    message[0:TOK, :] = (tgt_in * lax.rsqrt(token_sq[0:TOK] + 1e-06)).astype(BF16)
+    message[TOK : TOK + TOK // 2, :] = tgt_out.astype(BF16)
+    message[TOK + TOK // 2 : TMSG, :] = ids_ref[...]
+    copies = [
+        pltpu.make_async_copy(message, tmsg.at[i], sems.at[i]) for i in range(tmsg.shape[0])
+    ]
+    for copy in copies:
+        copy.start()
+
+    pmsg[0:ROWS, :] = pool_in.astype(BF16)
+    pmsg[ROWS:PMSG, :] = pool_out.astype(BF16)
+    low = lane_mask(pool_out.shape, True)
+    zero = jnp.zeros_like(pool_out)
+    out_rows = jnp.concatenate(
+        [jnp.where(low, pool_out, zero), jnp.where(low, zero, pool_out)], axis=0
+    )
+    in_sq = jnp.sum((pool_in * pool_in).T, axis=0, keepdims=True)
+    out_sq = jnp.sum((out_rows * out_rows).T, axis=0, keepdims=True)
+    scale_ref[...] = jnp.broadcast_to(lax.rsqrt(in_sq * out_sq + 1e-06), scale_ref.shape)
+    for copy in copies:
+        copy.wait()
 
 
 def prepare(own, parts, ids, copies):
+    vmem = pl.BlockSpec(memory_space=pltpu.VMEM)
     return pl.pallas_call(
         prepare_kernel,
+        out_specs=[pl.BlockSpec(memory_space=pl.ANY), vmem, vmem],
         out_shape=[
             jax.ShapeDtypeStruct((copies, TMSG, KH), BF16),
             jax.ShapeDtypeStruct((PMSG, KH), BF16),
             jax.ShapeDtypeStruct((8, ROWS), F32),
         ],
+        scratch_shapes=[pltpu.VMEM((TMSG, KH), BF16), pltpu.SemaphoreType.DMA((copies,))],
         compiler_params=pltpu.CompilerParams(vmem_limit_bytes=24 * MB),
         cost_estimate=pl.CostEstimate(flops=200_000_000, bytes_accessed=3_000_000, transcendentals=0),
         name="prepare",
     )(own, *parts, ids)
 
 
-def score_kernel(last, t_ref, *refs):
-    pools, refs = refs[:8], refs[8:]
+def score_kernel(last, *refs):
     if last:
-        tmsg, prev, scale, out, pin, pout, t_in, t_out, hot, best, rows = refs
+        t_ref, pin, pout, prev, tmsg, scale, out, t_in, t_out, hot, best, rows = refs
+        best[...] = prev[...]
     else:
-        tmsg, out, pin, pout, t_in, t_out, hot, best, rows = refs
-    half = ROWS // 2
-    low = lane_mask((half, KH), True)
-    for k, pool in enumerate(pools):
-        pin[k * ROWS : (k + 1) * ROWS, :] = pool[0:ROWS, :]
-        packed = pool[ROWS:PMSG, :].astype(F32)
-        turned = pltpu.roll(packed, KG, 1)
-        pout[k * ROWS : k * ROWS + half, :] = jnp.where(low, packed, turned).astype(BF16)
-        pout[k * ROWS + half : (k + 1) * ROWS, :] = jnp.where(low, turned, packed).astype(BF16)
-    best[...] = jnp.full(best.shape, -jnp.inf, F32)
+        pools, (tmsg, pin, pout, best, t_in, t_out, hot) = refs[:8], refs[8:]
+        half = ROWS // 2
+        low = lane_mask((half, KH), True)
+        for k, pool in enumerate(pools):
+            at = k * ROWS
+            pin[at : at + ROWS, :] = pool[0:ROWS, :]
+            packed = pool[ROWS:PMSG, :].astype(F32)
+            turned = pltpu.roll(packed, KG, 1)
+            pout[at : at + half, :] = jnp.where(low, packed, turned).astype(BF16)
+            pout[at + half : at + ROWS, :] = jnp.where(low, turned, packed).astype(BF16)
 
     lane = lax.broadcasted_iota(jnp.int32, (1, KH), 1)
     keep_low = (lane < KG).astype(F32).astype(BF16)
@@ -218,11 +230,12 @@
     tile = 512
     example = lax.broadcasted_iota(jnp.int32, (GROUP * EX, KH), 0).astype(F32)
 
-    def group(g, carry):
+    groups = tmsg.shape[0] // GROUP
+    for g in range(groups):
         for pair in range(GROUP // 2):
             b0 = g * GROUP + 2 * pair
             b1 = b0 + 1
-            at = pair * 2 * TOK
+            at = b0 * TOK
             t_in[at : at + TOK, :] = tmsg[b0, 0:TOK, :]
             t_in[at + TOK : at + TOK + 64, :] = tmsg[b1, 128:TOK, :]
             t_in[at + TOK + 64 : at + 2 * TOK, :] = tmsg[b1, 0:128, :]
@@ -239,63 +252,53 @@
             hot[:, at : at + 128] = (example == i0[0:1, :]).astype(F32).astype(BF16)
             hot[:, at + 128 : at + 256] = (example == mixed).astype(F32).astype(BF16)
             hot[:, at + 256 : at + 384] = (example == i1[0:1, :]).astype(F32).astype(BF16)
-
-        chunk = 512
-
-        def rows_of(c, carry):
-            at = pl.ds(pl.multiple_of(c * chunk, chunk), chunk)
-            left_in = pin[at, :]
-            left_out = pout[at, :]
-            total = None
-            for i in range(width // tile):
-                cols = slice(i * tile, (i + 1) * tile)
-                joined = dot_nt(left_in, t_in[cols, :]) * dot_nt(left_out, t_out[cols, :])
-                part = dot_nt(joined.astype(BF16), hot[:, cols])
-                total = part if total is None else total + part
-            best[at, :] = jnp.maximum(best[at, :], total)
-            return carry
-
-        return lax.fori_loop(0, pin.shape[0] // chunk, rows_of, carry)
-
-    lax.fori_loop(0, tmsg.shape[0] // GROUP, group, 0)
-    t = t_ref[0]
-    for k in range(8):
-        row = jnp.max(best[k * ROWS : (k + 1) * ROWS, :].T, axis=0, keepdims=True)
-        rows[pl.ds(lax.rem(t + 8 - k, 8), 1), :] = row
+    for g in range(groups):
+        total = None
+        for i in range(width // tile):
+            cols = slice(g * width + i * tile, g * width + (i + 1) * tile)
+            joined = dot_nt(pin[...], t_in[cols, :]) * dot_nt(pout[...], t_out[cols, :])
+            part = dot_nt(joined.astype(BF16), hot[:, cols])
+            total = part if total is None else total + part
+        if last or g:
+            best[...] = jnp.maximum(best[...], total)
+        else:
+            best[...] = total
     if last:
-        final = jnp.maximum(rows[...], prev[...])
+        t = t_ref[0]
+        for k in range(8):
+            row = jnp.max(best[k * ROWS : (k + 1) * ROWS, :].T, axis=0, keepdims=True)
+            rows[pl.ds(lax.rem(t + 8 - k, 8), 1), :] = row
         for i in range(out.shape[0]):
-            out[i, 0:8, :] = final
+            out[i, 0:8, :] = rows[...]
             out[i, 8:16, :] = scale[...]
-    else:
-        out[...] = rows[...]
-
-
-def score(t, pools, tmsg, *more):
-    last = len(more) > 0
-    width = GROUP * TOK
-    shape = (8, 16, ROWS) if last else (8, ROWS)
+
+
+def score(last, *operands):
+    tokens = operands[-2 if last else -1].shape[0] * TOK
     vmem = pl.BlockSpec(memory_space=pltpu.VMEM)
+    smem = pl.BlockSpec(memory_space=pltpu.SMEM)
+    unpacked = jax.ShapeDtypeStruct((8 * ROWS, KH), BF16)
+    maxima = jax.ShapeDtypeStruct((8 * ROWS, GROUP * EX), F32)
+    message = jax.ShapeDtypeStruct((8, 16, ROWS), F32)
+    scratch = [
+        pltpu.VMEM((tokens, KH), BF16),
+        pltpu.VMEM((tokens, KH), BF16),
+        pltpu.VMEM((GROUP * EX, tokens), BF16),
+    ]
+    if last:
+        scratch += [pltpu.VMEM(maxima.shape, F32), pltpu.VMEM((8, ROWS), F32)]
     return pl.pallas_call(
         functools.partial(score_kernel, last),
-        in_specs=[pl.BlockSpec(memory_space=pltpu.SMEM)] + [vmem] * (9 + len(more)),
-        out_specs=vmem,
-        out_shape=jax.ShapeDtypeStruct(shape, F32),
-        scratch_shapes=[
-            pltpu.VMEM((8 * ROWS, KH), BF16),
-            pltpu.VMEM((8 * ROWS, KH), BF16),
-            pltpu.VMEM((width, KH), BF16),
-            pltpu.VMEM((width, KH), BF16),
-            pltpu.VMEM((GROUP * EX, width), BF16),
-            pltpu.VMEM((8 * ROWS, GROUP * EX), F32),
-            pltpu.VMEM((8, ROWS), F32),
-        ],
+        in_specs=[smem] * last + [vmem] * (len(operands) - last),
+        out_specs=vmem if last else [vmem] * 3,
+        out_shape=message if last else [unpacked, unpacked, maxima],
+        scratch_shapes=scratch,
         compiler_params=pltpu.CompilerParams(vmem_limit_bytes=24 * MB),
         cost_estimate=pl.CostEstimate(
             flops=5_000_000_000, bytes_accessed=2_000_000, transcendentals=0
         ),
         name="score_last" if last else "score_first",
-    )(t[None], *pools, tmsg, *more)
+    )(*operands)
 
 
 def slots_kernel(t_ref, p_ref, got, owner, out):
@@ -375,20 +378,30 @@
 
     shared = (ph, pg, th, tg, fin, fout.T)
     after = lax.optimization_barrier
-    up, down, opposite = project(
-        LIMITS[0], t, (1, 7, 3, 5, 4), ((0, 0), (1, 0), (0, 1), (1, 1), (2, 0)), (BF16,) * 3, *shared
+    whole = lambda which, slot=0: ((which, slot * MSG, 0, MSG),)
+    halves = ((2, 0, 0, MSG // 2), (3, 0, MSG // 2, MSG))
+    up, down, opposite_up, opposite_down = project(
+        LIMITS[0],
+        t,
+        (1, 7, 3, 5, 4),
+        (whole(0), whole(1), whole(0, 1), whole(1, 1), halves),
+        (BF16,) * 4,
+        *shared,
     )
     from_low = shift(up, "tgt", n_tgt, 1)
     from_high = shift(down, "tgt", n_tgt, n_tgt - 1)
-    across = shift(opposite, "tgt", n_tgt, 4)
+    half_low = shift(opposite_up, "tgt", n_tgt, 2)
+    half_high = shift(opposite_down, "tgt", n_tgt, n_tgt - 2)
     t_next, up = after((t, up))
-    two_up, two_down = project(LIMITS[1], t_next, (2, 6), ((0, 0), (1, 0)), (F32, F32), *shared)
-    two_up, two_down = merge(from_low, from_high, two_up, two_down)
+    two_up, two_down = project(
+        LIMITS[1], t_next, (2, 6), (whole(0), whole(1)), (F32, F32), *shared
+    )
+    two_up, two_down = merge(from_low, from_high, half_low, half_high, two_up, two_down)
     t_next, two_up = after((t, two_up))
     from_low2 = shift(two_up, "tgt", n_tgt, 2)
     from_high2 = shift(two_down, "tgt", n_tgt, n_tgt - 2)
-    (own,) = project(LIMITS[2], t_next, (0,), ((0, 0),), (F32,), *shared)
-    parts = [from_low, from_high, across, from_low2, from_high2]
+    (own,) = project(LIMITS[2], t_next, (0,), (whole(0),), (F32,), *shared)
+    parts = [from_low, from_high, from_low2, from_high2]
     tmsg, pmsg, scale = prepare(own, parts, ids, n_pool // 2)
 
     same_core = [[2 * i + c for i in range(n_pool // 2)] for c in range(2)]
@@ -398,8 +411,8 @@
     pools = [pmsg] + [shift(pmsg, "tgt", n_tgt, k) for k in range(1, n_tgt)]
     near, *pools = after((near, *pools))
     far = lax.ppermute(near, "pool", [(i, i ^ 1) for i in range(n_pool)])
-    partial = score(t, pools, near)
-    best = score(t, pools, far, partial, scale)
+    pin, pout, partial = score(False, *pools, near)
+    best = score(True, t[None], pin, pout, partial, far, scale)
     got = lax.all_to_all(best, "tgt", split_axis=0, concat_axis=0, tiled=True)
     sent = slots(t, p, got, owner.T)
     arrived = lax.all_to_all(sent, "pool", split_axis=0, concat_axis=0, tiled=True)

time: 105 us -> 103 us (0.981)
  waiting for transfers between devices: 14.4 us -> 15.8 us
  Pallas kernels: 28.4 us -> 27.1 us
  starting transfers between devices: 44.6 us -> 43.4 us
    ppermute x12 -> x13, waiting for transfers between devices: 6.22 us -> 8.69 us  [shift(): return lax.ppermute(x, axis, [(i, (i + k) % n) for i in range(n)])]
    ppermute x1, starting transfers between devices: 5.47 us -> 3.12 us  [shards(): far = lax.ppermute(near, 'pool', [(i, i ^ 1) for i in range(n_pool)])]
    pallas_call x3, Pallas kernels: 15.8 us -> 13.9 us  [the longest x2 12 us: score(): pl.pallas_call(functools.partial(score_kernel, last), in_specs=[smem] * l...]
    ppermute x12 -> x13, starting transfers between devices: 27.2 us -> 29 us  [shift(): return lax.ppermute(x, axis, [(i, (i + k) % n) for i in range(n)])]
    all_to_all x1, waiting for transfers between devices: 1.07 us -> 0.01 us  [shards(): lax.all_to_all(tmsg, 'pool', split_axis=0, concat_axis=0, tiled=True, axi...]
  transfers between devices with their start and end apart: 15 -> 16, of which waited for: 7 -> 7; matrix products, arithmetic and copies ran while one was open for 0% -> 0% of each run, Pallas kernels for 12% -> 11%
where the time goes in v3:
time: 103 us
  starting transfers between devices  43.4 us (42%)
  Pallas kernels  27.1 us (26%)
  waiting for transfers between devices  15.8 us (15%)
  blocking collectives  15.5 us (15%)
    ppermute x13, starting transfers between devices, shift(): return lax.ppermute(x, axis, [(i, (i + k) % n) for i in range(n)])  29 us
    all_to_all x1, blocking collectives, shards(): lax.all_to_all(sent, 'pool', split_axis=0, concat_axis=0, tiled=True)  15.5 us
    pallas_call x3, Pallas kernels, project(): pl.pallas_call(functools.partial(project_kernel, steps, kinds), in_specs=...  12.1 us
    pallas_call x2, Pallas kernels, score(): pl.pallas_call(functools.partial(score_kernel, last), in_specs=[smem] * l...  12 us
    ppermute x13, waiting for transfers between devices, shift(): return lax.ppermute(x, axis, [(i, (i + k) % n) for i in range(n)])  8.69 us
    all_to_all x1, waiting for transfers between devices, shards(): got = lax.all_to_all(best, 'tgt', split_axis=0, concat_axis=0, tiled=True)  7.14 us
    all_to_all x1, starting transfers between devices, shards(): lax.all_to_all(tmsg, 'pool', split_axis=0, concat_axis=0, tiled=True, axi...  6.77 us
    all_to_all x1, starting transfers between devices, shards(): got = lax.all_to_all(best, 'tgt', split_axis=0, concat_axis=0, tiled=True)  4.56 us
  transfers between devices with their start and end apart: 16, of which 7 were waited for; matrix products, arithmetic and copies ran while one was open for 0% of the time, Pallas kernels for 11%

profile of v3, /device:TPU:1, one launch (start us, length us, event | category | flops | bytes accessed | tf_op | source)
XLA Modules:
  0.0 102.8 jit_solution(17706082551914669597)
XLA Ops:
  0.7 6.7 %project.3 = (bf16[960,128]{1,0:T(8,128)(2,1)}, bf16[960,128]{1,0:T(8,128)(2,1)}, bf16[240,128]{1,0:T(8,128)(2,1)}, bf16[240,128]{1,0:T(8,128)(2,1)}) custom-call(s32[1]{0:T(128)} %bitcast.t_ref.refs_0_, bf16[1024,1792]{1,0:T(8,128)(2,1)} %ph.5, bf16[1024,512]{1,0:T(8,128)(2,1)} %pg.5, bf16[1536,1792]{1,0:T(8,128)(2,1)} %th.5, bf16[1536,512]{1,0:T(8,128)(2,1)} %tg.5, ...), custom_call_target="tpu_custom_call" | custom-call | flops 850000000 | bytes 8000000 | tf_op jit(solution)/shard_map/project/pallas_call | solution.py:98
  7.3 6.5 %collective-permute-start.1 = (bf16[960,128]{1,0:T(8,128)(2,1)}, bf16[960,128]{1,0:T(8,128)(2,1)S(1)}, u32[]{:S(2)}, u32[]{:S(2)}) collective-permute-start(bf16[960,128]{1,0:T(8,128)(2,1)} %get-tuple-element.55), channel_id=1, source_target_pairs={{0,7},{1,0},{2,1},{3,2},{4,3},{5,4},{6,5},{7,6},{8,15},{9,8},{10,9... | collective-permute-start | bytes 737288 | tf_op jit(solution)/shard_map/ppermute | solution.py:366
  13.8 3.6 %collective-permute-start.3 = (bf16[240,128]{1,0:T(8,128)(2,1)}, bf16[240,128]{1,0:T(8,128)(2,1)S(1)}, u32[]{:S(2)}, u32[]{:S(2)}) collective-permute-start(bf16[240,128]{1,0:T(8,128)(2,1)} %get-tuple-element.57), channel_id=1, source_target_pairs={{0,6},{1,7},{2,0},{3,1},{4,2},{5,3},{6,4},{7,5},{8,14},{9,15},{10,... | collective-permute-start | bytes 184328 | tf_op jit(solution)/shard_map/ppermute | solution.py:366
  17.5 3.1 %project.4 = (f32[480,128]{1,0:T(8,128)S(1)}, f32[480,128]{1,0:T(8,128)S(1)}) custom-call(s32[1]{0:T(128)} %bitcast.3.t_ref, bf16[1024,1792]{1,0:T(8,128)(2,1)} %ph.5, bf16[1024,512]{1,0:T(8,128)(2,1)} %pg.5, bf16[1536,1792]{1,0:T(8,128)(2,1)} %th.5, bf16[1536,512]{1,0:T(8,128)(2,1)} %tg.5, bf16[1792,128]{1,0:T(8,128)(2,1)} %fin.5, bf16[64,512]{1,0:T(8,128)(2,1)S(1)} %bitcast.17), custom_call_target="tpu_custom_call" | custom-call | flops 340000000 | bytes 3200000 | tf_op jit(solution)/shard_map/project/pallas_call | solution.py:98
  20.6 1.9 %collective-permute-done.2.half_low = bf16[240,128]{1,0:T(8,128)(2,1)S(1)} collective-permute-done((bf16[240,128]{1,0:T(8,128)(2,1)}, bf16[240,128]{1,0:T(8,128)(2,1)S(1)}, u32[]{:S(2)}, u32[]{:S(2)}) %collective-permute-start.2) | collective-permute-done | bytes 61472 | tf_op jit(solution)/shard_map/ppermute | solution.py:366
  22.9 3.2 %collective-permute-start.5 = (bf16[480,128]{1,0:T(8,128)(2,1)S(1)}, bf16[480,128]{1,0:T(8,128)(2,1)S(1)}, u32[]{:S(2)}, u32[]{:S(2)}) collective-permute-start(bf16[480,128]{1,0:T(8,128)(2,1)S(1)} %get-tuple-element.64), channel_id=1, source_target_pairs={{0,6},{1,7},{2,0},{3,1},{4,2},{5,3},{6,4},{7,5},{8,14},{9,15},{10,... | collective-permute-start | bytes 368648 | tf_op jit(solution)/shard_map/ppermute | solution.py:366
  26.3 2.4 %project.5.own = f32[480,128]{1,0:T(8,128)S(1)} custom-call(s32[1]{0:T(128)} %bitcast.4.t_ref, bf16[1024,1792]{1,0:T(8,128)(2,1)} %ph.5, bf16[1024,512]{1,0:T(8,128)(2,1)} %pg.5, bf16[1536,1792]{1,0:T(8,128)(2,1)} %th.5, bf16[1536,512]{1,0:T(8,128)(2,1)} %tg.5, bf16[1792,128]{1,0:T(8,128)(2,1)S(1)} %copy-done, bf16[64,512]{1,0:T(8,128)(2,1)S(1)} %bitcast.18), custom_call_target="tpu_custom_call" | custom-call | flops 170000000 | bytes 1600000 | tf_op jit(solution)/shard_map/project/pallas_call | solution.py:98
  29.7 1.9 %prepare.1 = (bf16[16,304,128]{2,1,0:T(8,128)(2,1)}, bf16[192,128]{1,0:T(8,128)(2,1)S(1)}, f32[8,128]{1,0:T(8,128)S(1)}) custom-call(f32[480,128]{1,0:T(8,128)S(1)} %project.5.own, bf16[960,128]{1,0:T(8,128)(2,1)S(1)} %collective-permute-done.from_low.rest_0_, bf16[960,128]{1,0:T(8,128)(2,1)S(1)} %collective-permute-done.1.from_high.rest_1_, ...), custom_call_target="tpu_custom_call" | custom-call | flops 200000000 | bytes 3000000 | tf_op jit(solution)/shard_map/prepare/pallas_call | solution.py:195
  31.6 6.8 %all-to-all-start = ((bf16[16,304,128]{2,1,0:T(8,128)(2,1)}), bf16[16,304,128]{2,1,0:T(8,128)(2,1)S(1)}, u32[]{:S(2)}, u32[]{:S(2)}) async-start(bf16[16,304,128]{2,1,0:T(8,128)(2,1)} %get-tuple-element.65), calls=%async_computation | async-start | bytes 2490368 | tf_op jit(solution)/shard_map/all_to_all | solution.py:408
  38.4 4.8 %collective-permute-start.12 = (bf16[192,128]{1,0:T(8,128)(2,1)S(1)}, bf16[192,128]{1,0:T(8,128)(2,1)S(1)}, u32[]{:S(2)}, u32[]{:S(2)}) collective-permute-start(bf16[192,128]{1,0:T(8,128)(2,1)S(1)} %get-tuple-element.67.refs_0_), channel_id=1, source_target_pairs={{0,7},{1,0},{2,1},{3,2},{4,3},{5,4},{6,5},{7,6},{8,15},{9,8},{10,9... | collective-permute-start | bytes 147464 | tf_op jit(solution)/shard_map/ppermute | solution.py:366
  43.2 3.7 %collective-permute-start.10 = (bf16[192,128]{1,0:T(8,128)(2,1)S(1)}, bf16[192,128]{1,0:T(8,128)(2,1)S(1)}, u32[]{:S(2)}, u32[]{:S(2)}) collective-permute-start(bf16[192,128]{1,0:T(8,128)(2,1)S(1)} %get-tuple-element.67.refs_0_), channel_id=1, source_target_pairs={{0,5},{1,6},{2,7},{3,0},{4,1},{5,2},{6,3},{7,4},{8,13},{9,14},{10,... | collective-permute-start | bytes 147464 | tf_op jit(solution)/shard_map/ppermute | solution.py:366
  46.9 1.7 %collective-permute-start.9 = (bf16[192,128]{1,0:T(8,128)(2,1)S(1)}, bf16[192,128]{1,0:T(8,128)(2,1)S(1)}, u32[]{:S(2)}, u32[]{:S(2)}) collective-permute-start(bf16[192,128]{1,0:T(8,128)(2,1)S(1)} %get-tuple-element.67.refs_0_), channel_id=1, source_target_pairs={{0,4},{1,5},{2,6},{3,7},{4,0},{5,1},{6,2},{7,3},{8,12},{9,13},{10,... | collective-permute-start | bytes 147464 | tf_op jit(solution)/shard_map/ppermute | solution.py:366
  48.7 1.4 %collective-permute-start.8 = (bf16[192,128]{1,0:T(8,128)(2,1)S(1)}, bf16[192,128]{1,0:T(8,128)(2,1)S(1)}, u32[]{:S(2)}, u32[]{:S(2)}) collective-permute-start(bf16[192,128]{1,0:T(8,128)(2,1)S(1)} %get-tuple-element.67.refs_0_), channel_id=1, source_target_pairs={{0,3},{1,4},{2,5},{3,6},{4,7},{5,0},{6,1},{7,2},{8,11},{9,12},{10,... | collective-permute-start | bytes 147464 | tf_op jit(solution)/shard_map/ppermute | solution.py:366
  50.1 3.6 %collective-permute-start.7 = (bf16[192,128]{1,0:T(8,128)(2,1)S(1)}, bf16[192,128]{1,0:T(8,128)(2,1)S(1)}, u32[]{:S(2)}, u32[]{:S(2)}) collective-permute-start(bf16[192,128]{1,0:T(8,128)(2,1)S(1)} %get-tuple-element.67.refs_0_), channel_id=1, source_target_pairs={{0,2},{1,3},{2,4},{3,5},{4,6},{5,7},{6,0},{7,1},{8,10},{9,11},{10,... | collective-permute-start | bytes 147464 | tf_op jit(solution)/shard_map/ppermute | solution.py:366
  53.7 1.2 %collective-permute-done.9.refs_4_ = bf16[192,128]{1,0:T(8,128)(2,1)S(1)} collective-permute-done((bf16[192,128]{1,0:T(8,128)(2,1)S(1)}, bf16[192,128]{1,0:T(8,128)(2,1)S(1)}, u32[]{:S(2)}, u32[]{:S(2)}) %collective-permute-start.9) | collective-permute-done | bytes 49184 | tf_op jit(solution)/shard_map/ppermute | solution.py:366
  54.9 1.2 %collective-permute-done.8.refs_3_ = bf16[192,128]{1,0:T(8,128)(2,1)S(1)} collective-permute-done((bf16[192,128]{1,0:T(8,128)(2,1)S(1)}, bf16[192,128]{1,0:T(8,128)(2,1)S(1)}, u32[]{:S(2)}, u32[]{:S(2)}) %collective-permute-start.8) | collective-permute-done | bytes 49184 | tf_op jit(solution)/shard_map/ppermute | solution.py:366
  56.1 2.2 %collective-permute-done.7.refs_2_ = bf16[192,128]{1,0:T(8,128)(2,1)S(1)} collective-permute-done((bf16[192,128]{1,0:T(8,128)(2,1)S(1)}, bf16[192,128]{1,0:T(8,128)(2,1)S(1)}, u32[]{:S(2)}, u32[]{:S(2)}) %collective-permute-start.7) | collective-permute-done | bytes 49184 | tf_op jit(solution)/shard_map/ppermute | solution.py:366
  58.3 1.1 %collective-permute-done.6.refs_1_ = bf16[192,128]{1,0:T(8,128)(2,1)S(1)} collective-permute-done((bf16[192,128]{1,0:T(8,128)(2,1)S(1)}, bf16[192,128]{1,0:T(8,128)(2,1)S(1)}, u32[]{:S(2)}, u32[]{:S(2)}) %collective-permute-start.6) | collective-permute-done | bytes 49184 | tf_op jit(solution)/shard_map/ppermute | solution.py:366
  59.5 3.1 %collective-permute-start.13 = (bf16[16,304,128]{2,1,0:T(8,128)(2,1)S(1)}, bf16[16,304,128]{2,1,0:T(8,128)(2,1)S(1)}, u32[]{:S(2)}, u32[]{:S(2)}) collective-permute-start(bf16[16,304,128]{2,1,0:T(8,128)(2,1)S(1)} %all-to-all-done.refs_8_), channel_id=1, source_target_pairs={{0,8},{8,0},{16,24},{24,16},{32,40},{40,32},{48,56},{56,48},{64,72... | collective-permute-start | bytes 3735560 | tf_op jit(solution)/shard_map/ppermute | solution.py:413
  62.6 5.6 %score_first.1 = (bf16[1024,128]{1,0:T(8,128)(2,1)S(1)}, bf16[1024,128]{1,0:T(8,128)(2,1)S(1)}, f32[1024,128]{1,0:T(8,128)S(1)}) custom-call(bf16[192,128]{1,0:T(8,128)(2,1)S(1)} %get-tuple-element.67.refs_0_, bf16[192,128]{1,0:T(8,128)(2,1)S(1)} %collective-permute-done.6.refs_1_, bf16[192,128]{1,0:T(8,128)(2,1)S(1)} %collective-permute-done.7.refs_2_, ...), custom_call_target="tpu_custom_call" | custom-call | flops 5000000000 | bytes 2000000 | tf_op jit(solution)/shard_map/score_first/pallas_call | solution.py:290
  68.3 6.3 %score_last.1 = f32[8,16,128]{2,1,0:T(8,128)} custom-call(s32[1]{0:T(128)} %bitcast.t_ref.refs_0_, bf16[1024,128]{1,0:T(8,128)(2,1)S(1)} %get-tuple-element.76.refs_1_, bf16[1024,128]{1,0:T(8,128)(2,1)S(1)} %get-tuple-element.77.refs_2_, f32[1024,128]{1,0:T(8,128)S(1)} %get-tuple-element.78.refs_3_, ...), custom_call_target="tpu_custom_call" | custom-call | flops 5000000000 | bytes 2000000 | tf_op jit(solution)/shard_map/score_last/pallas_call | solution.py:290
  74.6 4.6 %all-to-all-start.1 = ((f32[8,16,128]{2,1,0:T(8,128)}), f32[8,16,128]{2,1,0:T(8,128)S(1)}, u32[]{:S(2)}, u32[]{:S(2)}) async-start(f32[8,16,128]{2,1,0:T(8,128)} %score_last.1), calls=%async_computation.1 | async-start | bytes 131072 | tf_op jit(solution)/shard_map/all_to_all | solution.py:416
  79.1 7.1 %all-to-all-done.1.got = f32[8,16,128]{2,1,0:T(8,128)S(1)} async-done(((f32[8,16,128]{2,1,0:T(8,128)}), f32[8,16,128]{2,1,0:T(8,128)S(1)}, u32[]{:S(2)}, u32[]{:S(2)}) %all-to-all-start.1) | async-done | bytes 65568 | tf_op jit(solution)/shard_map/all_to_all | solution.py:416
  86.6 15.5 %all_to_all.21 = f32[32,1,128]{2,1,0:T(1,128)S(1)} all-to-all(f32[32,1,128]{2,1,0:T(1,128)S(1)} %bitcast.20), channel_id=1, replica_groups=mesh['pool'=32,'tgt'=8] {'pool'}, dimensions={0} | all-to-all | bytes 32768 | tf_op jit(solution)/shard_map/all_to_all | solution.py:418
  (32 shorter events, 2.7 us)
Async XLA Ops:
  0.6 16.8 %copy-start.3 = (s32[1,192]{1,0:T(1,128)S(1)}, s32[1,192]{1,0:T(1,128)}, u32[]{:S(2)}) copy-start(s32[1,192]{1,0:T(1,128)} %param.18) | copy-start | bytes 2308
  0.6 16.8 %copy-start.1 = (bf16[512,64]{0,1:T(8,128)(2,1)S(1)}, bf16[512,64]{0,1:T(8,128)(2,1)}, u32[]{:S(2)}) copy-start(bf16[512,64]{0,1:T(8,128)(2,1)} %param.17) | copy-start | bytes 196612
  7.3 15.1 %collective-permute-start.1 = (bf16[960,128]{1,0:T(8,128)(2,1)}, bf16[960,128]{1,0:T(8,128)(2,1)S(1)}, u32[]{:S(2)}, u32[]{:S(2)}) collective-permute-start(bf16[960,128]{1,0:T(8,128)(2,1)} %get-tuple-element.55), channel_id=1, source_target_pairs={{0,7},{1,0},{2,1},{3,2},{4,3},{5,4},{6,5},{7,6},{8,15},{9,8},{10,9... | collective-permute-start | bytes 737288 | tf_op jit(solution)/shard_map/ppermute | solution.py:366
  13.8 8.6 %collective-permute-start = (bf16[960,128]{1,0:T(8,128)(2,1)}, bf16[960,128]{1,0:T(8,128)(2,1)S(1)}, u32[]{:S(2)}, u32[]{:S(2)}) collective-permute-start(bf16[960,128]{1,0:T(8,128)(2,1)} %get-tuple-element.54), channel_id=1, source_target_pairs={{0,1},{1,2},{2,3},{3,4},{4,5},{5,6},{6,7},{7,0},{8,9},{9,10},{10,1... | collective-permute-start | bytes 737288 | tf_op jit(solution)/shard_map/ppermute | solution.py:366
  13.8 8.6 %collective-permute-start.2 = (bf16[240,128]{1,0:T(8,128)(2,1)}, bf16[240,128]{1,0:T(8,128)(2,1)S(1)}, u32[]{:S(2)}, u32[]{:S(2)}) collective-permute-start(bf16[240,128]{1,0:T(8,128)(2,1)} %get-tuple-element.56), channel_id=1, source_target_pairs={{0,2},{1,3},{2,4},{3,5},{4,6},{5,7},{6,0},{7,1},{8,10},{9,11},{10,... | collective-permute-start | bytes 184328 | tf_op jit(solution)/shard_map/ppermute | solution.py:366
  13.8 8.6 %collective-permute-start.3 = (bf16[240,128]{1,0:T(8,128)(2,1)}, bf16[240,128]{1,0:T(8,128)(2,1)S(1)}, u32[]{:S(2)}, u32[]{:S(2)}) collective-permute-start(bf16[240,128]{1,0:T(8,128)(2,1)} %get-tuple-element.57), channel_id=1, source_target_pairs={{0,6},{1,7},{2,0},{3,1},{4,2},{5,3},{6,4},{7,5},{8,14},{9,15},{10,... | collective-permute-start | bytes 184328 | tf_op jit(solution)/shard_map/ppermute | solution.py:366
  17.4 8.8 %copy-start = (bf16[1792,128]{1,0:T(8,128)(2,1)S(1)}, bf16[1792,128]{1,0:T(8,128)(2,1)}, u32[]{:S(2)}) copy-start(bf16[1792,128]{1,0:T(8,128)(2,1)} %fin.5) | copy-start | bytes 1376260
  22.5 7.1 %collective-permute-start.4 = (bf16[480,128]{1,0:T(8,128)(2,1)S(1)}, bf16[480,128]{1,0:T(8,128)(2,1)S(1)}, u32[]{:S(2)}, u32[]{:S(2)}) collective-permute-start(bf16[480,128]{1,0:T(8,128)(2,1)S(1)} %get-tuple-element.63), channel_id=1, source_target_pairs={{0,2},{1,3},{2,4},{3,5},{4,6},{5,7},{6,0},{7,1},{8,10},{9,11},{10,... | collective-permute-start | bytes 368648 | tf_op jit(solution)/shard_map/ppermute | solution.py:366
  22.9 6.7 %collective-permute-start.5 = (bf16[480,128]{1,0:T(8,128)(2,1)S(1)}, bf16[480,128]{1,0:T(8,128)(2,1)S(1)}, u32[]{:S(2)}, u32[]{:S(2)}) collective-permute-start(bf16[480,128]{1,0:T(8,128)(2,1)S(1)} %get-tuple-element.64), channel_id=1, source_target_pairs={{0,6},{1,7},{2,0},{3,1},{4,2},{5,3},{6,4},{7,5},{8,14},{9,15},{10,... | collective-permute-start | bytes 368648 | tf_op jit(solution)/shard_map/ppermute | solution.py:366
  31.6 27.9 %all-to-all-start = ((bf16[16,304,128]{2,1,0:T(8,128)(2,1)}), bf16[16,304,128]{2,1,0:T(8,128)(2,1)S(1)}, u32[]{:S(2)}, u32[]{:S(2)}) async-start(bf16[16,304,128]{2,1,0:T(8,128)(2,1)} %get-tuple-element.65), calls=%async_computation | async-start | bytes 2490368 | tf_op jit(solution)/shard_map/all_to_all | solution.py:408
  38.4 11.7 %collective-permute-start.12 = (bf16[192,128]{1,0:T(8,128)(2,1)S(1)}, bf16[192,128]{1,0:T(8,128)(2,1)S(1)}, u32[]{:S(2)}, u32[]{:S(2)}) collective-permute-start(bf16[192,128]{1,0:T(8,128)(2,1)S(1)} %get-tuple-element.67.refs_0_), channel_id=1, source_target_pairs={{0,7},{1,0},{2,1},{3,2},{4,3},{5,4},{6,5},{7,6},{8,15},{9,8},{10,9... | collective-permute-start | bytes 147464 | tf_op jit(solution)/shard_map/ppermute | solution.py:366
  43.2 10.5 %collective-permute-start.11 = (bf16[192,128]{1,0:T(8,128)(2,1)S(1)}, bf16[192,128]{1,0:T(8,128)(2,1)S(1)}, u32[]{:S(2)}, u32[]{:S(2)}) collective-permute-start(bf16[192,128]{1,0:T(8,128)(2,1)S(1)} %get-tuple-element.67.refs_0_), channel_id=1, source_target_pairs={{0,6},{1,7},{2,0},{3,1},{4,2},{5,3},{6,4},{7,5},{8,14},{9,15},{10,... | collective-permute-start | bytes 147464 | tf_op jit(solution)/shard_map/ppermute | solution.py:366
  43.2 10.5 %collective-permute-start.10 = (bf16[192,128]{1,0:T(8,128)(2,1)S(1)}, bf16[192,128]{1,0:T(8,128)(2,1)S(1)}, u32[]{:S(2)}, u32[]{:S(2)}) collective-permute-start(bf16[192,128]{1,0:T(8,128)(2,1)S(1)} %get-tuple-element.67.refs_0_), channel_id=1, source_target_pairs={{0,5},{1,6},{2,7},{3,0},{4,1},{5,2},{6,3},{7,4},{8,13},{9,14},{10,... | collective-permute-start | bytes 147464 | tf_op jit(solution)/shard_map/ppermute | solution.py:366
  46.9 8.0 %collective-permute-start.9 = (bf16[192,128]{1,0:T(8,128)(2,1)S(1)}, bf16[192,128]{1,0:T(8,128)(2,1)S(1)}, u32[]{:S(2)}, u32[]{:S(2)}) collective-permute-start(bf16[192,128]{1,0:T(8,128)(2,1)S(1)} %get-tuple-element.67.refs_0_), channel_id=1, source_target_pairs={{0,4},{1,5},{2,6},{3,7},{4,0},{5,1},{6,2},{7,3},{8,12},{9,13},{10,... | collective-permute-start | bytes 147464 | tf_op jit(solution)/shard_map/ppermute | solution.py:366
  48.7 7.5 %collective-permute-start.8 = (bf16[192,128]{1,0:T(8,128)(2,1)S(1)}, bf16[192,128]{1,0:T(8,128)(2,1)S(1)}, u32[]{:S(2)}, u32[]{:S(2)}) collective-permute-start(bf16[192,128]{1,0:T(8,128)(2,1)S(1)} %get-tuple-element.67.refs_0_), channel_id=1, source_target_pairs={{0,3},{1,4},{2,5},{3,6},{4,7},{5,0},{6,1},{7,2},{8,11},{9,12},{10,... | collective-permute-start | bytes 147464 | tf_op jit(solution)/shard_map/ppermute | solution.py:366
  50.1 8.2 %collective-permute-start.7 = (bf16[192,128]{1,0:T(8,128)(2,1)S(1)}, bf16[192,128]{1,0:T(8,128)(2,1)S(1)}, u32[]{:S(2)}, u32[]{:S(2)}) collective-permute-start(bf16[192,128]{1,0:T(8,128)(2,1)S(1)} %get-tuple-element.67.refs_0_), channel_id=1, source_target_pairs={{0,2},{1,3},{2,4},{3,5},{4,6},{5,7},{6,0},{7,1},{8,10},{9,11},{10,... | collective-permute-start | bytes 147464 | tf_op jit(solution)/shard_map/ppermute | solution.py:366
  53.7 5.8 %collective-permute-start.6 = (bf16[192,128]{1,0:T(8,128)(2,1)S(1)}, bf16[192,128]{1,0:T(8,128)(2,1)S(1)}, u32[]{:S(2)}, u32[]{:S(2)}) collective-permute-start(bf16[192,128]{1,0:T(8,128)(2,1)S(1)} %get-tuple-element.67.refs_0_), channel_id=1, source_target_pairs={{0,1},{1,2},{2,3},{3,4},{4,5},{5,6},{6,7},{7,0},{8,9},{9,10},{10,1... | collective-permute-start | bytes 147464 | tf_op jit(solution)/shard_map/ppermute | solution.py:366
  59.5 8.7 %collective-permute-start.13 = (bf16[16,304,128]{2,1,0:T(8,128)(2,1)S(1)}, bf16[16,304,128]{2,1,0:T(8,128)(2,1)S(1)}, u32[]{:S(2)}, u32[]{:S(2)}) collective-permute-start(bf16[16,304,128]{2,1,0:T(8,128)(2,1)S(1)} %all-to-all-done.refs_8_), channel_id=1, source_target_pairs={{0,8},{8,0},{16,24},{24,16},{32,40},{40,32},{48,56},{56,48},{64,72... | collective-permute-start | bytes 3735560 | tf_op jit(solution)/shard_map/ppermute | solution.py:413
  68.2 18.1 %copy-start.2 = (s32[128,1]{0,1:T(1,128)S(1)}, s32[128,1]{0,1:T(1,128)}, u32[]{:S(2)}) copy-start(s32[128,1]{0,1:T(1,128)} %param.19) | copy-start | bytes 1540
  74.6 11.7 %all-to-all-start.1 = ((f32[8,16,128]{2,1,0:T(8,128)}), f32[8,16,128]{2,1,0:T(8,128)S(1)}, u32[]{:S(2)}, u32[]{:S(2)}) async-start(f32[8,16,128]{2,1,0:T(8,128)} %score_last.1), calls=%async_computation.1 | async-start | bytes 131072 | tf_op jit(solution)/shard_map/all_to_all | solution.py:416

commit v4 on v3

--- a/solution.py
+++ b/solution.py
@@ -22,6 +22,7 @@
 PMSG = ROWS + ROWS // 2
 MB = 1024 * 1024
 LIMITS = (60, 53, 53)
+POOL_ORDER = (7, 1, 6, 2, 5, 3, 4)
 
 
 def dot_nt(a, b, precision=None):
@@ -164,16 +165,20 @@
         ],
         axis=0,
     )
+    message[TOK : TOK + TOK // 2, :] = tgt_out.astype(BF16)
+    message[TOK + TOK // 2 : TMSG, :] = ids_ref[...]
+    copies = []
+    for i in range(tmsg.shape[0]):
+        for j, rows in enumerate((slice(TOK, TMSG), slice(0, TOK))):
+            here, there = message.at[rows, :], tmsg.at[i, rows, :]
+            copies.append(pltpu.make_async_copy(here, there, sems.at[i, j]))
+    for copy in copies[0::2]:
+        copy.start()
     gram = dot_nt(wide_in, wide_in, HIGHEST) * dot_nt(wide_out, wide_out, HIGHEST)
     spread = jnp.sum(jnp.where(same, gram, 0.0), axis=0, keepdims=True)
     token_sq = jnp.sum(jnp.where(same, spread, 0.0), axis=1, keepdims=True)
     message[0:TOK, :] = (tgt_in * lax.rsqrt(token_sq[0:TOK] + 1e-06)).astype(BF16)
-    message[TOK : TOK + TOK // 2, :] = tgt_out.astype(BF16)
-    message[TOK + TOK // 2 : TMSG, :] = ids_ref[...]
-    copies = [
-        pltpu.make_async_copy(message, tmsg.at[i], sems.at[i]) for i in range(tmsg.shape[0])
-    ]
-    for copy in copies:
+    for copy in copies[1::2]:
         copy.start()
 
     pmsg[0:ROWS, :] = pool_in.astype(BF16)
@@ -200,7 +205,7 @@
             jax.ShapeDtypeStruct((PMSG, KH), BF16),
             jax.ShapeDtypeStruct((8, ROWS), F32),
         ],
-        scratch_shapes=[pltpu.VMEM((TMSG, KH), BF16), pltpu.SemaphoreType.DMA((copies,))],
+        scratch_shapes=[pltpu.VMEM((TMSG, KH), BF16), pltpu.SemaphoreType.DMA((copies, 2))],
         compiler_params=pltpu.CompilerParams(vmem_limit_bytes=24 * MB),
         cost_estimate=pl.CostEstimate(flops=200_000_000, bytes_accessed=3_000_000, transcendentals=0),
         name="prepare",
@@ -215,7 +220,7 @@
         pools, (tmsg, pin, pout, best, t_in, t_out, hot) = refs[:8], refs[8:]
         half = ROWS // 2
         low = lane_mask((half, KH), True)
-        for k, pool in enumerate(pools):
+        for k, pool in zip((0,) + POOL_ORDER, pools):
             at = k * ROWS
             pin[at : at + ROWS, :] = pool[0:ROWS, :]
             packed = pool[ROWS:PMSG, :].astype(F32)
@@ -408,7 +413,7 @@
     near = lax.all_to_all(
         tmsg, "pool", split_axis=0, concat_axis=0, tiled=True, axis_index_groups=same_core
     )
-    pools = [pmsg] + [shift(pmsg, "tgt", n_tgt, k) for k in range(1, n_tgt)]
+    pools = [pmsg] + [shift(pmsg, "tgt", n_tgt, k) for k in POOL_ORDER]
     near, *pools = after((near, *pools))
     far = lax.ppermute(near, "pool", [(i, i ^ 1) for i in range(n_pool)])
     pin, pout, partial = score(False, *pools, near)

time: 103 us -> 102 us (level)
  waiting for transfers between devices: 15.8 us -> 11.8 us
  starting transfers between devices: 43.4 us -> 46.6 us
    ppermute x13, waiting for transfers between devices: 8.69 us -> 4.67 us  [shift(): return lax.ppermute(x, axis, [(i, (i + k) % n) for i in range(n)])]
    ppermute x1, starting transfers between devices: 3.12 us -> 5.73 us  [shards(): far = lax.ppermute(near, 'pool', [(i, i ^ 1) for i in range(n_pool)])]
  transfers between devices with their start and end apart: 16 -> 16, of which waited for: 7 -> 6; matrix products, arithmetic and copies ran while one was open for 0% -> 0% of each run, Pallas kernels for 11% -> 11%
where the time goes in v4:
time: 102 us; the launch traced here: 101 us
  starting transfers between devices  46.6 us (46%)
  Pallas kernels  27.2 us (27%)
  blocking collectives  15 us (15%)
  waiting for transfers between devices  11.8 us (12%)
    ppermute x13, starting transfers between devices, shift(): return lax.ppermute(x, axis, [(i, (i + k) % n) for i in range(n)])  28.7 us
    all_to_all x1, blocking collectives, shards(): lax.all_to_all(sent, 'pool', split_axis=0, concat_axis=0, tiled=True)  15 us
    pallas_call x3, Pallas kernels, project(): pl.pallas_call(functools.partial(project_kernel, steps, kinds), in_specs=...  12.1 us
    pallas_call x2, Pallas kernels, score(): pl.pallas_call(functools.partial(score_kernel, last), in_specs=[smem] * l...  12 us
    all_to_all x1, waiting for transfers between devices, shards(): got = lax.all_to_all(best, 'tgt', split_axis=0, concat_axis=0, tiled=True)  7.14 us
    all_to_all x1, starting transfers between devices, shards(): lax.all_to_all(tmsg, 'pool', split_axis=0, concat_axis=0, tiled=True, axi...  6.77 us
    ppermute x1, starting transfers between devices, shards(): far = lax.ppermute(near, 'pool', [(i, i ^ 1) for i in range(n_pool)])  5.73 us
    all_to_all x1, starting transfers between devices, shards(): got = lax.all_to_all(best, 'tgt', split_axis=0, concat_axis=0, tiled=True)  5.37 us
  transfers between devices with their start and end apart: 16, of which 6 were waited for; matrix products, arithmetic and copies ran while one was open for 0% of the time, Pallas kernels for 11%

profile of v4, /device:TPU:1, one launch (start us, length us, event | category | flops | bytes accessed | tf_op | source)
XLA Modules:
  0.0 101.5 jit_solution(16301598212606997798)
XLA Ops:
  0.7 6.7 %project.3 = (bf16[960,128]{1,0:T(8,128)(2,1)}, bf16[960,128]{1,0:T(8,128)(2,1)}, bf16[240,128]{1,0:T(8,128)(2,1)}, bf16[240,128]{1,0:T(8,128)(2,1)}) custom-call(s32[1]{0:T(128)} %bitcast.t_ref.refs_0_, bf16[1024,1792]{1,0:T(8,128)(2,1)} %ph.5, bf16[1024,512]{1,0:T(8,128)(2,1)} %pg.5, bf16[1536,1792]{1,0:T(8,128)(2,1)} %th.5, bf16[1536,512]{1,0:T(8,128)(2,1)} %tg.5, ...), custom_call_target="tpu_custom_call" | custom-call | flops 850000000 | bytes 8000000 | tf_op jit(solution)/shard_map/project/pallas_call | solution.py:99
  7.3 6.5 %collective-permute-start.1 = (bf16[960,128]{1,0:T(8,128)(2,1)}, bf16[960,128]{1,0:T(8,128)(2,1)S(1)}, u32[]{:S(2)}, u32[]{:S(2)}) collective-permute-start(bf16[960,128]{1,0:T(8,128)(2,1)} %get-tuple-element.55), channel_id=1, source_target_pairs={{0,7},{1,0},{2,1},{3,2},{4,3},{5,4},{6,5},{7,6},{8,15},{9,8},{10,9... | collective-permute-start | bytes 737288 | tf_op jit(solution)/shard_map/ppermute | solution.py:371
  13.8 3.6 %collective-permute-start.3 = (bf16[240,128]{1,0:T(8,128)(2,1)}, bf16[240,128]{1,0:T(8,128)(2,1)S(1)}, u32[]{:S(2)}, u32[]{:S(2)}) collective-permute-start(bf16[240,128]{1,0:T(8,128)(2,1)} %get-tuple-element.57), channel_id=1, source_target_pairs={{0,6},{1,7},{2,0},{3,1},{4,2},{5,3},{6,4},{7,5},{8,14},{9,15},{10,... | collective-permute-start | bytes 184328 | tf_op jit(solution)/shard_map/ppermute | solution.py:371
  17.5 3.1 %project.4 = (f32[480,128]{1,0:T(8,128)S(1)}, f32[480,128]{1,0:T(8,128)S(1)}) custom-call(s32[1]{0:T(128)} %bitcast.3.t_ref, bf16[1024,1792]{1,0:T(8,128)(2,1)} %ph.5, bf16[1024,512]{1,0:T(8,128)(2,1)} %pg.5, bf16[1536,1792]{1,0:T(8,128)(2,1)} %th.5, bf16[1536,512]{1,0:T(8,128)(2,1)} %tg.5, bf16[1792,128]{1,0:T(8,128)(2,1)} %fin.5, bf16[64,512]{1,0:T(8,128)(2,1)S(1)} %bitcast.17), custom_call_target="tpu_custom_call" | custom-call | flops 340000000 | bytes 3200000 | tf_op jit(solution)/shard_map/project/pallas_call | solution.py:99
  20.6 1.9 %collective-permute-done.2.half_low = bf16[240,128]{1,0:T(8,128)(2,1)S(1)} collective-permute-done((bf16[240,128]{1,0:T(8,128)(2,1)}, bf16[240,128]{1,0:T(8,128)(2,1)S(1)}, u32[]{:S(2)}, u32[]{:S(2)}) %collective-permute-start.2) | collective-permute-done | bytes 61472 | tf_op jit(solution)/shard_map/ppermute | solution.py:371
  22.9 3.2 %collective-permute-start.5 = (bf16[480,128]{1,0:T(8,128)(2,1)S(1)}, bf16[480,128]{1,0:T(8,128)(2,1)S(1)}, u32[]{:S(2)}, u32[]{:S(2)}) collective-permute-start(bf16[480,128]{1,0:T(8,128)(2,1)S(1)} %get-tuple-element.64), channel_id=1, source_target_pairs={{0,6},{1,7},{2,0},{3,1},{4,2},{5,3},{6,4},{7,5},{8,14},{9,15},{10,... | collective-permute-start | bytes 368648 | tf_op jit(solution)/shard_map/ppermute | solution.py:371
  26.3 2.4 %project.5.own = f32[480,128]{1,0:T(8,128)S(1)} custom-call(s32[1]{0:T(128)} %bitcast.4.t_ref, bf16[1024,1792]{1,0:T(8,128)(2,1)} %ph.5, bf16[1024,512]{1,0:T(8,128)(2,1)} %pg.5, bf16[1536,1792]{1,0:T(8,128)(2,1)} %th.5, bf16[1536,512]{1,0:T(8,128)(2,1)} %tg.5, bf16[1792,128]{1,0:T(8,128)(2,1)S(1)} %copy-done, bf16[64,512]{1,0:T(8,128)(2,1)S(1)} %bitcast.18), custom_call_target="tpu_custom_call" | custom-call | flops 170000000 | bytes 1600000 | tf_op jit(solution)/shard_map/project/pallas_call | solution.py:99
  28.7 1.0 collective-permute-done.4.rest_2_
  29.7 2.0 %prepare.1 = (bf16[16,304,128]{2,1,0:T(8,128)(2,1)}, bf16[192,128]{1,0:T(8,128)(2,1)S(1)}, f32[8,128]{1,0:T(8,128)S(1)}) custom-call(f32[480,128]{1,0:T(8,128)S(1)} %project.5.own, bf16[960,128]{1,0:T(8,128)(2,1)S(1)} %collective-permute-done.from_low.rest_0_, bf16[960,128]{1,0:T(8,128)(2,1)S(1)} %collective-permute-done.1.from_high.rest_1_, ...), custom_call_target="tpu_custom_call" | custom-call | flops 200000000 | bytes 3000000 | tf_op jit(solution)/shard_map/prepare/pallas_call | solution.py:200
  31.7 6.8 %all-to-all-start = ((bf16[16,304,128]{2,1,0:T(8,128)(2,1)}), bf16[16,304,128]{2,1,0:T(8,128)(2,1)S(1)}, u32[]{:S(2)}, u32[]{:S(2)}) async-start(bf16[16,304,128]{2,1,0:T(8,128)(2,1)} %get-tuple-element.65), calls=%async_computation | async-start | bytes 2490368 | tf_op jit(solution)/shard_map/all_to_all | solution.py:413
  38.5 4.2 %collective-permute-start.12 = (bf16[192,128]{1,0:T(8,128)(2,1)S(1)}, bf16[192,128]{1,0:T(8,128)(2,1)S(1)}, u32[]{:S(2)}, u32[]{:S(2)}) collective-permute-start(bf16[192,128]{1,0:T(8,128)(2,1)S(1)} %get-tuple-element.67.refs_0_), channel_id=1, source_target_pairs={{0,4},{1,5},{2,6},{3,7},{4,0},{5,1},{6,2},{7,3},{8,12},{9,13},{10,... | collective-permute-start | bytes 147464 | tf_op jit(solution)/shard_map/ppermute | solution.py:371
  42.7 3.5 %collective-permute-start.11 = (bf16[192,128]{1,0:T(8,128)(2,1)S(1)}, bf16[192,128]{1,0:T(8,128)(2,1)S(1)}, u32[]{:S(2)}, u32[]{:S(2)}) collective-permute-start(bf16[192,128]{1,0:T(8,128)(2,1)S(1)} %get-tuple-element.67.refs_0_), channel_id=1, source_target_pairs={{0,3},{1,4},{2,5},{3,6},{4,7},{5,0},{6,1},{7,2},{8,11},{9,12},{10,... | collective-permute-start | bytes 147464 | tf_op jit(solution)/shard_map/ppermute | solution.py:371
  46.2 0.9 collective-permute-start.10
  47.2 1.8 %collective-permute-start.9 = (bf16[192,128]{1,0:T(8,128)(2,1)S(1)}, bf16[192,128]{1,0:T(8,128)(2,1)S(1)}, u32[]{:S(2)}, u32[]{:S(2)}) collective-permute-start(bf16[192,128]{1,0:T(8,128)(2,1)S(1)} %get-tuple-element.67.refs_0_), channel_id=1, source_target_pairs={{0,2},{1,3},{2,4},{3,5},{4,6},{5,7},{6,0},{7,1},{8,10},{9,11},{10,... | collective-permute-start | bytes 147464 | tf_op jit(solution)/shard_map/ppermute | solution.py:371
  49.0 1.8 %collective-permute-start.8 = (bf16[192,128]{1,0:T(8,128)(2,1)S(1)}, bf16[192,128]{1,0:T(8,128)(2,1)S(1)}, u32[]{:S(2)}, u32[]{:S(2)}) collective-permute-start(bf16[192,128]{1,0:T(8,128)(2,1)S(1)} %get-tuple-element.67.refs_0_), channel_id=1, source_target_pairs={{0,6},{1,7},{2,0},{3,1},{4,2},{5,3},{6,4},{7,5},{8,14},{9,15},{10,... | collective-permute-start | bytes 147464 | tf_op jit(solution)/shard_map/ppermute | solution.py:371
  50.8 0.9 collective-permute-start.7
  51.7 1.7 %collective-permute-start.6 = (bf16[192,128]{1,0:T(8,128)(2,1)S(1)}, bf16[192,128]{1,0:T(8,128)(2,1)S(1)}, u32[]{:S(2)}, u32[]{:S(2)}) collective-permute-start(bf16[192,128]{1,0:T(8,128)(2,1)S(1)} %get-tuple-element.67.refs_0_), channel_id=1, source_target_pairs={{0,7},{1,0},{2,1},{3,2},{4,3},{5,4},{6,5},{7,6},{8,15},{9,8},{10,9... | collective-permute-start | bytes 147464 | tf_op jit(solution)/shard_map/ppermute | solution.py:371
  54.3 0.9 collective-permute-done.7.refs_2_
  55.2 5.7 %collective-permute-start.13 = (bf16[16,304,128]{2,1,0:T(8,128)(2,1)S(1)}, bf16[16,304,128]{2,1,0:T(8,128)(2,1)S(1)}, u32[]{:S(2)}, u32[]{:S(2)}) collective-permute-start(bf16[16,304,128]{2,1,0:T(8,128)(2,1)S(1)} %all-to-all-done.refs_8_), channel_id=1, source_target_pairs={{0,8},{8,0},{16,24},{24,16},{32,40},{40,32},{48,56},{56,48},{64,72... | collective-permute-start | bytes 3735560 | tf_op jit(solution)/shard_map/ppermute | solution.py:418
  60.9 5.6 %score_first.1 = (bf16[1024,128]{1,0:T(8,128)(2,1)S(1)}, bf16[1024,128]{1,0:T(8,128)(2,1)S(1)}, f32[1024,128]{1,0:T(8,128)S(1)}) custom-call(bf16[192,128]{1,0:T(8,128)(2,1)S(1)} %get-tuple-element.67.refs_0_, bf16[192,128]{1,0:T(8,128)(2,1)S(1)} %collective-permute-done.6.refs_1_, bf16[192,128]{1,0:T(8,128)(2,1)S(1)} %collective-permute-done.7.refs_2_, ...), custom_call_target="tpu_custom_call" | custom-call | flops 5000000000 | bytes 2000000 | tf_op jit(solution)/shard_map/score_first/pallas_call | solution.py:295
  66.6 6.3 %score_last.1 = f32[8,16,128]{2,1,0:T(8,128)} custom-call(s32[1]{0:T(128)} %bitcast.t_ref.refs_0_, bf16[1024,128]{1,0:T(8,128)(2,1)S(1)} %get-tuple-element.76.refs_1_, bf16[1024,128]{1,0:T(8,128)(2,1)S(1)} %get-tuple-element.77.refs_2_, f32[1024,128]{1,0:T(8,128)S(1)} %get-tuple-element.78.refs_3_, ...), custom_call_target="tpu_custom_call" | custom-call | flops 5000000000 | bytes 2000000 | tf_op jit(solution)/shard_map/score_last/pallas_call | solution.py:295
  72.9 5.4 %all-to-all-start.1 = ((f32[8,16,128]{2,1,0:T(8,128)}), f32[8,16,128]{2,1,0:T(8,128)S(1)}, u32[]{:S(2)}, u32[]{:S(2)}) async-start(f32[8,16,128]{2,1,0:T(8,128)} %score_last.1), calls=%async_computation.1 | async-start | bytes 131072 | tf_op jit(solution)/shard_map/all_to_all | solution.py:421
  78.3 7.1 %all-to-all-done.1.got = f32[8,16,128]{2,1,0:T(8,128)S(1)} async-done(((f32[8,16,128]{2,1,0:T(8,128)}), f32[8,16,128]{2,1,0:T(8,128)S(1)}, u32[]{:S(2)}, u32[]{:S(2)}) %all-to-all-start.1) | async-done | bytes 65568 | tf_op jit(solution)/shard_map/all_to_all | solution.py:421
  85.7 15.0 %all_to_all.21 = f32[32,1,128]{2,1,0:T(1,128)S(1)} all-to-all(f32[32,1,128]{2,1,0:T(1,128)S(1)} %bitcast.20), channel_id=1, replica_groups=mesh['pool'=32,'tgt'=8] {'pool'}, dimensions={0} | all-to-all | bytes 32768 | tf_op jit(solution)/shard_map/all_to_all | solution.py:423
  (32 shorter events, 2.6 us)
Async XLA Ops:
  0.6 16.8 %copy-start.3 = (s32[1,192]{1,0:T(1,128)S(1)}, s32[1,192]{1,0:T(1,128)}, u32[]{:S(2)}) copy-start(s32[1,192]{1,0:T(1,128)} %param.18) | copy-start | bytes 2308
  0.6 16.8 %copy-start.1 = (bf16[512,64]{0,1:T(8,128)(2,1)S(1)}, bf16[512,64]{0,1:T(8,128)(2,1)}, u32[]{:S(2)}) copy-start(bf16[512,64]{0,1:T(8,128)(2,1)} %param.17) | copy-start | bytes 196612
  7.3 15.1 %collective-permute-start.1 = (bf16[960,128]{1,0:T(8,128)(2,1)}, bf16[960,128]{1,0:T(8,128)(2,1)S(1)}, u32[]{:S(2)}, u32[]{:S(2)}) collective-permute-start(bf16[960,128]{1,0:T(8,128)(2,1)} %get-tuple-element.55), channel_id=1, source_target_pairs={{0,7},{1,0},{2,1},{3,2},{4,3},{5,4},{6,5},{7,6},{8,15},{9,8},{10,9... | collective-permute-start | bytes 737288 | tf_op jit(solution)/shard_map/ppermute | solution.py:371
  13.8 8.6 %collective-permute-start = (bf16[960,128]{1,0:T(8,128)(2,1)}, bf16[960,128]{1,0:T(8,128)(2,1)S(1)}, u32[]{:S(2)}, u32[]{:S(2)}) collective-permute-start(bf16[960,128]{1,0:T(8,128)(2,1)} %get-tuple-element.54), channel_id=1, source_target_pairs={{0,1},{1,2},{2,3},{3,4},{4,5},{5,6},{6,7},{7,0},{8,9},{9,10},{10,1... | collective-permute-start | bytes 737288 | tf_op jit(solution)/shard_map/ppermute | solution.py:371
  13.8 8.6 %collective-permute-start.2 = (bf16[240,128]{1,0:T(8,128)(2,1)}, bf16[240,128]{1,0:T(8,128)(2,1)S(1)}, u32[]{:S(2)}, u32[]{:S(2)}) collective-permute-start(bf16[240,128]{1,0:T(8,128)(2,1)} %get-tuple-element.56), channel_id=1, source_target_pairs={{0,2},{1,3},{2,4},{3,5},{4,6},{5,7},{6,0},{7,1},{8,10},{9,11},{10,... | collective-permute-start | bytes 184328 | tf_op jit(solution)/shard_map/ppermute | solution.py:371
  13.8 8.6 %collective-permute-start.3 = (bf16[240,128]{1,0:T(8,128)(2,1)}, bf16[240,128]{1,0:T(8,128)(2,1)S(1)}, u32[]{:S(2)}, u32[]{:S(2)}) collective-permute-start(bf16[240,128]{1,0:T(8,128)(2,1)} %get-tuple-element.57), channel_id=1, source_target_pairs={{0,6},{1,7},{2,0},{3,1},{4,2},{5,3},{6,4},{7,5},{8,14},{9,15},{10,... | collective-permute-start | bytes 184328 | tf_op jit(solution)/shard_map/ppermute | solution.py:371
  17.4 8.8 %copy-start = (bf16[1792,128]{1,0:T(8,128)(2,1)S(1)}, bf16[1792,128]{1,0:T(8,128)(2,1)}, u32[]{:S(2)}) copy-start(bf16[1792,128]{1,0:T(8,128)(2,1)} %fin.5) | copy-start | bytes 1376260
  22.5 7.1 %collective-permute-start.4 = (bf16[480,128]{1,0:T(8,128)(2,1)S(1)}, bf16[480,128]{1,0:T(8,128)(2,1)S(1)}, u32[]{:S(2)}, u32[]{:S(2)}) collective-permute-start(bf16[480,128]{1,0:T(8,128)(2,1)S(1)} %get-tuple-element.63), channel_id=1, source_target_pairs={{0,2},{1,3},{2,4},{3,5},{4,6},{5,7},{6,0},{7,1},{8,10},{9,11},{10,... | collective-permute-start | bytes 368648 | tf_op jit(solution)/shard_map/ppermute | solution.py:371
  22.9 6.7 %collective-permute-start.5 = (bf16[480,128]{1,0:T(8,128)(2,1)S(1)}, bf16[480,128]{1,0:T(8,128)(2,1)S(1)}, u32[]{:S(2)}, u32[]{:S(2)}) collective-permute-start(bf16[480,128]{1,0:T(8,128)(2,1)S(1)} %get-tuple-element.64), channel_id=1, source_target_pairs={{0,6},{1,7},{2,0},{3,1},{4,2},{5,3},{6,4},{7,5},{8,14},{9,15},{10,... | collective-permute-start | bytes 368648 | tf_op jit(solution)/shard_map/ppermute | solution.py:371
  31.7 23.5 %all-to-all-start = ((bf16[16,304,128]{2,1,0:T(8,128)(2,1)}), bf16[16,304,128]{2,1,0:T(8,128)(2,1)S(1)}, u32[]{:S(2)}, u32[]{:S(2)}) async-start(bf16[16,304,128]{2,1,0:T(8,128)(2,1)} %get-tuple-element.65), calls=%async_computation | async-start | bytes 2490368 | tf_op jit(solution)/shard_map/all_to_all | solution.py:413
  38.5 12.3 %collective-permute-start.12 = (bf16[192,128]{1,0:T(8,128)(2,1)S(1)}, bf16[192,128]{1,0:T(8,128)(2,1)S(1)}, u32[]{:S(2)}, u32[]{:S(2)}) collective-permute-start(bf16[192,128]{1,0:T(8,128)(2,1)S(1)} %get-tuple-element.67.refs_0_), channel_id=1, source_target_pairs={{0,4},{1,5},{2,6},{3,7},{4,0},{5,1},{6,2},{7,3},{8,12},{9,13},{10,... | collective-permute-start | bytes 147464 | tf_op jit(solution)/shard_map/ppermute | solution.py:371
  42.7 9.0 %collective-permute-start.11 = (bf16[192,128]{1,0:T(8,128)(2,1)S(1)}, bf16[192,128]{1,0:T(8,128)(2,1)S(1)}, u32[]{:S(2)}, u32[]{:S(2)}) collective-permute-start(bf16[192,128]{1,0:T(8,128)(2,1)S(1)} %get-tuple-element.67.refs_0_), channel_id=1, source_target_pairs={{0,3},{1,4},{2,5},{3,6},{4,7},{5,0},{6,1},{7,2},{8,11},{9,12},{10,... | collective-permute-start | bytes 147464 | tf_op jit(solution)/shard_map/ppermute | solution.py:371
  46.2 7.2 %collective-permute-start.10 = (bf16[192,128]{1,0:T(8,128)(2,1)S(1)}, bf16[192,128]{1,0:T(8,128)(2,1)S(1)}, u32[]{:S(2)}, u32[]{:S(2)}) collective-permute-start(bf16[192,128]{1,0:T(8,128)(2,1)S(1)} %get-tuple-element.67.refs_0_), channel_id=1, source_target_pairs={{0,5},{1,6},{2,7},{3,0},{4,1},{5,2},{6,3},{7,4},{8,13},{9,14},{10,... | collective-permute-start | bytes 147464 | tf_op jit(solution)/shard_map/ppermute | solution.py:371
  47.2 6.8 %collective-permute-start.9 = (bf16[192,128]{1,0:T(8,128)(2,1)S(1)}, bf16[192,128]{1,0:T(8,128)(2,1)S(1)}, u32[]{:S(2)}, u32[]{:S(2)}) collective-permute-start(bf16[192,128]{1,0:T(8,128)(2,1)S(1)} %get-tuple-element.67.refs_0_), channel_id=1, source_target_pairs={{0,2},{1,3},{2,4},{3,5},{4,6},{5,7},{6,0},{7,1},{8,10},{9,11},{10,... | collective-permute-start | bytes 147464 | tf_op jit(solution)/shard_map/ppermute | solution.py:371
  49.0 5.3 %collective-permute-start.8 = (bf16[192,128]{1,0:T(8,128)(2,1)S(1)}, bf16[192,128]{1,0:T(8,128)(2,1)S(1)}, u32[]{:S(2)}, u32[]{:S(2)}) collective-permute-start(bf16[192,128]{1,0:T(8,128)(2,1)S(1)} %get-tuple-element.67.refs_0_), channel_id=1, source_target_pairs={{0,6},{1,7},{2,0},{3,1},{4,2},{5,3},{6,4},{7,5},{8,14},{9,15},{10,... | collective-permute-start | bytes 147464 | tf_op jit(solution)/shard_map/ppermute | solution.py:371
  50.8 4.5 %collective-permute-start.7 = (bf16[192,128]{1,0:T(8,128)(2,1)S(1)}, bf16[192,128]{1,0:T(8,128)(2,1)S(1)}, u32[]{:S(2)}, u32[]{:S(2)}) collective-permute-start(bf16[192,128]{1,0:T(8,128)(2,1)S(1)} %get-tuple-element.67.refs_0_), channel_id=1, source_target_pairs={{0,1},{1,2},{2,3},{3,4},{4,5},{5,6},{6,7},{7,0},{8,9},{9,10},{10,1... | collective-permute-start | bytes 147464 | tf_op jit(solution)/shard_map/ppermute | solution.py:371
  51.7 3.5 %collective-permute-start.6 = (bf16[192,128]{1,0:T(8,128)(2,1)S(1)}, bf16[192,128]{1,0:T(8,128)(2,1)S(1)}, u32[]{:S(2)}, u32[]{:S(2)}) collective-permute-start(bf16[192,128]{1,0:T(8,128)(2,1)S(1)} %get-tuple-element.67.refs_0_), channel_id=1, source_target_pairs={{0,7},{1,0},{2,1},{3,2},{4,3},{5,4},{6,5},{7,6},{8,15},{9,8},{10,9... | collective-permute-start | bytes 147464 | tf_op jit(solution)/shard_map/ppermute | solution.py:371
  55.2 11.4 %collective-permute-start.13 = (bf16[16,304,128]{2,1,0:T(8,128)(2,1)S(1)}, bf16[16,304,128]{2,1,0:T(8,128)(2,1)S(1)}, u32[]{:S(2)}, u32[]{:S(2)}) collective-permute-start(bf16[16,304,128]{2,1,0:T(8,128)(2,1)S(1)} %all-to-all-done.refs_8_), channel_id=1, source_target_pairs={{0,8},{8,0},{16,24},{24,16},{32,40},{40,32},{48,56},{56,48},{64,72... | collective-permute-start | bytes 3735560 | tf_op jit(solution)/shard_map/ppermute | solution.py:418
  66.6 18.9 %copy-start.2 = (s32[128,1]{0,1:T(1,128)S(1)}, s32[128,1]{0,1:T(1,128)}, u32[]{:S(2)}) copy-start(s32[128,1]{0,1:T(1,128)} %param.19) | copy-start | bytes 1540
  72.9 12.5 %all-to-all-start.1 = ((f32[8,16,128]{2,1,0:T(8,128)}), f32[8,16,128]{2,1,0:T(8,128)S(1)}, u32[]{:S(2)}, u32[]{:S(2)}) async-start(f32[8,16,128]{2,1,0:T(8,128)} %score_last.1), calls=%async_computation.1 | async-start | bytes 131072 | tf_op jit(solution)/shard_map/all_to_all | solution.py:421

commit v5 on v4

--- a/solution.py
+++ b/solution.py
@@ -22,7 +22,7 @@
 PMSG = ROWS + ROWS // 2
 MB = 1024 * 1024
 LIMITS = (60, 53, 53)
-POOL_ORDER = (7, 1, 6, 2, 5, 3, 4)
+POOL_ORDER = (7, 1, 6, 2, 4, 5, 3)
 
 
 def dot_nt(a, b, precision=None):
@@ -64,7 +64,7 @@
         moves.append(here)
     for copy in weights:
         copy.wait()
-    together = min(2, len(steps))
+    together = len(steps)
     for first in range(0, len(steps), together):
         count = min(together, len(steps) - first)
         for i in range(first, first + count):
@@ -215,7 +215,6 @@
 def score_kernel(last, *refs):
     if last:
         t_ref, pin, pout, prev, tmsg, scale, out, t_in, t_out, hot, best, rows = refs
-        best[...] = prev[...]
     else:
         pools, (tmsg, pin, pout, best, t_in, t_out, hot) = refs[:8], refs[8:]
         half = ROWS // 2
@@ -265,7 +264,8 @@
             part = dot_nt(joined.astype(BF16), hot[:, cols])
             total = part if total is None else total + part
         if last or g:
-            best[...] = jnp.maximum(best[...], total)
+            so_far = best if g else prev
+            best[...] = jnp.maximum(so_far[...], total)
         else:
             best[...] = total
     if last:

time: 102 us -> 101 us (level)
  transfers between devices with their start and end apart: 16 -> 16, of which waited for: 6 -> 5; matrix products, arithmetic and copies ran while one was open for 0% -> 0% of each run, Pallas kernels for 11% -> 11%
where the time goes in v5:
time: 101 us
  starting transfers between devices  46.4 us (46%)
  Pallas kernels  26.9 us (27%)
  blocking collectives  15 us (15%)
  waiting for transfers between devices  11.9 us (12%)
    ppermute x13, starting transfers between devices, shift(): return lax.ppermute(x, axis, [(i, (i + k) % n) for i in range(n)])  28.7 us
    all_to_all x1, blocking collectives, shards(): lax.all_to_all(sent, 'pool', split_axis=0, concat_axis=0, tiled=True)  15 us
    pallas_call x2, Pallas kernels, score(): pl.pallas_call(functools.partial(score_kernel, last), in_specs=[smem] * l...  12 us
    pallas_call x3, Pallas kernels, project(): pl.pallas_call(functools.partial(project_kernel, steps, kinds), in_specs=...  11.8 us
    all_to_all x1, waiting for transfers between devices, shards(): got = lax.all_to_all(best, 'tgt', split_axis=0, concat_axis=0, tiled=True)  7.14 us
    all_to_all x1, starting transfers between devices, shards(): lax.all_to_all(tmsg, 'pool', split_axis=0, concat_axis=0, tiled=True, axi...  6.76 us
    ppermute x1, starting transfers between devices, shards(): far = lax.ppermute(near, 'pool', [(i, i ^ 1) for i in range(n_pool)])  5.6 us
    all_to_all x1, starting transfers between devices, shards(): got = lax.all_to_all(best, 'tgt', split_axis=0, concat_axis=0, tiled=True)  5.35 us
  transfers between devices with their start and end apart: 16, of which 5 were waited for; matrix products, arithmetic and copies ran while one was open for 0% of the time, Pallas kernels for 11%

profile of v5, /device:TPU:1, one launch (start us, length us, event | category | flops | bytes accessed | tf_op | source)
XLA Modules:
  0.0 101.2 jit_solution(14230155364250088048)
XLA Ops:
  0.7 6.4 %project.3 = (bf16[960,128]{1,0:T(8,128)(2,1)}, bf16[960,128]{1,0:T(8,128)(2,1)}, bf16[240,128]{1,0:T(8,128)(2,1)}, bf16[240,128]{1,0:T(8,128)(2,1)}) custom-call(s32[1]{0:T(128)} %bitcast.t_ref.refs_0_, bf16[1024,1792]{1,0:T(8,128)(2,1)} %ph.5, bf16[1024,512]{1,0:T(8,128)(2,1)} %pg.5, bf16[1536,1792]{1,0:T(8,128)(2,1)} %th.5, bf16[1536,512]{1,0:T(8,128)(2,1)} %tg.5, ...), custom_call_target="tpu_custom_call" | custom-call | flops 850000000 | bytes 8000000 | tf_op jit(solution)/shard_map/project/pallas_call | solution.py:99
  7.0 6.5 %collective-permute-start.1 = (bf16[960,128]{1,0:T(8,128)(2,1)}, bf16[960,128]{1,0:T(8,128)(2,1)S(1)}, u32[]{:S(2)}, u32[]{:S(2)}) collective-permute-start(bf16[960,128]{1,0:T(8,128)(2,1)} %get-tuple-element.55), channel_id=1, source_target_pairs={{0,7},{1,0},{2,1},{3,2},{4,3},{5,4},{6,5},{7,6},{8,15},{9,8},{10,9... | collective-permute-start | bytes 737288 | tf_op jit(solution)/shard_map/ppermute | solution.py:371
  13.5 3.6 %collective-permute-start.3 = (bf16[240,128]{1,0:T(8,128)(2,1)}, bf16[240,128]{1,0:T(8,128)(2,1)S(1)}, u32[]{:S(2)}, u32[]{:S(2)}) collective-permute-start(bf16[240,128]{1,0:T(8,128)(2,1)} %get-tuple-element.57), channel_id=1, source_target_pairs={{0,6},{1,7},{2,0},{3,1},{4,2},{5,3},{6,4},{7,5},{8,14},{9,15},{10,... | collective-permute-start | bytes 184328 | tf_op jit(solution)/shard_map/ppermute | solution.py:371
  17.2 3.1 %project.4 = (f32[480,128]{1,0:T(8,128)S(1)}, f32[480,128]{1,0:T(8,128)S(1)}) custom-call(s32[1]{0:T(128)} %bitcast.3.t_ref, bf16[1024,1792]{1,0:T(8,128)(2,1)} %ph.5, bf16[1024,512]{1,0:T(8,128)(2,1)} %pg.5, bf16[1536,1792]{1,0:T(8,128)(2,1)} %th.5, bf16[1536,512]{1,0:T(8,128)(2,1)} %tg.5, bf16[1792,128]{1,0:T(8,128)(2,1)} %fin.5, bf16[64,512]{1,0:T(8,128)(2,1)S(1)} %bitcast.17), custom_call_target="tpu_custom_call" | custom-call | flops 340000000 | bytes 3200000 | tf_op jit(solution)/shard_map/project/pallas_call | solution.py:99
  20.3 1.9 %collective-permute-done.2.half_low = bf16[240,128]{1,0:T(8,128)(2,1)S(1)} collective-permute-done((bf16[240,128]{1,0:T(8,128)(2,1)}, bf16[240,128]{1,0:T(8,128)(2,1)S(1)}, u32[]{:S(2)}, u32[]{:S(2)}) %collective-permute-start.2) | collective-permute-done | bytes 61472 | tf_op jit(solution)/shard_map/ppermute | solution.py:371
  22.7 3.2 %collective-permute-start.5 = (bf16[480,128]{1,0:T(8,128)(2,1)S(1)}, bf16[480,128]{1,0:T(8,128)(2,1)S(1)}, u32[]{:S(2)}, u32[]{:S(2)}) collective-permute-start(bf16[480,128]{1,0:T(8,128)(2,1)S(1)} %get-tuple-element.64), channel_id=1, source_target_pairs={{0,6},{1,7},{2,0},{3,1},{4,2},{5,3},{6,4},{7,5},{8,14},{9,15},{10,... | collective-permute-start | bytes 368648 | tf_op jit(solution)/shard_map/ppermute | solution.py:371
  26.0 2.4 %project.5.own = f32[480,128]{1,0:T(8,128)S(1)} custom-call(s32[1]{0:T(128)} %bitcast.4.t_ref, bf16[1024,1792]{1,0:T(8,128)(2,1)} %ph.5, bf16[1024,512]{1,0:T(8,128)(2,1)} %pg.5, bf16[1536,1792]{1,0:T(8,128)(2,1)} %th.5, bf16[1536,512]{1,0:T(8,128)(2,1)} %tg.5, bf16[1792,128]{1,0:T(8,128)(2,1)S(1)} %copy-done, bf16[64,512]{1,0:T(8,128)(2,1)S(1)} %bitcast.18), custom_call_target="tpu_custom_call" | custom-call | flops 170000000 | bytes 1600000 | tf_op jit(solution)/shard_map/project/pallas_call | solution.py:99
  28.4 1.0 collective-permute-done.4.rest_2_
  29.4 2.0 %prepare.1 = (bf16[16,304,128]{2,1,0:T(8,128)(2,1)}, bf16[192,128]{1,0:T(8,128)(2,1)S(1)}, f32[8,128]{1,0:T(8,128)S(1)}) custom-call(f32[480,128]{1,0:T(8,128)S(1)} %project.5.own, bf16[960,128]{1,0:T(8,128)(2,1)S(1)} %collective-permute-done.from_low.rest_0_, bf16[960,128]{1,0:T(8,128)(2,1)S(1)} %collective-permute-done.1.from_high.rest_1_, ...), custom_call_target="tpu_custom_call" | custom-call | flops 200000000 | bytes 3000000 | tf_op jit(solution)/shard_map/prepare/pallas_call | solution.py:200
  31.4 6.8 %all-to-all-start = ((bf16[16,304,128]{2,1,0:T(8,128)(2,1)}), bf16[16,304,128]{2,1,0:T(8,128)(2,1)S(1)}, u32[]{:S(2)}, u32[]{:S(2)}) async-start(bf16[16,304,128]{2,1,0:T(8,128)(2,1)} %get-tuple-element.65), calls=%async_computation | async-start | bytes 2490368 | tf_op jit(solution)/shard_map/all_to_all | solution.py:413
  38.2 6.0 %collective-permute-start.12 = (bf16[192,128]{1,0:T(8,128)(2,1)S(1)}, bf16[192,128]{1,0:T(8,128)(2,1)S(1)}, u32[]{:S(2)}, u32[]{:S(2)}) collective-permute-start(bf16[192,128]{1,0:T(8,128)(2,1)S(1)} %get-tuple-element.67.refs_0_), channel_id=1, source_target_pairs={{0,3},{1,4},{2,5},{3,6},{4,7},{5,0},{6,1},{7,2},{8,11},{9,12},{10,... | collective-permute-start | bytes 147464 | tf_op jit(solution)/shard_map/ppermute | solution.py:371
  44.2 2.7 %collective-permute-start.10 = (bf16[192,128]{1,0:T(8,128)(2,1)S(1)}, bf16[192,128]{1,0:T(8,128)(2,1)S(1)}, u32[]{:S(2)}, u32[]{:S(2)}) collective-permute-start(bf16[192,128]{1,0:T(8,128)(2,1)S(1)} %get-tuple-element.67.refs_0_), channel_id=1, source_target_pairs={{0,4},{1,5},{2,6},{3,7},{4,0},{5,1},{6,2},{7,3},{8,12},{9,13},{10,... | collective-permute-start | bytes 147464 | tf_op jit(solution)/shard_map/ppermute | solution.py:371
  46.9 1.9 %collective-permute-start.9 = (bf16[192,128]{1,0:T(8,128)(2,1)S(1)}, bf16[192,128]{1,0:T(8,128)(2,1)S(1)}, u32[]{:S(2)}, u32[]{:S(2)}) collective-permute-start(bf16[192,128]{1,0:T(8,128)(2,1)S(1)} %get-tuple-element.67.refs_0_), channel_id=1, source_target_pairs={{0,2},{1,3},{2,4},{3,5},{4,6},{5,7},{6,0},{7,1},{8,10},{9,11},{10,... | collective-permute-start | bytes 147464 | tf_op jit(solution)/shard_map/ppermute | solution.py:371
  48.7 1.7 %collective-permute-start.8 = (bf16[192,128]{1,0:T(8,128)(2,1)S(1)}, bf16[192,128]{1,0:T(8,128)(2,1)S(1)}, u32[]{:S(2)}, u32[]{:S(2)}) collective-permute-start(bf16[192,128]{1,0:T(8,128)(2,1)S(1)} %get-tuple-element.67.refs_0_), channel_id=1, source_target_pairs={{0,6},{1,7},{2,0},{3,1},{4,2},{5,3},{6,4},{7,5},{8,14},{9,15},{10,... | collective-permute-start | bytes 147464 | tf_op jit(solution)/shard_map/ppermute | solution.py:371
  50.5 0.9 collective-permute-start.7
  51.4 1.8 %collective-permute-start.6 = (bf16[192,128]{1,0:T(8,128)(2,1)S(1)}, bf16[192,128]{1,0:T(8,128)(2,1)S(1)}, u32[]{:S(2)}, u32[]{:S(2)}) collective-permute-start(bf16[192,128]{1,0:T(8,128)(2,1)S(1)} %get-tuple-element.67.refs_0_), channel_id=1, source_target_pairs={{0,7},{1,0},{2,1},{3,2},{4,3},{5,4},{6,5},{7,6},{8,15},{9,8},{10,9... | collective-permute-start | bytes 147464 | tf_op jit(solution)/shard_map/ppermute | solution.py:371
  53.1 1.2 %collective-permute-done.8.refs_3_ = bf16[192,128]{1,0:T(8,128)(2,1)S(1)} collective-permute-done((bf16[192,128]{1,0:T(8,128)(2,1)S(1)}, bf16[192,128]{1,0:T(8,128)(2,1)S(1)}, u32[]{:S(2)}, u32[]{:S(2)}) %collective-permute-start.8) | collective-permute-done | bytes 49184 | tf_op jit(solution)/shard_map/ppermute | solution.py:371
  55.0 5.6 %collective-permute-start.13 = (bf16[16,304,128]{2,1,0:T(8,128)(2,1)S(1)}, bf16[16,304,128]{2,1,0:T(8,128)(2,1)S(1)}, u32[]{:S(2)}, u32[]{:S(2)}) collective-permute-start(bf16[16,304,128]{2,1,0:T(8,128)(2,1)S(1)} %all-to-all-done.refs_8_), channel_id=1, source_target_pairs={{0,8},{8,0},{16,24},{24,16},{32,40},{40,32},{48,56},{56,48},{64,72... | collective-permute-start | bytes 3735560 | tf_op jit(solution)/shard_map/ppermute | solution.py:418
  60.6 5.6 %score_first.1 = (bf16[1024,128]{1,0:T(8,128)(2,1)S(1)}, bf16[1024,128]{1,0:T(8,128)(2,1)S(1)}, f32[1024,128]{1,0:T(8,128)S(1)}) custom-call(bf16[192,128]{1,0:T(8,128)(2,1)S(1)} %get-tuple-element.67.refs_0_, bf16[192,128]{1,0:T(8,128)(2,1)S(1)} %collective-permute-done.6.refs_1_, bf16[192,128]{1,0:T(8,128)(2,1)S(1)} %collective-permute-done.7.refs_2_, ...), custom_call_target="tpu_custom_call" | custom-call | flops 5000000000 | bytes 2000000 | tf_op jit(solution)/shard_map/score_first/pallas_call | solution.py:295
  66.3 6.3 %score_last.1 = f32[8,16,128]{2,1,0:T(8,128)} custom-call(s32[1]{0:T(128)} %bitcast.t_ref.refs_0_, bf16[1024,128]{1,0:T(8,128)(2,1)S(1)} %get-tuple-element.76.refs_1_, bf16[1024,128]{1,0:T(8,128)(2,1)S(1)} %get-tuple-element.77.refs_2_, f32[1024,128]{1,0:T(8,128)S(1)} %get-tuple-element.78.refs_3_, ...), custom_call_target="tpu_custom_call" | custom-call | flops 5000000000 | bytes 2000000 | tf_op jit(solution)/shard_map/score_last/pallas_call | solution.py:295
  72.6 5.3 %all-to-all-start.1 = ((f32[8,16,128]{2,1,0:T(8,128)}), f32[8,16,128]{2,1,0:T(8,128)S(1)}, u32[]{:S(2)}, u32[]{:S(2)}) async-start(f32[8,16,128]{2,1,0:T(8,128)} %score_last.1), calls=%async_computation.1 | async-start | bytes 131072 | tf_op jit(solution)/shard_map/all_to_all | solution.py:421
  78.0 7.1 %all-to-all-done.1.got = f32[8,16,128]{2,1,0:T(8,128)S(1)} async-done(((f32[8,16,128]{2,1,0:T(8,128)}), f32[8,16,128]{2,1,0:T(8,128)S(1)}, u32[]{:S(2)}, u32[]{:S(2)}) %all-to-all-start.1) | async-done | bytes 65568 | tf_op jit(solution)/shard_map/all_to_all | solution.py:421
  85.4 15.0 %all_to_all.21 = f32[32,1,128]{2,1,0:T(1,128)S(1)} all-to-all(f32[32,1,128]{2,1,0:T(1,128)S(1)} %bitcast.20), channel_id=1, replica_groups=mesh['pool'=32,'tgt'=8] {'pool'}, dimensions={0} | all-to-all | bytes 32768 | tf_op jit(solution)/shard_map/all_to_all | solution.py:423
  100.4 0.8 finish.1
  (32 shorter events, 1.7 us)
Async XLA Ops:
  0.6 16.5 %copy-start.3 = (s32[1,192]{1,0:T(1,128)S(1)}, s32[1,192]{1,0:T(1,128)}, u32[]{:S(2)}) copy-start(s32[1,192]{1,0:T(1,128)} %param.18) | copy-start | bytes 2308
  0.6 16.5 %copy-start.1 = (bf16[512,64]{0,1:T(8,128)(2,1)S(1)}, bf16[512,64]{0,1:T(8,128)(2,1)}, u32[]{:S(2)}) copy-start(bf16[512,64]{0,1:T(8,128)(2,1)} %param.17) | copy-start | bytes 196612
  7.0 15.1 %collective-permute-start.1 = (bf16[960,128]{1,0:T(8,128)(2,1)}, bf16[960,128]{1,0:T(8,128)(2,1)S(1)}, u32[]{:S(2)}, u32[]{:S(2)}) collective-permute-start(bf16[960,128]{1,0:T(8,128)(2,1)} %get-tuple-element.55), channel_id=1, source_target_pairs={{0,7},{1,0},{2,1},{3,2},{4,3},{5,4},{6,5},{7,6},{8,15},{9,8},{10,9... | collective-permute-start | bytes 737288 | tf_op jit(solution)/shard_map/ppermute | solution.py:371
  13.5 8.6 %collective-permute-start = (bf16[960,128]{1,0:T(8,128)(2,1)}, bf16[960,128]{1,0:T(8,128)(2,1)S(1)}, u32[]{:S(2)}, u32[]{:S(2)}) collective-permute-start(bf16[960,128]{1,0:T(8,128)(2,1)} %get-tuple-element.54), channel_id=1, source_target_pairs={{0,1},{1,2},{2,3},{3,4},{4,5},{5,6},{6,7},{7,0},{8,9},{9,10},{10,1... | collective-permute-start | bytes 737288 | tf_op jit(solution)/shard_map/ppermute | solution.py:371
  13.5 8.6 %collective-permute-start.2 = (bf16[240,128]{1,0:T(8,128)(2,1)}, bf16[240,128]{1,0:T(8,128)(2,1)S(1)}, u32[]{:S(2)}, u32[]{:S(2)}) collective-permute-start(bf16[240,128]{1,0:T(8,128)(2,1)} %get-tuple-element.56), channel_id=1, source_target_pairs={{0,2},{1,3},{2,4},{3,5},{4,6},{5,7},{6,0},{7,1},{8,10},{9,11},{10,... | collective-permute-start | bytes 184328 | tf_op jit(solution)/shard_map/ppermute | solution.py:371
  13.5 8.6 %collective-permute-start.3 = (bf16[240,128]{1,0:T(8,128)(2,1)}, bf16[240,128]{1,0:T(8,128)(2,1)S(1)}, u32[]{:S(2)}, u32[]{:S(2)}) collective-permute-start(bf16[240,128]{1,0:T(8,128)(2,1)} %get-tuple-element.57), channel_id=1, source_target_pairs={{0,6},{1,7},{2,0},{3,1},{4,2},{5,3},{6,4},{7,5},{8,14},{9,15},{10,... | collective-permute-start | bytes 184328 | tf_op jit(solution)/shard_map/ppermute | solution.py:371
  17.2 8.8 %copy-start = (bf16[1792,128]{1,0:T(8,128)(2,1)S(1)}, bf16[1792,128]{1,0:T(8,128)(2,1)}, u32[]{:S(2)}) copy-start(bf16[1792,128]{1,0:T(8,128)(2,1)} %fin.5) | copy-start | bytes 1376260
  22.2 7.1 %collective-permute-start.4 = (bf16[480,128]{1,0:T(8,128)(2,1)S(1)}, bf16[480,128]{1,0:T(8,128)(2,1)S(1)}, u32[]{:S(2)}, u32[]{:S(2)}) collective-permute-start(bf16[480,128]{1,0:T(8,128)(2,1)S(1)} %get-tuple-element.63), channel_id=1, source_target_pairs={{0,2},{1,3},{2,4},{3,5},{4,6},{5,7},{6,0},{7,1},{8,10},{9,11},{10,... | collective-permute-start | bytes 368648 | tf_op jit(solution)/shard_map/ppermute | solution.py:371
  22.7 6.7 %collective-permute-start.5 = (bf16[480,128]{1,0:T(8,128)(2,1)S(1)}, bf16[480,128]{1,0:T(8,128)(2,1)S(1)}, u32[]{:S(2)}, u32[]{:S(2)}) collective-permute-start(bf16[480,128]{1,0:T(8,128)(2,1)S(1)} %get-tuple-element.64), channel_id=1, source_target_pairs={{0,6},{1,7},{2,0},{3,1},{4,2},{5,3},{6,4},{7,5},{8,14},{9,15},{10,... | collective-permute-start | bytes 368648 | tf_op jit(solution)/shard_map/ppermute | solution.py:371
  31.4 23.7 %all-to-all-start = ((bf16[16,304,128]{2,1,0:T(8,128)(2,1)}), bf16[16,304,128]{2,1,0:T(8,128)(2,1)S(1)}, u32[]{:S(2)}, u32[]{:S(2)}) async-start(bf16[16,304,128]{2,1,0:T(8,128)(2,1)} %get-tuple-element.65), calls=%async_computation | async-start | bytes 2490368 | tf_op jit(solution)/shard_map/all_to_all | solution.py:413
  38.2 12.3 %collective-permute-start.12 = (bf16[192,128]{1,0:T(8,128)(2,1)S(1)}, bf16[192,128]{1,0:T(8,128)(2,1)S(1)}, u32[]{:S(2)}, u32[]{:S(2)}) collective-permute-start(bf16[192,128]{1,0:T(8,128)(2,1)S(1)} %get-tuple-element.67.refs_0_), channel_id=1, source_target_pairs={{0,3},{1,4},{2,5},{3,6},{4,7},{5,0},{6,1},{7,2},{8,11},{9,12},{10,... | collective-permute-start | bytes 147464 | tf_op jit(solution)/shard_map/ppermute | solution.py:371
  44.2 7.2 %collective-permute-start.11 = (bf16[192,128]{1,0:T(8,128)(2,1)S(1)}, bf16[192,128]{1,0:T(8,128)(2,1)S(1)}, u32[]{:S(2)}, u32[]{:S(2)}) collective-permute-start(bf16[192,128]{1,0:T(8,128)(2,1)S(1)} %get-tuple-element.67.refs_0_), channel_id=1, source_target_pairs={{0,5},{1,6},{2,7},{3,0},{4,1},{5,2},{6,3},{7,4},{8,13},{9,14},{10,... | collective-permute-start | bytes 147464 | tf_op jit(solution)/shard_map/ppermute | solution.py:371
  44.2 9.0 %collective-permute-start.10 = (bf16[192,128]{1,0:T(8,128)(2,1)S(1)}, bf16[192,128]{1,0:T(8,128)(2,1)S(1)}, u32[]{:S(2)}, u32[]{:S(2)}) collective-permute-start(bf16[192,128]{1,0:T(8,128)(2,1)S(1)} %get-tuple-element.67.refs_0_), channel_id=1, source_target_pairs={{0,4},{1,5},{2,6},{3,7},{4,0},{5,1},{6,2},{7,3},{8,12},{9,13},{10,... | collective-permute-start | bytes 147464 | tf_op jit(solution)/shard_map/ppermute | solution.py:371
  46.9 6.3 %collective-permute-start.9 = (bf16[192,128]{1,0:T(8,128)(2,1)S(1)}, bf16[192,128]{1,0:T(8,128)(2,1)S(1)}, u32[]{:S(2)}, u32[]{:S(2)}) collective-permute-start(bf16[192,128]{1,0:T(8,128)(2,1)S(1)} %get-tuple-element.67.refs_0_), channel_id=1, source_target_pairs={{0,2},{1,3},{2,4},{3,5},{4,6},{5,7},{6,0},{7,1},{8,10},{9,11},{10,... | collective-permute-start | bytes 147464 | tf_op jit(solution)/shard_map/ppermute | solution.py:371
  48.7 5.6 %collective-permute-start.8 = (bf16[192,128]{1,0:T(8,128)(2,1)S(1)}, bf16[192,128]{1,0:T(8,128)(2,1)S(1)}, u32[]{:S(2)}, u32[]{:S(2)}) collective-permute-start(bf16[192,128]{1,0:T(8,128)(2,1)S(1)} %get-tuple-element.67.refs_0_), channel_id=1, source_target_pairs={{0,6},{1,7},{2,0},{3,1},{4,2},{5,3},{6,4},{7,5},{8,14},{9,15},{10,... | collective-permute-start | bytes 147464 | tf_op jit(solution)/shard_map/ppermute | solution.py:371
  50.5 4.6 %collective-permute-start.7 = (bf16[192,128]{1,0:T(8,128)(2,1)S(1)}, bf16[192,128]{1,0:T(8,128)(2,1)S(1)}, u32[]{:S(2)}, u32[]{:S(2)}) collective-permute-start(bf16[192,128]{1,0:T(8,128)(2,1)S(1)} %get-tuple-element.67.refs_0_), channel_id=1, source_target_pairs={{0,1},{1,2},{2,3},{3,4},{4,5},{5,6},{6,7},{7,0},{8,9},{9,10},{10,1... | collective-permute-start | bytes 147464 | tf_op jit(solution)/shard_map/ppermute | solution.py:371
  51.4 3.7 %collective-permute-start.6 = (bf16[192,128]{1,0:T(8,128)(2,1)S(1)}, bf16[192,128]{1,0:T(8,128)(2,1)S(1)}, u32[]{:S(2)}, u32[]{:S(2)}) collective-permute-start(bf16[192,128]{1,0:T(8,128)(2,1)S(1)} %get-tuple-element.67.refs_0_), channel_id=1, source_target_pairs={{0,7},{1,0},{2,1},{3,2},{4,3},{5,4},{6,5},{7,6},{8,15},{9,8},{10,9... | collective-permute-start | bytes 147464 | tf_op jit(solution)/shard_map/ppermute | solution.py:371
  55.0 11.2 %collective-permute-start.13 = (bf16[16,304,128]{2,1,0:T(8,128)(2,1)S(1)}, bf16[16,304,128]{2,1,0:T(8,128)(2,1)S(1)}, u32[]{:S(2)}, u32[]{:S(2)}) collective-permute-start(bf16[16,304,128]{2,1,0:T(8,128)(2,1)S(1)} %all-to-all-done.refs_8_), channel_id=1, source_target_pairs={{0,8},{8,0},{16,24},{24,16},{32,40},{40,32},{48,56},{56,48},{64,72... | collective-permute-start | bytes 3735560 | tf_op jit(solution)/shard_map/ppermute | solution.py:418
  66.3 18.8 %copy-start.2 = (s32[128,1]{0,1:T(1,128)S(1)}, s32[128,1]{0,1:T(1,128)}, u32[]{:S(2)}) copy-start(s32[128,1]{0,1:T(1,128)} %param.19) | copy-start | bytes 1540
  72.6 12.5 %all-to-all-start.1 = ((f32[8,16,128]{2,1,0:T(8,128)}), f32[8,16,128]{2,1,0:T(8,128)S(1)}, u32[]{:S(2)}, u32[]{:S(2)}) async-start(f32[8,16,128]{2,1,0:T(8,128)} %score_last.1), calls=%async_computation.1 | async-start | bytes 131072 | tf_op jit(solution)/shard_map/all_to_all | solution.py:421

commit v6 on v5

--- a/solution.py
+++ b/solution.py
@@ -21,7 +21,7 @@
 TMSG = TOK + TOK // 2 + 16
 PMSG = ROWS + ROWS // 2
 MB = 1024 * 1024
-LIMITS = (60, 53, 53)
+LIMITS = (60, 53)
 POOL_ORDER = (7, 1, 6, 2, 4, 5, 3)
 
 
@@ -398,14 +398,12 @@
     half_low = shift(opposite_up, "tgt", n_tgt, 2)
     half_high = shift(opposite_down, "tgt", n_tgt, n_tgt - 2)
     t_next, up = after((t, up))
-    two_up, two_down = project(
-        LIMITS[1], t_next, (2, 6), (whole(0), whole(1)), (F32, F32), *shared
+    two_up, two_down, own = project(
+        LIMITS[1], t_next, (2, 6, 0), (whole(0), whole(1), whole(2)), (F32,) * 3, *shared
     )
     two_up, two_down = merge(from_low, from_high, half_low, half_high, two_up, two_down)
-    t_next, two_up = after((t, two_up))
     from_low2 = shift(two_up, "tgt", n_tgt, 2)
     from_high2 = shift(two_down, "tgt", n_tgt, n_tgt - 2)
-    (own,) = project(LIMITS[2], t_next, (0,), (whole(0),), (F32,), *shared)
     parts = [from_low, from_high, from_low2, from_high2]
     tmsg, pmsg, scale = prepare(own, parts, ids, n_pool // 2)
 

time: 101 us -> 101 us (level)
  waiting for transfers between devices: 11.9 us -> 13.5 us
  Pallas kernels: 26.9 us -> 25.4 us
    ppermute x13, waiting for transfers between devices: 4.8 us -> 6.37 us  [shift(): return lax.ppermute(x, axis, [(i, (i + k) % n) for i in range(n)])]
    pallas_call x3 -> x2, Pallas kernels: 11.8 us -> 10.3 us  [project(): pl.pallas_call(functools.partial(project_kernel, steps, kinds), in_specs=...]
  transfers between devices with their start and end apart: 16 -> 16, of which waited for: 5 -> 5; matrix products, arithmetic and copies ran while one was open for 0% -> 0% of each run, Pallas kernels for 11% -> 9%
where the time goes in v6:
time: 101 us
  starting transfers between devices  46.4 us (46%)
  Pallas kernels  25.4 us (25%)
  blocking collectives  15 us (15%)
  waiting for transfers between devices  13.5 us (13%)
    ppermute x13, starting transfers between devices, shift(): return lax.ppermute(x, axis, [(i, (i + k) % n) for i in range(n)])  28.7 us
    all_to_all x1, blocking collectives, shards(): lax.all_to_all(sent, 'pool', split_axis=0, concat_axis=0, tiled=True)  15 us
    pallas_call x2, Pallas kernels, score(): pl.pallas_call(functools.partial(score_kernel, last), in_specs=[smem] * l...  12 us
    pallas_call x2, Pallas kernels, project(): pl.pallas_call(functools.partial(project_kernel, steps, kinds), in_specs=...  10.3 us
    all_to_all x1, waiting for transfers between devices, shards(): got = lax.all_to_all(best, 'tgt', split_axis=0, concat_axis=0, tiled=True)  7.14 us
    all_to_all x1, starting transfers between devices, shards(): lax.all_to_all(tmsg, 'pool', split_axis=0, concat_axis=0, tiled=True, axi...  6.76 us
    ppermute x13, waiting for transfers between devices, shift(): return lax.ppermute(x, axis, [(i, (i + k) % n) for i in range(n)])  6.37 us
    ppermute x1, starting transfers between devices, shards(): far = lax.ppermute(near, 'pool', [(i, i ^ 1) for i in range(n_pool)])  5.61 us
  transfers between devices with their start and end apart: 16, of which 5 were waited for; matrix products, arithmetic and copies ran while one was open for 0% of the time, Pallas kernels for 9%

profile of v6, /device:TPU:1, one launch (start us, length us, event | category | flops | bytes accessed | tf_op | source)
XLA Modules:
  0.0 101.2 jit_solution(16751150090107532335)
XLA Ops:
  0.6 6.4 %project.2 = (bf16[960,128]{1,0:T(8,128)(2,1)}, bf16[960,128]{1,0:T(8,128)(2,1)}, bf16[240,128]{1,0:T(8,128)(2,1)}, bf16[240,128]{1,0:T(8,128)(2,1)}) custom-call(s32[1]{0:T(128)} %bitcast.t_ref.refs_0_, bf16[1024,1792]{1,0:T(8,128)(2,1)} %ph.3, bf16[1024,512]{1,0:T(8,128)(2,1)} %pg.3, bf16[1536,1792]{1,0:T(8,128)(2,1)} %th.3, bf16[1536,512]{1,0:T(8,128)(2,1)} %tg.3, ...), custom_call_target="tpu_custom_call" | custom-call | flops 850000000 | bytes 8000000 | tf_op jit(solution)/shard_map/project/pallas_call | solution.py:99
  7.0 6.5 %collective-permute-start.1 = (bf16[960,128]{1,0:T(8,128)(2,1)}, bf16[960,128]{1,0:T(8,128)(2,1)S(1)}, u32[]{:S(2)}, u32[]{:S(2)}) collective-permute-start(bf16[960,128]{1,0:T(8,128)(2,1)} %get-tuple-element.56), channel_id=1, source_target_pairs={{0,7},{1,0},{2,1},{3,2},{4,3},{5,4},{6,5},{7,6},{8,15},{9,8},{10,9... | collective-permute-start | bytes 737288 | tf_op jit(solution)/shard_map/ppermute | solution.py:371
  13.5 3.6 %collective-permute-start.3 = (bf16[240,128]{1,0:T(8,128)(2,1)}, bf16[240,128]{1,0:T(8,128)(2,1)S(1)}, u32[]{:S(2)}, u32[]{:S(2)}) collective-permute-start(bf16[240,128]{1,0:T(8,128)(2,1)} %get-tuple-element.58), channel_id=1, source_target_pairs={{0,6},{1,7},{2,0},{3,1},{4,2},{5,3},{6,4},{7,5},{8,14},{9,15},{10,... | collective-permute-start | bytes 184328 | tf_op jit(solution)/shard_map/ppermute | solution.py:371
  17.1 3.9 %project.3 = (f32[480,128]{1,0:T(8,128)S(1)}, f32[480,128]{1,0:T(8,128)S(1)}, f32[480,128]{1,0:T(8,128)S(1)}) custom-call(s32[1]{0:T(128)} %bitcast.3.t_ref, bf16[1024,1792]{1,0:T(8,128)(2,1)} %ph.3, bf16[1024,512]{1,0:T(8,128)(2,1)} %pg.3, bf16[1536,1792]{1,0:T(8,128)(2,1)} %th.3, bf16[1536,512]{1,0:T(8,128)(2,1)} %tg.3, bf16[1792,128]{1,0:T(8,128)(2,1)} %fin.3, ...), custom_call_target="tpu_custom_call" | custom-call | flops 510000000 | bytes 4800000 | tf_op jit(solution)/shard_map/project/pallas_call | solution.py:99
  21.0 1.1 %collective-permute-done.2.half_low = bf16[240,128]{1,0:T(8,128)(2,1)S(1)} collective-permute-done((bf16[240,128]{1,0:T(8,128)(2,1)}, bf16[240,128]{1,0:T(8,128)(2,1)S(1)}, u32[]{:S(2)}, u32[]{:S(2)}) %collective-permute-start.2) | collective-permute-done | bytes 61472 | tf_op jit(solution)/shard_map/ppermute | solution.py:371
  22.7 3.2 %collective-permute-start.5 = (bf16[480,128]{1,0:T(8,128)(2,1)S(1)}, bf16[480,128]{1,0:T(8,128)(2,1)S(1)}, u32[]{:S(2)}, u32[]{:S(2)}) collective-permute-start(bf16[480,128]{1,0:T(8,128)(2,1)S(1)} %get-tuple-element.62), channel_id=1, source_target_pairs={{0,6},{1,7},{2,0},{3,1},{4,2},{5,3},{6,4},{7,5},{8,14},{9,15},{10,... | collective-permute-start | bytes 368648 | tf_op jit(solution)/shard_map/ppermute | solution.py:371
  26.0 3.3 %collective-permute-done.4.rest_2_ = bf16[480,128]{1,0:T(8,128)(2,1)S(1)} collective-permute-done((bf16[480,128]{1,0:T(8,128)(2,1)S(1)}, bf16[480,128]{1,0:T(8,128)(2,1)S(1)}, u32[]{:S(2)}, u32[]{:S(2)}) %collective-permute-start.4) | collective-permute-done | bytes 122912 | tf_op jit(solution)/shard_map/ppermute | solution.py:371
  29.4 2.0 %prepare.1 = (bf16[16,304,128]{2,1,0:T(8,128)(2,1)}, bf16[192,128]{1,0:T(8,128)(2,1)S(1)}, f32[8,128]{1,0:T(8,128)S(1)}) custom-call(f32[480,128]{1,0:T(8,128)S(1)} %get-tuple-element.55.own, bf16[960,128]{1,0:T(8,128)(2,1)S(1)} %collective-permute-done.from_low.rest_0_, bf16[960,128]{1,0:T(8,128)(2,1)S(1)} %collective-permute-done.1.from_high.rest_1_, ...), custom_call_target="tpu_custom_call" | custom-call | flops 200000000 | bytes 3000000 | tf_op jit(solution)/shard_map/prepare/pallas_call | solution.py:200
  31.4 6.8 %all-to-all-start = ((bf16[16,304,128]{2,1,0:T(8,128)(2,1)}), bf16[16,304,128]{2,1,0:T(8,128)(2,1)S(1)}, u32[]{:S(2)}, u32[]{:S(2)}) async-start(bf16[16,304,128]{2,1,0:T(8,128)(2,1)} %get-tuple-element.63), calls=%async_computation | async-start | bytes 2490368 | tf_op jit(solution)/shard_map/all_to_all | solution.py:411
  38.1 6.0 %collective-permute-start.12 = (bf16[192,128]{1,0:T(8,128)(2,1)S(1)}, bf16[192,128]{1,0:T(8,128)(2,1)S(1)}, u32[]{:S(2)}, u32[]{:S(2)}) collective-permute-start(bf16[192,128]{1,0:T(8,128)(2,1)S(1)} %get-tuple-element.65.refs_0_), channel_id=1, source_target_pairs={{0,3},{1,4},{2,5},{3,6},{4,7},{5,0},{6,1},{7,2},{8,11},{9,12},{10,... | collective-permute-start | bytes 147464 | tf_op jit(solution)/shard_map/ppermute | solution.py:371
  44.2 2.7 %collective-permute-start.10 = (bf16[192,128]{1,0:T(8,128)(2,1)S(1)}, bf16[192,128]{1,0:T(8,128)(2,1)S(1)}, u32[]{:S(2)}, u32[]{:S(2)}) collective-permute-start(bf16[192,128]{1,0:T(8,128)(2,1)S(1)} %get-tuple-element.65.refs_0_), channel_id=1, source_target_pairs={{0,4},{1,5},{2,6},{3,7},{4,0},{5,1},{6,2},{7,3},{8,12},{9,13},{10,... | collective-permute-start | bytes 147464 | tf_op jit(solution)/shard_map/ppermute | solution.py:371
  46.9 1.9 %collective-permute-start.9 = (bf16[192,128]{1,0:T(8,128)(2,1)S(1)}, bf16[192,128]{1,0:T(8,128)(2,1)S(1)}, u32[]{:S(2)}, u32[]{:S(2)}) collective-permute-start(bf16[192,128]{1,0:T(8,128)(2,1)S(1)} %get-tuple-element.65.refs_0_), channel_id=1, source_target_pairs={{0,2},{1,3},{2,4},{3,5},{4,6},{5,7},{6,0},{7,1},{8,10},{9,11},{10,... | collective-permute-start | bytes 147464 | tf_op jit(solution)/shard_map/ppermute | solution.py:371
  48.7 1.7 %collective-permute-start.8 = (bf16[192,128]{1,0:T(8,128)(2,1)S(1)}, bf16[192,128]{1,0:T(8,128)(2,1)S(1)}, u32[]{:S(2)}, u32[]{:S(2)}) collective-permute-start(bf16[192,128]{1,0:T(8,128)(2,1)S(1)} %get-tuple-element.65.refs_0_), channel_id=1, source_target_pairs={{0,6},{1,7},{2,0},{3,1},{4,2},{5,3},{6,4},{7,5},{8,14},{9,15},{10,... | collective-permute-start | bytes 147464 | tf_op jit(solution)/shard_map/ppermute | solution.py:371
  50.4 0.9 collective-permute-start.7
  51.3 1.8 %collective-permute-start.6 = (bf16[192,128]{1,0:T(8,128)(2,1)S(1)}, bf16[192,128]{1,0:T(8,128)(2,1)S(1)}, u32[]{:S(2)}, u32[]{:S(2)}) collective-permute-start(bf16[192,128]{1,0:T(8,128)(2,1)S(1)} %get-tuple-element.65.refs_0_), channel_id=1, source_target_pairs={{0,7},{1,0},{2,1},{3,2},{4,3},{5,4},{6,5},{7,6},{8,15},{9,8},{10,9... | collective-permute-start | bytes 147464 | tf_op jit(solution)/shard_map/ppermute | solution.py:371
  53.1 1.2 %collective-permute-done.8.refs_3_ = bf16[192,128]{1,0:T(8,128)(2,1)S(1)} collective-permute-done((bf16[192,128]{1,0:T(8,128)(2,1)S(1)}, bf16[192,128]{1,0:T(8,128)(2,1)S(1)}, u32[]{:S(2)}, u32[]{:S(2)}) %collective-permute-start.8) | collective-permute-done | bytes 49184 | tf_op jit(solution)/shard_map/ppermute | solution.py:371
  54.3 0.7 collective-permute-done.7.refs_2_
  55.0 5.6 %collective-permute-start.13 = (bf16[16,304,128]{2,1,0:T(8,128)(2,1)S(1)}, bf16[16,304,128]{2,1,0:T(8,128)(2,1)S(1)}, u32[]{:S(2)}, u32[]{:S(2)}) collective-permute-start(bf16[16,304,128]{2,1,0:T(8,128)(2,1)S(1)} %all-to-all-done.refs_8_), channel_id=1, source_target_pairs={{0,8},{8,0},{16,24},{24,16},{32,40},{40,32},{48,56},{56,48},{64,72... | collective-permute-start | bytes 3735560 | tf_op jit(solution)/shard_map/ppermute | solution.py:416
  60.6 5.6 %score_first.1 = (bf16[1024,128]{1,0:T(8,128)(2,1)S(1)}, bf16[1024,128]{1,0:T(8,128)(2,1)S(1)}, f32[1024,128]{1,0:T(8,128)S(1)}) custom-call(bf16[192,128]{1,0:T(8,128)(2,1)S(1)} %get-tuple-element.65.refs_0_, bf16[192,128]{1,0:T(8,128)(2,1)S(1)} %collective-permute-done.6.refs_1_, bf16[192,128]{1,0:T(8,128)(2,1)S(1)} %collective-permute-done.7.refs_2_, ...), custom_call_target="tpu_custom_call" | custom-call | flops 5000000000 | bytes 2000000 | tf_op jit(solution)/shard_map/score_first/pallas_call | solution.py:295
  66.3 6.3 %score_last.1 = f32[8,16,128]{2,1,0:T(8,128)} custom-call(s32[1]{0:T(128)} %bitcast.t_ref.refs_0_, bf16[1024,128]{1,0:T(8,128)(2,1)S(1)} %get-tuple-element.74.refs_1_, bf16[1024,128]{1,0:T(8,128)(2,1)S(1)} %get-tuple-element.75.refs_2_, f32[1024,128]{1,0:T(8,128)S(1)} %get-tuple-element.76.refs_3_, ...), custom_call_target="tpu_custom_call" | custom-call | flops 5000000000 | bytes 2000000 | tf_op jit(solution)/shard_map/score_last/pallas_call | solution.py:295
  72.6 5.3 %all-to-all-start.1 = ((f32[8,16,128]{2,1,0:T(8,128)}), f32[8,16,128]{2,1,0:T(8,128)S(1)}, u32[]{:S(2)}, u32[]{:S(2)}) async-start(f32[8,16,128]{2,1,0:T(8,128)} %score_last.1), calls=%async_computation.1 | async-start | bytes 131072 | tf_op jit(solution)/shard_map/all_to_all | solution.py:419
  78.0 7.1 %all-to-all-done.1.got = f32[8,16,128]{2,1,0:T(8,128)S(1)} async-done(((f32[8,16,128]{2,1,0:T(8,128)}), f32[8,16,128]{2,1,0:T(8,128)S(1)}, u32[]{:S(2)}, u32[]{:S(2)}) %all-to-all-start.1) | async-done | bytes 65568 | tf_op jit(solution)/shard_map/all_to_all | solution.py:419
  85.4 15.0 %all_to_all.21 = f32[32,1,128]{2,1,0:T(1,128)S(1)} all-to-all(f32[32,1,128]{2,1,0:T(1,128)S(1)} %bitcast.18), channel_id=1, replica_groups=mesh['pool'=32,'tgt'=8] {'pool'}, dimensions={0} | all-to-all | bytes 32768 | tf_op jit(solution)/shard_map/all_to_all | solution.py:421
  100.4 0.8 finish.1
  (29 shorter events, 0.9 us)
Async XLA Ops:
  0.6 16.5 %copy-start = (bf16[512,64]{0,1:T(8,128)(2,1)S(1)}, bf16[512,64]{0,1:T(8,128)(2,1)}, u32[]{:S(2)}) copy-start(bf16[512,64]{0,1:T(8,128)(2,1)} %param.17) | copy-start | bytes 196612
  7.0 15.1 %collective-permute-start.1 = (bf16[960,128]{1,0:T(8,128)(2,1)}, bf16[960,128]{1,0:T(8,128)(2,1)S(1)}, u32[]{:S(2)}, u32[]{:S(2)}) collective-permute-start(bf16[960,128]{1,0:T(8,128)(2,1)} %get-tuple-element.56), channel_id=1, source_target_pairs={{0,7},{1,0},{2,1},{3,2},{4,3},{5,4},{6,5},{7,6},{8,15},{9,8},{10,9... | collective-permute-start | bytes 737288 | tf_op jit(solution)/shard_map/ppermute | solution.py:371
  13.5 8.6 %collective-permute-start = (bf16[960,128]{1,0:T(8,128)(2,1)}, bf16[960,128]{1,0:T(8,128)(2,1)S(1)}, u32[]{:S(2)}, u32[]{:S(2)}) collective-permute-start(bf16[960,128]{1,0:T(8,128)(2,1)} %get-tuple-element.53), channel_id=1, source_target_pairs={{0,1},{1,2},{2,3},{3,4},{4,5},{5,6},{6,7},{7,0},{8,9},{9,10},{10,1... | collective-permute-start | bytes 737288 | tf_op jit(solution)/shard_map/ppermute | solution.py:371
  13.5 8.6 %collective-permute-start.2 = (bf16[240,128]{1,0:T(8,128)(2,1)}, bf16[240,128]{1,0:T(8,128)(2,1)S(1)}, u32[]{:S(2)}, u32[]{:S(2)}) collective-permute-start(bf16[240,128]{1,0:T(8,128)(2,1)} %get-tuple-element.57), channel_id=1, source_target_pairs={{0,2},{1,3},{2,4},{3,5},{4,6},{5,7},{6,0},{7,1},{8,10},{9,11},{10,... | collective-permute-start | bytes 184328 | tf_op jit(solution)/shard_map/ppermute | solution.py:371
  13.5 8.6 %collective-permute-start.3 = (bf16[240,128]{1,0:T(8,128)(2,1)}, bf16[240,128]{1,0:T(8,128)(2,1)S(1)}, u32[]{:S(2)}, u32[]{:S(2)}) collective-permute-start(bf16[240,128]{1,0:T(8,128)(2,1)} %get-tuple-element.58), channel_id=1, source_target_pairs={{0,6},{1,7},{2,0},{3,1},{4,2},{5,3},{6,4},{7,5},{8,14},{9,15},{10,... | collective-permute-start | bytes 184328 | tf_op jit(solution)/shard_map/ppermute | solution.py:371
  17.1 8.8 %copy-start.2 = (s32[1,192]{1,0:T(1,128)S(1)}, s32[1,192]{1,0:T(1,128)}, u32[]{:S(2)}) copy-start(s32[1,192]{1,0:T(1,128)} %param.18) | copy-start | bytes 2308
  22.2 7.1 %collective-permute-start.4 = (bf16[480,128]{1,0:T(8,128)(2,1)S(1)}, bf16[480,128]{1,0:T(8,128)(2,1)S(1)}, u32[]{:S(2)}, u32[]{:S(2)}) collective-permute-start(bf16[480,128]{1,0:T(8,128)(2,1)S(1)} %get-tuple-element.61), channel_id=1, source_target_pairs={{0,2},{1,3},{2,4},{3,5},{4,6},{5,7},{6,0},{7,1},{8,10},{9,11},{10,... | collective-permute-start | bytes 368648 | tf_op jit(solution)/shard_map/ppermute | solution.py:371
  22.7 6.7 %collective-permute-start.5 = (bf16[480,128]{1,0:T(8,128)(2,1)S(1)}, bf16[480,128]{1,0:T(8,128)(2,1)S(1)}, u32[]{:S(2)}, u32[]{:S(2)}) collective-permute-start(bf16[480,128]{1,0:T(8,128)(2,1)S(1)} %get-tuple-element.62), channel_id=1, source_target_pairs={{0,6},{1,7},{2,0},{3,1},{4,2},{5,3},{6,4},{7,5},{8,14},{9,15},{10,... | collective-permute-start | bytes 368648 | tf_op jit(solution)/shard_map/ppermute | solution.py:371
  31.4 23.7 %all-to-all-start = ((bf16[16,304,128]{2,1,0:T(8,128)(2,1)}), bf16[16,304,128]{2,1,0:T(8,128)(2,1)S(1)}, u32[]{:S(2)}, u32[]{:S(2)}) async-start(bf16[16,304,128]{2,1,0:T(8,128)(2,1)} %get-tuple-element.63), calls=%async_computation | async-start | bytes 2490368 | tf_op jit(solution)/shard_map/all_to_all | solution.py:411
  38.1 12.3 %collective-permute-start.12 = (bf16[192,128]{1,0:T(8,128)(2,1)S(1)}, bf16[192,128]{1,0:T(8,128)(2,1)S(1)}, u32[]{:S(2)}, u32[]{:S(2)}) collective-permute-start(bf16[192,128]{1,0:T(8,128)(2,1)S(1)} %get-tuple-element.65.refs_0_), channel_id=1, source_target_pairs={{0,3},{1,4},{2,5},{3,6},{4,7},{5,0},{6,1},{7,2},{8,11},{9,12},{10,... | collective-permute-start | bytes 147464 | tf_op jit(solution)/shard_map/ppermute | solution.py:371
  44.2 7.2 %collective-permute-start.11 = (bf16[192,128]{1,0:T(8,128)(2,1)S(1)}, bf16[192,128]{1,0:T(8,128)(2,1)S(1)}, u32[]{:S(2)}, u32[]{:S(2)}) collective-permute-start(bf16[192,128]{1,0:T(8,128)(2,1)S(1)} %get-tuple-element.65.refs_0_), channel_id=1, source_target_pairs={{0,5},{1,6},{2,7},{3,0},{4,1},{5,2},{6,3},{7,4},{8,13},{9,14},{10,... | collective-permute-start | bytes 147464 | tf_op jit(solution)/shard_map/ppermute | solution.py:371
  44.2 9.0 %collective-permute-start.10 = (bf16[192,128]{1,0:T(8,128)(2,1)S(1)}, bf16[192,128]{1,0:T(8,128)(2,1)S(1)}, u32[]{:S(2)}, u32[]{:S(2)}) collective-permute-start(bf16[192,128]{1,0:T(8,128)(2,1)S(1)} %get-tuple-element.65.refs_0_), channel_id=1, source_target_pairs={{0,4},{1,5},{2,6},{3,7},{4,0},{5,1},{6,2},{7,3},{8,12},{9,13},{10,... | collective-permute-start | bytes 147464 | tf_op jit(solution)/shard_map/ppermute | solution.py:371
  46.9 6.3 %collective-permute-start.9 = (bf16[192,128]{1,0:T(8,128)(2,1)S(1)}, bf16[192,128]{1,0:T(8,128)(2,1)S(1)}, u32[]{:S(2)}, u32[]{:S(2)}) collective-permute-start(bf16[192,128]{1,0:T(8,128)(2,1)S(1)} %get-tuple-element.65.refs_0_), channel_id=1, source_target_pairs={{0,2},{1,3},{2,4},{3,5},{4,6},{5,7},{6,0},{7,1},{8,10},{9,11},{10,... | collective-permute-start | bytes 147464 | tf_op jit(solution)/shard_map/ppermute | solution.py:371
  48.7 5.6 %collective-permute-start.8 = (bf16[192,128]{1,0:T(8,128)(2,1)S(1)}, bf16[192,128]{1,0:T(8,128)(2,1)S(1)}, u32[]{:S(2)}, u32[]{:S(2)}) collective-permute-start(bf16[192,128]{1,0:T(8,128)(2,1)S(1)} %get-tuple-element.65.refs_0_), channel_id=1, source_target_pairs={{0,6},{1,7},{2,0},{3,1},{4,2},{5,3},{6,4},{7,5},{8,14},{9,15},{10,... | collective-permute-start | bytes 147464 | tf_op jit(solution)/shard_map/ppermute | solution.py:371
  50.4 4.6 %collective-permute-start.7 = (bf16[192,128]{1,0:T(8,128)(2,1)S(1)}, bf16[192,128]{1,0:T(8,128)(2,1)S(1)}, u32[]{:S(2)}, u32[]{:S(2)}) collective-permute-start(bf16[192,128]{1,0:T(8,128)(2,1)S(1)} %get-tuple-element.65.refs_0_), channel_id=1, source_target_pairs={{0,1},{1,2},{2,3},{3,4},{4,5},{5,6},{6,7},{7,0},{8,9},{9,10},{10,1... | collective-permute-start | bytes 147464 | tf_op jit(solution)/shard_map/ppermute | solution.py:371
  51.3 3.7 %collective-permute-start.6 = (bf16[192,128]{1,0:T(8,128)(2,1)S(1)}, bf16[192,128]{1,0:T(8,128)(2,1)S(1)}, u32[]{:S(2)}, u32[]{:S(2)}) collective-permute-start(bf16[192,128]{1,0:T(8,128)(2,1)S(1)} %get-tuple-element.65.refs_0_), channel_id=1, source_target_pairs={{0,7},{1,0},{2,1},{3,2},{4,3},{5,4},{6,5},{7,6},{8,15},{9,8},{10,9... | collective-permute-start | bytes 147464 | tf_op jit(solution)/shard_map/ppermute | solution.py:371
  55.0 11.2 %collective-permute-start.13 = (bf16[16,304,128]{2,1,0:T(8,128)(2,1)S(1)}, bf16[16,304,128]{2,1,0:T(8,128)(2,1)S(1)}, u32[]{:S(2)}, u32[]{:S(2)}) collective-permute-start(bf16[16,304,128]{2,1,0:T(8,128)(2,1)S(1)} %all-to-all-done.refs_8_), channel_id=1, source_target_pairs={{0,8},{8,0},{16,24},{24,16},{32,40},{40,32},{48,56},{56,48},{64,72... | collective-permute-start | bytes 3735560 | tf_op jit(solution)/shard_map/ppermute | solution.py:416
  66.3 18.8 %copy-start.1 = (s32[128,1]{0,1:T(1,128)S(1)}, s32[128,1]{0,1:T(1,128)}, u32[]{:S(2)}) copy-start(s32[128,1]{0,1:T(1,128)} %param.19) | copy-start | bytes 1540
  72.6 12.5 %all-to-all-start.1 = ((f32[8,16,128]{2,1,0:T(8,128)}), f32[8,16,128]{2,1,0:T(8,128)S(1)}, u32[]{:S(2)}, u32[]{:S(2)}) async-start(f32[8,16,128]{2,1,0:T(8,128)} %score_last.1), calls=%async_computation.1 | async-start | bytes 131072 | tf_op jit(solution)/shard_map/all_to_all | solution.py:419
